TPU v7x, 512 devices: a whole 4x4x16 slice. The times are simulated.
512 devices in a mesh: lat: 16 (over y, x), lon: 32 (over z, core).
Axes of the slice: x: 4, y: 4, z: 16, core: 2. Of those that a mesh axis runs over, the one named last changes fastest.
Arguments:
- grad_field: bfloat16 [720, 1440, 128], P('lat', 'lon'), may hold values from -6 to 6
- legendre: bfloat16 [384, 720, 672], P('lon', 'lat'), may hold values from -0.21875 to 0.21875
Outputs:
- grad_coeff: bfloat16 [672, 384, 2, 128], P(None, 'lon')
All inputs are finite; a program needn't handle non-finite values.
Results may differ from a plain program's by a relative error of at most 0.023.
Values may be sent and summed in bfloat16 or wider, within the bound.
No kernel may reach another device: no remote copies, remote signals or barrier semaphores. Data moves between devices by JAX's collectives and lax.ppermute only.
A program may use at most 64 MiB of HBM per device.

v0:
```python
import jax
import jax.numpy as jnp
from jax import lax
from jax.sharding import PartitionSpec as P

DEGREES = 672
ORDERS = 384
NLON = 1440


def fourier_table(columns):
    column_ids = jnp.arange(columns, dtype=jnp.int32)
    order_ids = jnp.arange(ORDERS, dtype=jnp.int32)
    phases = (column_ids[:, None] * order_ids[None, :] % NLON).astype(jnp.float32) * (
        2.0 * jnp.pi / NLON
    )
    order_weight = jnp.where(order_ids == 0, 1.0, 2.0).astype(jnp.float32) / jnp.sqrt(
        jnp.float32(NLON)
    )
    cosines = order_weight[None, :] * jnp.cos(phases)
    sines = -order_weight[None, :] * jnp.sin(phases)
    return jnp.stack([cosines, sines]).astype(jnp.bfloat16)


def on_device(grad_field, legendre):
    orders_held = legendre.shape[0]
    lon_index = lax.axis_index("lon")
    row_columns = lax.all_to_all(grad_field, "lon", split_axis=2, concat_axis=1, tiled=True)
    whole_table = fourier_table(NLON)
    full_spectrum = jnp.einsum(
        "kjc,rjm->mkrc", row_columns, whole_table, preferred_element_type=jnp.float32
    ).astype(jnp.bfloat16)
    spectrum = lax.all_to_all(full_spectrum, "lon", split_axis=0, concat_axis=3, tiled=True)
    order_ids = lon_index * orders_held + jnp.arange(orders_held, dtype=jnp.int32)
    degree_ids = jnp.arange(DEGREES, dtype=jnp.int32)
    allowed = degree_ids[None, None, :] >= order_ids[:, None, None]
    masked = jnp.where(allowed, legendre, jnp.zeros_like(legendre))
    own_degrees = lax.psum_scatter(
        jnp.einsum("mkl,mkrc->lmrc", masked, spectrum, preferred_element_type=jnp.float32).astype(
            jnp.bfloat16
        ),
        "lat",
        scatter_dimension=0,
        tiled=True,
    )
    return lax.all_gather(own_degrees, "lat", axis=0, tiled=True)


def solution(mesh):
    return jax.shard_map(
        on_device,
        mesh=mesh,
        in_specs=(P("lat", "lon", None), P("lon", "lat", None)),
        out_specs=P(None, "lon", None, None),
        check_vma=False,
    )
```

profile of v0, /device:TPU:24, one launch (start us, length us, event | category | flops | bytes accessed | tf_op | source)
XLA Modules:
  0.0 317.6 jit_solution(8339652288427249179)
XLA Ops:
  6.5 1.9 copy.13
  8.5 3.4 %reshape.143 = bf16[32,2,4050]{2,1,0:T(2,128)(2,1)} reshape(bf16[128,45,45]{2,1,0:T(8,128)(2,1)S(1)} %bitcast.37) | data formatting | bytes 1036800
  11.8 15.5 %all-to-all-start = ((bf16[32,2,4050]{2,1,0:T(2,128)(2,1)}), bf16[32,2,4050]{2,1,0:T(2,128)(2,1)S(1)}, u32[]{:S(2)}, u32[]{:S(2)}) async-start(bf16[32,2,4050]{2,1,0:T(2,128)(2,1)} %reshape.143), calls=%async_computation | async-start | bytes 1048576 | tf_op jit(solution)/shard_map/all_to_all | solution.py:28
  27.4 10.4 %multiply_convert_fusion = (bf16[1,1440,384]{2,1,0:T(8,128)(2,1)S(1)}, bf16[1,1440,384]{2,1,0:T(8,128)(2,1)}) fusion(f32[384]{0:T(512)S(1)} %fusion.14, f32[384]{0:T(512)S(1)} %select_multiply_fusion), kind=kLoop, calls=%fused_computation.8 | loop fusion | flops 7188480 | bytes 2214912 | tf_op jit(solution)/shard_map/convert.1
  37.7 23.3 %all-to-all-done = bf16[32,2,4050]{2,1,0:T(2,128)(2,1)S(1)} async-done(((bf16[32,2,4050]{2,1,0:T(2,128)(2,1)}), bf16[32,2,4050]{2,1,0:T(2,128)(2,1)S(1)}, u32[]{:S(2)}, u32[]{:S(2)}) %all-to-all-start) | async-done | bytes 518432 | tf_op jit(solution)/shard_map/all_to_all | solution.py:28
  61.1 4.3 %reshape.144 = bf16[128,45,45]{2,1,0:T(8,128)(2,1)S(1)} reshape(bf16[32,2,4050]{2,1,0:T(2,128)(2,1)S(1)} %all-to-all-done) | data formatting | bytes 1036800
  65.4 0.4 copy.14
  65.8 0.3 copy.24
  66.1 2.9 reshape.138
  68.9 1.9 fusion.9
  70.8 0.8 copy.17
  71.6 0.0 copy-start
  71.6 1.8 reshape.145
  73.4 3.9 %all-to-all-start.1 = ((bf16[32,2,2160]{2,1,0:T(2,128)(2,1)}), bf16[32,2,2160]{2,1,0:T(2,128)(2,1)S(1)}, u32[]{:S(2)}, u32[]{:S(2)}) async-start(bf16[32,2,2160]{2,1,0:T(2,128)(2,1)} %reshape.145), calls=%async_computation.1 | async-start | bytes 557056 | tf_op jit(solution)/shard_map/all_to_all | solution.py:33
  77.3 0.2 all-reduce.3.cloned.1.call-start
  77.6 0.1 iota_compare_fusion
  77.6 23.2 %all-to-all-done.1 = bf16[32,2,2160]{2,1,0:T(2,128)(2,1)S(1)} async-done(((bf16[32,2,2160]{2,1,0:T(2,128)(2,1)}), bf16[32,2,2160]{2,1,0:T(2,128)(2,1)S(1)}, u32[]{:S(2)}, u32[]{:S(2)}) %all-to-all-start.1) | async-done | bytes 276512 | tf_op jit(solution)/shard_map/all_to_all | solution.py:33
  100.8 1.4 reshape.146
  102.3 0.4 copy.18
  102.7 0.0 copy-done
  102.7 1.3 convert_bitcast_fusion
  104.0 5.2 %copy.20 = bf16[672,12,2,128]{3,2,1,0:T(2,128)(2,1)} copy(bf16[672,12,2,128]{3,0,2,1:T(8,128)(2,1)S(1)} %convert_bitcast_fusion) | data formatting | bytes 8257536 | tf_op jit(solution)/shard_map/convert_element_type | solution.py:39
  109.1 0.0 all-reduce.3.cloned.1.call-update
  109.2 0.0 all-gather.2.cloned.1.call-start
  109.2 1.3 dynamic-slice
  111.1 122.6 %all-reduce.3.cloned.1.call-done = bf16[672,12,2,128]{3,2,1,0:T(2,128)(2,1)} async-done(((bf16[672,12,2,128]{3,2,1,0:T(2,128)(2,1)}), bf16[672,12,2,128]{3,2,1,0:T(2,128)(2,1)}) %all-reduce.3.cloned.1.call-update) | async-done | bytes 4128784
  233.8 1.8 constant_dynamic-slice_fusion
  235.6 0.0 all-gather.2.cloned.1.call-update
  235.6 68.2 %all-gather.2.cloned.1.call-done = bf16[672,12,2,128]{3,2,1,0:T(2,128)(2,1)} async-done(((bf16[42,12,2,128]{3,2,1,0:T(2,128)(2,1)}), bf16[672,12,2,128]{3,2,1,0:T(2,128)(2,1)}) %all-gather.2.cloned.1.call-update) | async-done | bytes 4128784 | tf_op jit(solution)/shard_map/all_gather | solution.py:46
  303.8 7.0 %copy.28 = bf16[672,12,2,128]{3,2,1,0:T(2,128)(2,1)} copy(bf16[672,12,2,128]{3,2,1,0:T(2,128)(2,1)} %all-gather.2.cloned.1.call-done) | data formatting | bytes 8257536
  (3 shorter events, 0.0 us)
Async XLA Ops:
  11.8 49.3 %all-to-all-start = ((bf16[32,2,4050]{2,1,0:T(2,128)(2,1)}), bf16[32,2,4050]{2,1,0:T(2,128)(2,1)S(1)}, u32[]{:S(2)}, u32[]{:S(2)}) async-start(bf16[32,2,4050]{2,1,0:T(2,128)(2,1)} %reshape.143), calls=%async_computation | async-start | bytes 1048576 | tf_op jit(solution)/shard_map/all_to_all | solution.py:28
  71.6 31.0 %copy-start = (bf16[12,45,672]{2,1,0:T(8,128)(2,1)S(1)}, bf16[12,45,672]{2,1,0:T(8,128)(2,1)}, u32[]{:S(2)}) copy-start(bf16[12,45,672]{2,1,0:T(8,128)(2,1)} %param.3) | copy-start | bytes 2177284
  73.4 27.4 %all-to-all-start.1 = ((bf16[32,2,2160]{2,1,0:T(2,128)(2,1)}), bf16[32,2,2160]{2,1,0:T(2,128)(2,1)S(1)}, u32[]{:S(2)}, u32[]{:S(2)}) async-start(bf16[32,2,2160]{2,1,0:T(2,128)(2,1)} %reshape.145), calls=%async_computation.1 | async-start | bytes 557056 | tf_op jit(solution)/shard_map/all_to_all | solution.py:33
  77.3 156.4 %all-reduce.3.cloned.1.call-start = ((), (), s32[]{:S(2)}) async-start(), calls=%async_computation.3 | async-start | bytes 8257536
  109.2 194.6 %all-gather.2.cloned.1.call-start = ((), (), s32[]{:S(2)}) async-start(), calls=%async_computation.2 | async-start | bytes 4386816 | tf_op jit(solution)/shard_map/all_gather | solution.py:46
Sparse Core Ops, SparseCore 0:
  109.3 124.4 all-reduce.2
  237.2 66.4 all-gather.1
where the time goes:
time: 319 us; the launch traced here: 318 us
  waiting for transfers between devices  237 us (74%)
  local copies, waits for them, and re-layouts  32.8 us (10%)
  starting transfers between devices  19.6 us (6%)
  between operations  14.2 us (4%)
  other arithmetic  10.5 us (3%)
    unnamed x3, waiting for transfers between devices  123 us
    all_gather x1, waiting for transfers between devices, on_device(): return lax.all_gather(own_degrees, 'lat', axis=0, tiled=True)  68.2 us
    all_to_all x1, waiting for transfers between devices, on_device(): lax.all_to_all(grad_field, 'lon', split_axis=2, concat_axis=1, tiled=True)  23.3 us
    all_to_all x1, waiting for transfers between devices, on_device(): lax.all_to_all(full_spectrum, 'lon', split_axis=0, concat_axis=3, tiled=T...  23.2 us
    unnamed x10, local copies, waits for them, and re-layouts  23 us
    all_to_all x1, starting transfers between devices, on_device(): lax.all_to_all(grad_field, 'lon', split_axis=2, concat_axis=1, tiled=True)  15.5 us
    another operation x1, other arithmetic  10.4 us
  transfers between devices with their start and end apart: 4, of which 4 were waited for; matrix products, arithmetic and copies ran while one was open for 4% of the time, Pallas kernels for 0%

commit v1 on v0

v1 whole, which is shorter than its diff:
```python
import jax
import jax.numpy as jnp
from jax import lax
from jax.experimental import pallas as pl
from jax.experimental.pallas import tpu as pltpu
from jax.sharding import Mesh, PartitionSpec as P

DEGREES = 672
ORDERS = 384
NLON = 1440
CH = 128
SIDE = 4
LAT = SIDE * SIDE
LON = 32
ROWS = 45
COLS = 45
PAD = 48
HELD = ORDERS // LON
OWN = HELD // SIDE
EXTRA = ROWS - LON
SENT = PAD + PAD // 2
BACK = 40
F32, BF16 = jnp.float32, jnp.bfloat16
VMEM_LIMIT = 48 * 1024 * 1024


def call(body, out_shape, scratch=(), n_in=1):
    whole = pl.BlockSpec(memory_space=pltpu.VMEM)
    return pl.pallas_call(
        body,
        out_shape=out_shape,
        in_specs=[whole] * n_in,
        out_specs=whole,
        scratch_shapes=list(scratch),
        compiler_params=pltpu.CompilerParams(vmem_limit_bytes=VMEM_LIMIT),
    )


def left_half(shape):
    return lax.broadcasted_iota(jnp.int32, shape, len(shape) - 1) < CH // 2


def pack_rows(grad_ref, out_ref, rows):
    rows[...] = jnp.zeros_like(rows)
    half = PAD // 2
    left = left_half((half, CH))
    for d in range(LON):
        rows[0:COLS, :] = grad_ref[d].astype(F32)
        out_ref[d, 0:PAD, :] = rows[...].astype(BF16)
    for extra in range(EXTRA):
        rows[0:COLS, :] = grad_ref[LON + extra].astype(F32)
        early, late = rows[0:half, :], rows[half:PAD, :]
        first = jnp.where(left, early, pltpu.roll(late, CH // 2, 1))
        second = jnp.where(left, pltpu.roll(early, CH // 2, 1), late)
        out_ref[2 * extra, PAD:SENT, :] = first.astype(BF16)
        out_ref[2 * extra + 1, PAD:SENT, :] = second.astype(BF16)
    for d in range(2 * EXTRA, LON):
        out_ref[d, PAD:SENT, :] = jnp.zeros((half, CH), BF16)


def spectrum_rows(x_ref, table_ref, out_ref, both):
    half = PAD // 2
    left = left_half((half, CH))
    for d in range(LON):
        at = d * PAD
        both[at : at + PAD, 0:CH] = x_ref[d, 0:PAD, :]
        packed = x_ref[d, PAD:SENT, :].astype(F32)
        early = jnp.where(left, packed, 0.0)
        late = jnp.where(left, pltpu.roll(packed, CH // 2, 1), 0.0)
        both[at : at + PAD, CH : 2 * CH] = jnp.concatenate([early, late], 0).astype(BF16)
    n = 2 * HELD
    found = jnp.dot(table_ref[...], both[...], preferred_element_type=F32)
    left8 = left_half((8, CH))
    for d in range(LON):
        whole = found[d * n : (d + 1) * n, 0:CH]
        part = found[d * n : (d + 1) * n, CH : 2 * CH]
        mixed = jnp.where(left8, part[0:8], pltpu.roll(part[16:24], CH // 2, 1))
        out_ref[d] = jnp.concatenate([whole, mixed, part[8:16]], 0).astype(BF16)


def turn_rows(r_ref, out_ref, flat):
    for d in range(LON):
        flat[d * BACK : (d + 1) * BACK, :] = r_ref[d].astype(F32)
    n = 2 * HELD
    left = left_half((16, CH))
    for order in range(HELD):
        colour, place = divmod(order, OWN)
        for part in range(2):
            i = part * HELD + order
            lanes = slice(part * CH, (part + 1) * CH)
            main = flat[pl.ds(i, LON, stride=BACK), :]
            at = n + (i if i < 16 else i - 16)
            even = flat[pl.ds(at, 16, stride=2 * BACK), :]
            odd = flat[pl.ds(BACK + at, 16, stride=2 * BACK), :]
            if i < 16:
                rest = jnp.where(left, even, pltpu.roll(odd, CH // 2, 1))
            else:
                rest = jnp.where(left, pltpu.roll(even, CH // 2, 1), odd)
            column = jnp.concatenate([main, rest], 0).astype(BF16)
            for t in range(LAT):
                if (t % SIDE + 2 * (t // SIDE)) % SIDE == colour:
                    out_ref[t, place, :, lanes] = column


def turn_legendre(p0_ref, p1_ref, p2_ref, p3_ref, out_ref, tall):
    for place in range(OWN):
        for hop, ref in enumerate((p0_ref, p1_ref, p2_ref, p3_ref)):
            for shift in range(SIDE):
                at = (hop * SIDE + shift) * PAD
                tall[at : at + PAD, :] = ref[shift, place].astype(F32)
        out_ref[place] = tall[...].T[0:DEGREES].astype(BF16)


def legendre_sum(s_ref, p_ref, out_ref, gathered, spread):
    y, x = lax.axis_index("y"), lax.axis_index("x")
    for hop in range(SIDE):
        for shift in range(SIDE):
            row = lax.rem(y + (SIDE - hop), SIDE)
            column = lax.rem(x + (3 * SIDE - 2 * hop - shift), SIDE)
            at = (hop * SIDE + shift) * PAD
            for place in range(OWN):
                gathered[place, at : at + PAD, :] = s_ref[row * SIDE + column, place]
    for place in range(OWN):
        found = jnp.dot(p_ref[place], gathered[place], preferred_element_type=F32)
        for part in range(2):
            rows = pl.ds(2 * place + part, DEGREES, stride=2 * OWN)
            spread[rows, :] = found[:, part * CH : (part + 1) * CH]
    out_ref[...] = spread[...].astype(BF16)


def fourier_table():
    rows = jnp.arange(2 * ORDERS, dtype=jnp.int32)[:, None]
    columns = jnp.arange(LON * PAD, dtype=jnp.int32)[None, :]
    part = rows % (2 * HELD) // HELD
    order = rows // (2 * HELD) * HELD + rows % HELD
    within = columns % PAD
    longitude = columns // PAD * COLS + within
    phases = ((longitude * order + part * (NLON // 4)) % NLON).astype(F32)
    weight = jnp.where(order == 0, 1.0, 2.0).astype(F32) / jnp.sqrt(F32(NLON))
    values = weight * jnp.cos(phases * (2.0 * jnp.pi / NLON))
    return jnp.where(within < COLS, values, 0.0).astype(BF16)


def along(axis, value, step):
    return lax.ppermute(value, axis, [(i, (i + step) % SIDE) for i in range(SIDE)])


def same_colour(value, step):
    pairs = []
    for y in range(SIDE):
        for x in range(SIDE):
            to = (y + step) % SIDE * SIDE + (x + 2 * step) % SIDE
            pairs.append((y * SIDE + x, to))
    return lax.ppermute(value, ("y", "x"), pairs)


def on_device(grad_field, legendre):
    y, x, lon = lax.axis_index("y"), lax.axis_index("x"), lax.axis_index("lon")
    colour = (x + 2 * y) % SIDE
    struct = jax.ShapeDtypeStruct

    packed = call(
        pack_rows, struct((LON, SENT, CH), BF16), [pltpu.VMEM((PAD, CH), F32)]
    )(grad_field)
    row_columns = lax.all_to_all(packed, "lon", 0, 0, tiled=True)

    order_ids = lon * HELD + jnp.arange(HELD, dtype=jnp.int32)
    degree_ids = jnp.arange(DEGREES, dtype=jnp.int32)
    allowed = degree_ids[None, None, :] >= order_ids[:, None, None]
    masked = jnp.where(allowed, legendre, jnp.zeros_like(legendre))
    masked = jnp.pad(masked, ((0, 0), (0, PAD - ROWS), (0, 768 - DEGREES)))
    masked = masked.reshape(SIDE, OWN, PAD, 768)
    line = [lax.dynamic_index_in_dim(masked, colour, 0, keepdims=False)]
    for step in (1, 2, 3):
        theirs = lax.dynamic_index_in_dim(masked, (colour + step) % SIDE, 0, keepdims=False)
        line.append(along("x", theirs, step))
    line = jnp.stack(line)
    lines = [line] + [same_colour(line, step) for step in (1, 2, 3)]

    returned = call(
        spectrum_rows,
        struct((LON, BACK, CH), BF16),
        [pltpu.VMEM((LON * PAD, 2 * CH), BF16)],
        n_in=2,
    )(row_columns, fourier_table())
    by_sender = lax.all_to_all(returned, "lon", 0, 0, tiled=True)
    turned = call(
        turn_rows,
        struct((LAT, OWN, PAD, 2 * CH), BF16),
        [pltpu.VMEM((LON * BACK, CH), F32)],
    )(by_sender)
    spectrum = lax.all_to_all(turned, ("y", "x"), 0, 0, tiled=True)

    upright = call(
        turn_legendre,
        struct((OWN, DEGREES, LAT * PAD), BF16),
        [pltpu.VMEM((LAT * PAD, 768), F32)],
        n_in=4,
    )(*lines)
    own = call(
        legendre_sum,
        struct((DEGREES * OWN * 2, CH), BF16),
        [
            pltpu.VMEM((OWN, LAT * PAD, 2 * CH), BF16),
            pltpu.VMEM((DEGREES * OWN * 2, CH), F32),
        ],
        n_in=2,
    )(spectrum, upright)

    middle = DEGREES * OWN
    after = along("x", own, -1)
    before = along("x", own, 1)
    low = along("y", own[:middle], 1)
    high = along("y", own[middle:], -1)
    parts = [(own, 0), (after, 1), (before, 3)]
    out = jnp.zeros((DEGREES, HELD, 2, CH), BF16)
    for value, step in parts:
        value = value.reshape(DEGREES, OWN, 2, CH)
        at = (colour + step) % SIDE * OWN
        out = lax.dynamic_update_slice(out, value, (0, at, 0, 0))
    at = (colour + 2) % SIDE * OWN
    for value, start in ((low, 0), (high, DEGREES // 2)):
        value = value.reshape(DEGREES // 2, OWN, 2, CH)
        out = lax.dynamic_update_slice(out, value, (start, at, 0, 0))
    return out


def solution(mesh):
    fine = Mesh(mesh.devices.reshape(SIDE, SIDE, LON), ("y", "x", "lon"))
    return jax.shard_map(
        on_device,
        mesh=fine,
        in_specs=(P(("y", "x"), "lon", None), P("lon", ("y", "x"), None)),
        out_specs=P(None, "lon", None, None),
        check_vma=False,
    )
```

time: 319 us -> 192 us (0.60)
  waiting for transfers between devices: 237 us -> 84.9 us
  starting transfers between devices: 19.6 us -> 60.8 us
  local copies, waits for them, and re-layouts: 32.8 us -> 13.7 us
  between operations: 14.2 us -> 0.36 us
  other arithmetic: 10.5 us -> 21.3 us
  Pallas kernels: 0 us -> 7.9 us
    unnamed x3 -> x0, waiting for transfers between devices: 123 us -> none
    all_gather x1 -> x0, waiting for transfers between devices: 68.2 us -> none  [on_device(): return lax.all_gather(own_degrees, 'lat', axis=0, tiled=True)]
    ppermute x0 -> x10, waiting for transfers between devices: none -> 55.6 us  [the longest x3 42.7 us: same_colour(): return lax.ppermute(value, ('y', 'x'), pairs)]
    ppermute x0 -> x10, starting transfers between devices: none -> 34.3 us  [the longest x7 23.2 us: along(): lax.ppermute(value, axis, [(i, (i + step) % SIDE) for i in range(SIDE)])]
    convert_element_type x0 -> x1, other arithmetic: none -> 19.8 us  [fourier_table(): return jnp.where(within < COLS, values, 0.0).astype(BF16)]
    unnamed x10 -> x6, local copies, waits for them, and re-layouts: 23 us -> 4.9 us
    all_to_all x2 -> x3, waiting for transfers between devices: 46.5 us -> 29.3 us  [the longest x1 16.7 us: on_device(): row_columns = lax.all_to_all(packed, 'lon', 0, 0, tiled=True)]
    another operation x1, other arithmetic: 10.4 us -> 0.11 us  [on_device(): line = jnp.stack(line)]
  transfers between devices with their start and end apart: 4 -> 13, of which waited for: 4 -> 6; matrix products, arithmetic and copies ran while one was open for 4% -> 15% of each run, Pallas kernels for 0% -> 2%
where the time goes in v1:
time: 192 us; the launch traced here: 189 us
  waiting for transfers between devices  84.9 us (44%)
  starting transfers between devices  60.8 us (32%)
  other arithmetic  21.3 us (11%)
  local copies, waits for them, and re-layouts  13.7 us (7%)
  Pallas kernels  7.9 us (4%)
    ppermute x3, waiting for transfers between devices, same_colour(): return lax.ppermute(value, ('y', 'x'), pairs)  42.7 us
    ppermute x7, starting transfers between devices, along(): lax.ppermute(value, axis, [(i, (i + step) % SIDE) for i in range(SIDE)])  23.2 us
    convert_element_type x1, other arithmetic, fourier_table(): return jnp.where(within < COLS, values, 0.0).astype(BF16)  19.8 us
    all_to_all x1, waiting for transfers between devices, on_device(): row_columns = lax.all_to_all(packed, 'lon', 0, 0, tiled=True)  16.7 us
    all_to_all x1, starting transfers between devices, on_device(): row_columns = lax.all_to_all(packed, 'lon', 0, 0, tiled=True)  15.5 us
    ppermute x7, waiting for transfers between devices, along(): lax.ppermute(value, axis, [(i, (i + step) % SIDE) for i in range(SIDE)])  12.9 us
    all_to_all x1, waiting for transfers between devices, on_device(): by_sender = lax.all_to_all(returned, 'lon', 0, 0, tiled=True)  12.6 us
    ppermute x3, starting transfers between devices, same_colour(): return lax.ppermute(value, ('y', 'x'), pairs)  11.1 us
  transfers between devices with their start and end apart: 13, of which 6 were waited for; matrix products, arithmetic and copies ran while one was open for 15% of the time, Pallas kernels for 2%

profile of v1, /device:TPU:24, one launch (start us, length us, event | category | flops | bytes accessed | tf_op | source)
XLA Modules:
  0.0 188.9 jit_solution(12558228991692917823)
XLA Ops:
  0.0 1.0 copy-done.1
  1.1 1.1 shard_map.28
  2.2 15.5 %all-to-all-start = ((bf16[32,72,128]{2,1,0:T(8,128)(2,1)}), bf16[32,72,128]{2,1,0:T(8,128)(2,1)S(1)}, u32[]{:S(2)}, u32[]{:S(2)}) async-start(bf16[32,72,128]{2,1,0:T(8,128)(2,1)} %shard_map.28), calls=%async_computation | async-start | bytes 1179648 | tf_op jit(solution)/shard_map/all_to_all | solution.py:165
  17.8 19.8 %fusion.5.table_ref = bf16[768,1536]{1,0:T(8,128)(2,1)S(1)} fusion(s32[768]{0:T(1024)S(1)} %get-tuple-element.12, s32[768]{0:T(1024)S(1)} %get-tuple-element.11, s32[1536]{0:T(1024)S(1)} %fusion.18, f32[768]{0:T(1024)S(1)} %select_multiply_fusion, pred[1536]{0:T(1024)(128)(4,1)S(1)} %fusion.22), kind=kLoop, calls=%fused_computation.6 | loop fusion | flops 15335424 | bytes 2376192 | tf_op jit(solution)/shard_map/convert_element_type | solution.py:141
  37.5 16.7 %all-to-all-done.x_ref = bf16[32,72,128]{2,1,0:T(8,128)(2,1)S(1)} async-done(((bf16[32,72,128]{2,1,0:T(8,128)(2,1)}), bf16[32,72,128]{2,1,0:T(8,128)(2,1)S(1)}, u32[]{:S(2)}, u32[]{:S(2)}) %all-to-all-start) | async-done | bytes 589856 | tf_op jit(solution)/shard_map/all_to_all | solution.py:165
  54.2 1.7 shard_map.29
  55.9 3.9 %all-to-all-start.1 = ((bf16[32,40,128]{2,1,0:T(8,128)(2,1)}), bf16[32,40,128]{2,1,0:T(8,128)(2,1)S(1)}, u32[]{:S(2)}, u32[]{:S(2)}) async-start(bf16[32,40,128]{2,1,0:T(8,128)(2,1)} %shard_map.29), calls=%async_computation.1 | async-start | bytes 655360 | tf_op jit(solution)/shard_map/all_to_all | solution.py:186
  59.9 0.1 iota_compare_fusion
  60.0 1.2 broadcast_select_fusion
  61.2 0.1 pad.4
  61.3 0.1 constant_dynamic-slice_fusion
  61.4 3.4 %collective-permute-start = (bf16[3,48,768]{2,1,0:T(8,128)(2,1)S(1)}, bf16[3,48,768]{2,1,0:T(8,128)(2,1)S(1)}, u32[]{:S(2)}, u32[]{:S(2)}) collective-permute-start(bf16[3,48,768]{2,1,0:T(8,128)(2,1)S(1)} %get-tuple-element.10), channel_id=1, source_target_pairs={{0,32},{32,64},{64,96},{96,0},{1,33},{33,65},{65,97},{97,1},{2,34}... | collective-permute-start | bytes 663560 | tf_op jit(solution)/shard_map/ppermute | solution.py:145
  64.8 4.6 %collective-permute-start.1 = (bf16[3,48,768]{2,1,0:T(8,128)(2,1)S(1)}, bf16[3,48,768]{2,1,0:T(8,128)(2,1)S(1)}, u32[]{:S(2)}, u32[]{:S(2)}) collective-permute-start(bf16[3,48,768]{2,1,0:T(8,128)(2,1)S(1)} %get-tuple-element.9), channel_id=1, source_target_pairs={{0,64},{32,96},{64,0},{96,32},{1,65},{33,97},{65,1},{97,33},{2,66}... | collective-permute-start | bytes 663560 | tf_op jit(solution)/shard_map/ppermute | solution.py:145
  69.5 3.3 %collective-permute-start.2 = (bf16[3,48,768]{2,1,0:T(8,128)(2,1)S(1)}, bf16[3,48,768]{2,1,0:T(8,128)(2,1)S(1)}, u32[]{:S(2)}, u32[]{:S(2)}) collective-permute-start(bf16[3,48,768]{2,1,0:T(8,128)(2,1)S(1)} %get-tuple-element.8), channel_id=1, source_target_pairs={{0,96},{32,0},{64,32},{96,64},{1,97},{33,1},{65,33},{97,65},{2,98}... | collective-permute-start | bytes 663560 | tf_op jit(solution)/shard_map/ppermute | solution.py:145
  72.8 12.6 %all-to-all-done.1.r_ref = bf16[32,40,128]{2,1,0:T(8,128)(2,1)S(1)} async-done(((bf16[32,40,128]{2,1,0:T(8,128)(2,1)}), bf16[32,40,128]{2,1,0:T(8,128)(2,1)S(1)}, u32[]{:S(2)}, u32[]{:S(2)}) %all-to-all-start.1) | async-done | bytes 327712 | tf_op jit(solution)/shard_map/all_to_all | solution.py:186
  85.4 1.4 shard_map.30
  86.8 7.2 %all-to-all-start.2 = ((bf16[16,3,48,256]{3,2,1,0:T(8,128)(2,1)}), bf16[16,3,48,256]{3,2,1,0:T(8,128)(2,1)S(1)}, u32[]{:S(2)}, u32[]{:S(2)}) async-start(bf16[16,3,48,256]{3,2,1,0:T(8,128)(2,1)} %shard_map.30), calls=%async_computation.2 | async-start | bytes 2359296 | tf_op jit(solution)/shard_map/all_to_all | solution.py:192
  93.9 0.0 collective-permute-done
  94.0 0.0 collective-permute-done.1
  94.0 0.0 collective-permute-done.2
  94.0 0.1 pad_maximum_fusion.p0_ref
  94.1 4.9 %collective-permute-start.3 = (bf16[4,3,48,768]{3,2,1,0:T(8,128)(2,1)S(1)}, bf16[4,3,48,768]{3,2,1,0:T(8,128)(2,1)S(1)}, u32[]{:S(2)}, u32[]{:S(2)}) collective-permute-start(bf16[4,3,48,768]{3,2,1,0:T(8,128)(2,1)S(1)} %pad_maximum_fusion.p0_ref), channel_id=1, source_target_pairs={{0,192},{32,224},{64,128},{96,160},{128,320},{160,352},{192,256},{... | collective-permute-start | bytes 2654216 | tf_op jit(solution)/shard_map/ppermute | solution.py:154
  99.0 4.3 %collective-permute-start.4 = (bf16[4,3,48,768]{3,2,1,0:T(8,128)(2,1)S(1)}, bf16[4,3,48,768]{3,2,1,0:T(8,128)(2,1)S(1)}, u32[]{:S(2)}, u32[]{:S(2)}) collective-permute-start(bf16[4,3,48,768]{3,2,1,0:T(8,128)(2,1)S(1)} %pad_maximum_fusion.p0_ref), channel_id=1, source_target_pairs={{0,256},{32,288},{64,320},{96,352},{128,384},{160,416},{192,448},{... | collective-permute-start | bytes 2654216 | tf_op jit(solution)/shard_map/ppermute | solution.py:154
  103.3 1.9 %collective-permute-start.5 = (bf16[4,3,48,768]{3,2,1,0:T(8,128)(2,1)S(1)}, bf16[4,3,48,768]{3,2,1,0:T(8,128)(2,1)S(1)}, u32[]{:S(2)}, u32[]{:S(2)}) collective-permute-start(bf16[4,3,48,768]{3,2,1,0:T(8,128)(2,1)S(1)} %pad_maximum_fusion.p0_ref), channel_id=1, source_target_pairs={{0,448},{32,480},{64,384},{96,416},{128,64},{160,96},{192,0},{224,... | collective-permute-start | bytes 2654216 | tf_op jit(solution)/shard_map/ppermute | solution.py:154
  105.2 25.5 %collective-permute-done.3.p1_ref = bf16[4,3,48,768]{3,2,1,0:T(8,128)(2,1)S(1)} collective-permute-done((bf16[4,3,48,768]{3,2,1,0:T(8,128)(2,1)S(1)}, bf16[4,3,48,768]{3,2,1,0:T(8,128)(2,1)S(1)}, u32[]{:S(2)}, u32[]{:S(2)}) %collective-permute-start.3) | collective-permute-done | bytes 884768 | tf_op jit(solution)/shard_map/ppermute | solution.py:154
  130.6 0.0 collective-permute-done.4.p2_ref
  130.6 17.2 %collective-permute-done.5.p3_ref = bf16[4,3,48,768]{3,2,1,0:T(8,128)(2,1)S(1)} collective-permute-done((bf16[4,3,48,768]{3,2,1,0:T(8,128)(2,1)S(1)}, bf16[4,3,48,768]{3,2,1,0:T(8,128)(2,1)S(1)}, u32[]{:S(2)}, u32[]{:S(2)}) %collective-permute-start.5) | collective-permute-done | bytes 884768 | tf_op jit(solution)/shard_map/ppermute | solution.py:154
  147.9 2.6 %shard_map.31.p_ref = bf16[3,672,768]{2,1,0:T(8,128)(2,1)} custom-call(bf16[4,3,48,768]{3,2,1,0:T(8,128)(2,1)S(1)} %pad_maximum_fusion.p0_ref, bf16[4,3,48,768]{3,2,1,0:T(8,128)(2,1)S(1)} %collective-permute-done.3.p1_ref, bf16[4,3,48,768]{3,2,1,0:T(8,128)(2,1)S(1)} %collective-permute-done.4.p2_ref, bf16[4,3,48,768]{3,2,1,0:T(8,128)(2,1)S(1)} %collective-permute-done.5.p3_ref), custom_call_target="tpu_custom_call" | custom-call | tf_op jit(solution)/shard_map/pallas_call | solution.py:194
  150.5 0.0 all-to-all-done.2.s_ref
  150.5 1.9 copy-done
  152.4 1.1 shard_map.32
  153.5 3.7 %collective-permute-start.6 = (bf16[4032,128]{1,0:T(8,128)(2,1)S(1)}, bf16[4032,128]{1,0:T(8,128)(2,1)S(1)}, u32[]{:S(2)}, u32[]{:S(2)}) collective-permute-start(bf16[4032,128]{1,0:T(8,128)(2,1)S(1)} %shard_map.32), channel_id=1, source_target_pairs={{0,96},{32,0},{64,32},{96,64},{1,97},{33,1},{65,33},{97,65},{2,98}... | collective-permute-start | bytes 3096584 | tf_op jit(solution)/shard_map/ppermute | solution.py:145
  157.2 2.1 %collective-permute-start.7 = (bf16[4032,128]{1,0:T(8,128)(2,1)S(1)}, bf16[4032,128]{1,0:T(8,128)(2,1)S(1)}, u32[]{:S(2)}, u32[]{:S(2)}) collective-permute-start(bf16[4032,128]{1,0:T(8,128)(2,1)S(1)} %shard_map.32), channel_id=1, source_target_pairs={{0,32},{32,64},{64,96},{96,0},{1,33},{33,65},{65,97},{97,1},{2,34}... | collective-permute-start | bytes 3096584 | tf_op jit(solution)/shard_map/ppermute | solution.py:145
  159.3 1.0 fusion.38
  160.3 3.6 %collective-permute-start.8 = (bf16[2016,128]{1,0:T(8,128)(2,1)}, bf16[2016,128]{1,0:T(8,128)(2,1)}, u32[]{:S(2)}, u32[]{:S(2)}) collective-permute-start(bf16[2016,128]{1,0:T(8,128)(2,1)} %get-tuple-element.6), channel_id=1, source_target_pairs={{0,128},{128,256},{256,384},{384,0},{1,129},{129,257},{257,385},{3... | collective-permute-start | bytes 1548296 | tf_op jit(solution)/shard_map/ppermute | solution.py:145
  164.0 2.4 %collective-permute-start.9 = (bf16[2016,128]{1,0:T(8,128)(2,1)}, bf16[2016,128]{1,0:T(8,128)(2,1)S(1)}, u32[]{:S(2)}, u32[]{:S(2)}) collective-permute-start(bf16[2016,128]{1,0:T(8,128)(2,1)} %get-tuple-element.5), channel_id=1, source_target_pairs={{0,384},{128,0},{256,128},{384,256},{1,385},{129,1},{257,129},{385... | collective-permute-start | bytes 1548296 | tf_op jit(solution)/shard_map/ppermute | solution.py:145
  166.4 2.1 %broadcast_in_dim.38 = bf16[672,12,2,128]{3,2,1,0:T(2,128)(2,1)S(1)} broadcast(bf16[]{:T(256)} %constant.122.clone.1), dimensions={} | broadcast | bytes 4128770 | tf_op jit(solution)/shard_map/broadcast_in_dim | solution.py:216
  168.6 0.9 constant_dynamic-update-slice_fusion.4
  169.5 9.2 %collective-permute-done.6 = bf16[4032,128]{1,0:T(8,128)(2,1)S(1)} collective-permute-done((bf16[4032,128]{1,0:T(8,128)(2,1)S(1)}, bf16[4032,128]{1,0:T(8,128)(2,1)S(1)}, u32[]{:S(2)}, u32[]{:S(2)}) %collective-permute-start.6) | collective-permute-done | bytes 1032224 | tf_op jit(solution)/shard_map/ppermute | solution.py:145
  178.7 0.9 constant_dynamic-update-slice_fusion.3
  179.7 3.7 %collective-permute-done.7 = bf16[4032,128]{1,0:T(8,128)(2,1)S(1)} collective-permute-done((bf16[4032,128]{1,0:T(8,128)(2,1)S(1)}, bf16[4032,128]{1,0:T(8,128)(2,1)S(1)}, u32[]{:S(2)}, u32[]{:S(2)}) %collective-permute-start.7) | collective-permute-done | bytes 1032224 | tf_op jit(solution)/shard_map/ppermute | solution.py:145
  183.3 0.9 constant_dynamic-update-slice_fusion.2
  184.3 0.0 collective-permute-done.8
  184.3 1.5 constant_dynamic-update-slice_fusion.1
  185.8 0.0 copy-start.2
  185.8 0.0 collective-permute-done.9
  185.8 2.0 %copy-done.2 = bf16[672,12,2,128]{3,2,1,0:T(2,128)(2,1)} copy-done((bf16[672,12,2,128]{3,2,1,0:T(2,128)(2,1)}, bf16[672,12,2,128]{3,2,1,0:T(2,128)(2,1)S(1)}, u32[]{:S(2)}) %copy-start.2) | copy-done | bytes 4128792
  187.8 1.1 constant_dynamic-update-slice_fusion
  (7 shorter events, 0.1 us)
Async XLA Ops:
  0.0 1.1 copy-start.1
  2.2 52.0 %all-to-all-start = ((bf16[32,72,128]{2,1,0:T(8,128)(2,1)}), bf16[32,72,128]{2,1,0:T(8,128)(2,1)S(1)}, u32[]{:S(2)}, u32[]{:S(2)}) async-start(bf16[32,72,128]{2,1,0:T(8,128)(2,1)} %shard_map.28), calls=%async_computation | async-start | bytes 1179648 | tf_op jit(solution)/shard_map/all_to_all | solution.py:165
  55.9 29.5 %all-to-all-start.1 = ((bf16[32,40,128]{2,1,0:T(8,128)(2,1)}), bf16[32,40,128]{2,1,0:T(8,128)(2,1)S(1)}, u32[]{:S(2)}, u32[]{:S(2)}) async-start(bf16[32,40,128]{2,1,0:T(8,128)(2,1)} %shard_map.29), calls=%async_computation.1 | async-start | bytes 655360 | tf_op jit(solution)/shard_map/all_to_all | solution.py:186
  61.4 32.5 %collective-permute-start = (bf16[3,48,768]{2,1,0:T(8,128)(2,1)S(1)}, bf16[3,48,768]{2,1,0:T(8,128)(2,1)S(1)}, u32[]{:S(2)}, u32[]{:S(2)}) collective-permute-start(bf16[3,48,768]{2,1,0:T(8,128)(2,1)S(1)} %get-tuple-element.10), channel_id=1, source_target_pairs={{0,32},{32,64},{64,96},{96,0},{1,33},{33,65},{65,97},{97,1},{2,34}... | collective-permute-start | bytes 663560 | tf_op jit(solution)/shard_map/ppermute | solution.py:145
  64.8 29.1 %collective-permute-start.1 = (bf16[3,48,768]{2,1,0:T(8,128)(2,1)S(1)}, bf16[3,48,768]{2,1,0:T(8,128)(2,1)S(1)}, u32[]{:S(2)}, u32[]{:S(2)}) collective-permute-start(bf16[3,48,768]{2,1,0:T(8,128)(2,1)S(1)} %get-tuple-element.9), channel_id=1, source_target_pairs={{0,64},{32,96},{64,0},{96,32},{1,65},{33,97},{65,1},{97,33},{2,66}... | collective-permute-start | bytes 663560 | tf_op jit(solution)/shard_map/ppermute | solution.py:145
  69.5 24.5 %collective-permute-start.2 = (bf16[3,48,768]{2,1,0:T(8,128)(2,1)S(1)}, bf16[3,48,768]{2,1,0:T(8,128)(2,1)S(1)}, u32[]{:S(2)}, u32[]{:S(2)}) collective-permute-start(bf16[3,48,768]{2,1,0:T(8,128)(2,1)S(1)} %get-tuple-element.8), channel_id=1, source_target_pairs={{0,96},{32,0},{64,32},{96,64},{1,97},{33,1},{65,33},{97,65},{2,98}... | collective-permute-start | bytes 663560 | tf_op jit(solution)/shard_map/ppermute | solution.py:145
  86.8 63.7 %all-to-all-start.2 = ((bf16[16,3,48,256]{3,2,1,0:T(8,128)(2,1)}), bf16[16,3,48,256]{3,2,1,0:T(8,128)(2,1)S(1)}, u32[]{:S(2)}, u32[]{:S(2)}) async-start(bf16[16,3,48,256]{3,2,1,0:T(8,128)(2,1)} %shard_map.30), calls=%async_computation.2 | async-start | bytes 2359296 | tf_op jit(solution)/shard_map/all_to_all | solution.py:192
  94.1 36.5 %collective-permute-start.3 = (bf16[4,3,48,768]{3,2,1,0:T(8,128)(2,1)S(1)}, bf16[4,3,48,768]{3,2,1,0:T(8,128)(2,1)S(1)}, u32[]{:S(2)}, u32[]{:S(2)}) collective-permute-start(bf16[4,3,48,768]{3,2,1,0:T(8,128)(2,1)S(1)} %pad_maximum_fusion.p0_ref), channel_id=1, source_target_pairs={{0,192},{32,224},{64,128},{96,160},{128,320},{160,352},{192,256},{... | collective-permute-start | bytes 2654216 | tf_op jit(solution)/shard_map/ppermute | solution.py:154
  99.0 31.7 %collective-permute-start.4 = (bf16[4,3,48,768]{3,2,1,0:T(8,128)(2,1)S(1)}, bf16[4,3,48,768]{3,2,1,0:T(8,128)(2,1)S(1)}, u32[]{:S(2)}, u32[]{:S(2)}) collective-permute-start(bf16[4,3,48,768]{3,2,1,0:T(8,128)(2,1)S(1)} %pad_maximum_fusion.p0_ref), channel_id=1, source_target_pairs={{0,256},{32,288},{64,320},{96,352},{128,384},{160,416},{192,448},{... | collective-permute-start | bytes 2654216 | tf_op jit(solution)/shard_map/ppermute | solution.py:154
  103.3 44.6 %collective-permute-start.5 = (bf16[4,3,48,768]{3,2,1,0:T(8,128)(2,1)S(1)}, bf16[4,3,48,768]{3,2,1,0:T(8,128)(2,1)S(1)}, u32[]{:S(2)}, u32[]{:S(2)}) collective-permute-start(bf16[4,3,48,768]{3,2,1,0:T(8,128)(2,1)S(1)} %pad_maximum_fusion.p0_ref), channel_id=1, source_target_pairs={{0,448},{32,480},{64,384},{96,416},{128,64},{160,96},{192,0},{224,... | collective-permute-start | bytes 2654216 | tf_op jit(solution)/shard_map/ppermute | solution.py:154
  150.5 1.9 copy-start
  153.5 25.3 %collective-permute-start.6 = (bf16[4032,128]{1,0:T(8,128)(2,1)S(1)}, bf16[4032,128]{1,0:T(8,128)(2,1)S(1)}, u32[]{:S(2)}, u32[]{:S(2)}) collective-permute-start(bf16[4032,128]{1,0:T(8,128)(2,1)S(1)} %shard_map.32), channel_id=1, source_target_pairs={{0,96},{32,0},{64,32},{96,64},{1,97},{33,1},{65,33},{97,65},{2,98}... | collective-permute-start | bytes 3096584 | tf_op jit(solution)/shard_map/ppermute | solution.py:145
  157.2 26.1 %collective-permute-start.7 = (bf16[4032,128]{1,0:T(8,128)(2,1)S(1)}, bf16[4032,128]{1,0:T(8,128)(2,1)S(1)}, u32[]{:S(2)}, u32[]{:S(2)}) collective-permute-start(bf16[4032,128]{1,0:T(8,128)(2,1)S(1)} %shard_map.32), channel_id=1, source_target_pairs={{0,32},{32,64},{64,96},{96,0},{1,33},{33,65},{65,97},{97,1},{2,34}... | collective-permute-start | bytes 3096584 | tf_op jit(solution)/shard_map/ppermute | solution.py:145
  160.3 23.9 %collective-permute-start.8 = (bf16[2016,128]{1,0:T(8,128)(2,1)}, bf16[2016,128]{1,0:T(8,128)(2,1)}, u32[]{:S(2)}, u32[]{:S(2)}) collective-permute-start(bf16[2016,128]{1,0:T(8,128)(2,1)} %get-tuple-element.6), channel_id=1, source_target_pairs={{0,128},{128,256},{256,384},{384,0},{1,129},{129,257},{257,385},{3... | collective-permute-start | bytes 1548296 | tf_op jit(solution)/shard_map/ppermute | solution.py:145
  164.0 21.8 %collective-permute-start.9 = (bf16[2016,128]{1,0:T(8,128)(2,1)}, bf16[2016,128]{1,0:T(8,128)(2,1)S(1)}, u32[]{:S(2)}, u32[]{:S(2)}) collective-permute-start(bf16[2016,128]{1,0:T(8,128)(2,1)} %get-tuple-element.5), channel_id=1, source_target_pairs={{0,384},{128,0},{256,128},{384,256},{1,385},{129,1},{257,129},{385... | collective-permute-start | bytes 1548296 | tf_op jit(solution)/shard_map/ppermute | solution.py:145
  185.8 2.0 %copy-start.2 = (bf16[672,12,2,128]{3,2,1,0:T(2,128)(2,1)}, bf16[672,12,2,128]{3,2,1,0:T(2,128)(2,1)S(1)}, u32[]{:S(2)}) copy-start(bf16[672,12,2,128]{3,2,1,0:T(2,128)(2,1)S(1)} %constant_dynamic-update-slice_fusion.1) | copy-start | bytes 12386308

commit v2 on v1

--- a/solution.py
+++ b/solution.py
@@ -21,16 +21,21 @@
 SENT = PAD + PAD // 2
 BACK = 40
 F32, BF16 = jnp.float32, jnp.bfloat16
-VMEM_LIMIT = 48 * 1024 * 1024
+HOPS = (0, 1, 3, 2)
+SHIFTS = (0, 1, 3, 2)
+VMEM_LIMIT = 20 * 1024 * 1024
+CUTS = (0, 384, DEGREES)
+TILES = (9, 7)
 
 
 def call(body, out_shape, scratch=(), n_in=1):
     whole = pl.BlockSpec(memory_space=pltpu.VMEM)
+    many = isinstance(out_shape, list)
     return pl.pallas_call(
         body,
         out_shape=out_shape,
         in_specs=[whole] * n_in,
-        out_specs=whole,
+        out_specs=[whole] * len(out_shape) if many else whole,
         scratch_shapes=list(scratch),
         compiler_params=pltpu.CompilerParams(vmem_limit_bytes=VMEM_LIMIT),
     )
@@ -102,43 +107,86 @@
                     out_ref[t, place, :, lanes] = column
 
 
-def turn_legendre(p0_ref, p1_ref, p2_ref, p3_ref, out_ref, tall):
-    for place in range(OWN):
-        for hop, ref in enumerate((p0_ref, p1_ref, p2_ref, p3_ref)):
+def pack_legendre(legendre_ref, out_ref, wide):
+    lon = lax.axis_index("lon")
+    wide[...] = jnp.zeros_like(wide)
+    degree = lax.broadcasted_iota(jnp.int32, (ROWS, DEGREES), 1)
+    end = DEGREES // CH
+    cut = CUTS[1] // CH
+    for colour in range(SIDE):
+        tails = jnp.zeros((PAD, CH), F32)
+        for place in range(OWN):
+            order = colour * OWN + place
+            value = legendre_ref[order].astype(F32)
+            wide[0:ROWS, 0:DEGREES] = jnp.where(degree >= lon * HELD + order, value, 0.0)
+            for tile in range(end):
+                if tile < cut:
+                    at = place * cut + tile
+                else:
+                    at = TILES[0] + place * (end - cut) + tile - cut
+                lanes = slice(tile * CH, (tile + 1) * CH)
+                out_ref[colour, at] = wide[:, lanes].astype(BF16)
+            tail = wide[:, end * CH : (end + 1) * CH]
+            tails += pltpu.roll(tail, place * (DEGREES - end * CH), 1)
+        out_ref[colour, sum(TILES) - 1] = tails.astype(BF16)
+
+
+def turn_legendre(*refs):
+    *parts, out_ref, tall = refs
+    degrees = out_ref.shape[1]
+    full, size = degrees // CH, degrees % CH
+    for tile in range(parts[0].shape[1]):
+        for hop, part in enumerate(parts):
             for shift in range(SIDE):
                 at = (hop * SIDE + shift) * PAD
-                tall[at : at + PAD, :] = ref[shift, place].astype(F32)
-        out_ref[place] = tall[...].T[0:DEGREES].astype(BF16)
+                tall[at : at + PAD, :] = part[shift, tile].astype(F32)
+        turned = tall[...].T.astype(BF16)
+        place, at = tile // full, tile % full * CH
+        if place < OWN:
+            out_ref[place, at : at + CH, :] = turned
+        else:
+            for place in range(OWN):
+                out_ref[place, full * CH :, :] = turned[place * size : (place + 1) * size]
 
 
 def legendre_sum(s_ref, p_ref, out_ref, gathered, spread):
     y, x = lax.axis_index("y"), lax.axis_index("x")
-    for hop in range(SIDE):
+    for hop, step in enumerate(HOPS):
+        row = lax.rem(y + (SIDE - step), SIDE)
         for shift in range(SIDE):
-            row = lax.rem(y + (SIDE - hop), SIDE)
-            column = lax.rem(x + (3 * SIDE - 2 * hop - shift), SIDE)
+            column = lax.rem(x + (3 * SIDE - 2 * step - SHIFTS[shift]), SIDE)
             at = (hop * SIDE + shift) * PAD
             for place in range(OWN):
                 gathered[place, at : at + PAD, :] = s_ref[row * SIDE + column, place]
     for place in range(OWN):
         found = jnp.dot(p_ref[place], gathered[place], preferred_element_type=F32)
         for part in range(2):
-            rows = pl.ds(2 * place + part, DEGREES, stride=2 * OWN)
+            rows = pl.ds(2 * place + part, p_ref.shape[1], stride=2 * OWN)
             spread[rows, :] = found[:, part * CH : (part + 1) * CH]
     out_ref[...] = spread[...].astype(BF16)
 
 
-def fourier_table():
-    rows = jnp.arange(2 * ORDERS, dtype=jnp.int32)[:, None]
-    columns = jnp.arange(LON * PAD, dtype=jnp.int32)[None, :]
+def fourier_factors():
+    rows = jnp.arange(2 * ORDERS, dtype=jnp.int32)[None, :]
     part = rows % (2 * HELD) // HELD
     order = rows // (2 * HELD) * HELD + rows % HELD
-    within = columns % PAD
-    longitude = columns // PAD * COLS + within
-    phases = ((longitude * order + part * (NLON // 4)) % NLON).astype(F32)
+    device = jnp.arange(LON, dtype=jnp.int32)[:, None]
+    within = jnp.arange(PAD, dtype=jnp.int32)[:, None]
     weight = jnp.where(order == 0, 1.0, 2.0).astype(F32) / jnp.sqrt(F32(NLON))
-    values = weight * jnp.cos(phases * (2.0 * jnp.pi / NLON))
-    return jnp.where(within < COLS, values, 0.0).astype(BF16)
+    weight = jnp.where(within < COLS, weight, 0.0)
+    turn = 2.0 * jnp.pi / NLON
+    first = (device * COLS * order % NLON).astype(F32) * turn
+    rest = ((within * order + part * (NLON // 4)) % NLON).astype(F32) * turn
+    return jnp.cos(first), jnp.sin(first), weight * jnp.cos(rest), weight * jnp.sin(rest)
+
+
+def fourier_table(cos_a, sin_a, cos_b, sin_b, out_ref, tall):
+    for d in range(LON):
+        row = slice(d, d + 1)
+        tall[d * PAD : (d + 1) * PAD, :] = (
+            cos_a[row, :] * cos_b[...] - sin_a[row, :] * sin_b[...]
+        )
+    out_ref[...] = tall[...].T.astype(BF16)
 
 
 def along(axis, value, step):
@@ -155,8 +203,7 @@
 
 
 def on_device(grad_field, legendre):
-    y, x, lon = lax.axis_index("y"), lax.axis_index("x"), lax.axis_index("lon")
-    colour = (x + 2 * y) % SIDE
+    colour = (lax.axis_index("x") + 2 * lax.axis_index("y")) % SIDE
     struct = jax.ShapeDtypeStruct
 
     packed = call(
@@ -164,26 +211,35 @@
     )(grad_field)
     row_columns = lax.all_to_all(packed, "lon", 0, 0, tiled=True)
 
-    order_ids = lon * HELD + jnp.arange(HELD, dtype=jnp.int32)
-    degree_ids = jnp.arange(DEGREES, dtype=jnp.int32)
-    allowed = degree_ids[None, None, :] >= order_ids[:, None, None]
-    masked = jnp.where(allowed, legendre, jnp.zeros_like(legendre))
-    masked = jnp.pad(masked, ((0, 0), (0, PAD - ROWS), (0, 768 - DEGREES)))
-    masked = masked.reshape(SIDE, OWN, PAD, 768)
+    masked = call(
+        pack_legendre,
+        struct((SIDE, sum(TILES), PAD, CH), BF16),
+        [pltpu.VMEM((PAD, 768), F32)],
+    )(legendre)
     line = [lax.dynamic_index_in_dim(masked, colour, 0, keepdims=False)]
-    for step in (1, 2, 3):
+    for step in SHIFTS[1:]:
         theirs = lax.dynamic_index_in_dim(masked, (colour + step) % SIDE, 0, keepdims=False)
         line.append(along("x", theirs, step))
-    line = jnp.stack(line)
-    lines = [line] + [same_colour(line, step) for step in (1, 2, 3)]
+    table = call(
+        fourier_table,
+        struct((2 * ORDERS, LON * PAD), BF16),
+        [pltpu.VMEM((LON * PAD, 2 * ORDERS), F32)],
+        n_in=4,
+    )(*fourier_factors())
+    first = jnp.stack([part[: TILES[0]] for part in line])
+    second = jnp.stack([part[TILES[0] :] for part in line])
+    one, three, two = (same_colour(first, step) for step in HOPS[1:])
+    one_b, three_b, two_b = (same_colour(second, step) for step in HOPS[1:])
+    row_columns, one = lax.optimization_barrier((row_columns, one))
 
     returned = call(
         spectrum_rows,
         struct((LON, BACK, CH), BF16),
         [pltpu.VMEM((LON * PAD, 2 * CH), BF16)],
         n_in=2,
-    )(row_columns, fourier_table())
+    )(row_columns, table)
     by_sender = lax.all_to_all(returned, "lon", 0, 0, tiled=True)
+    by_sender, three, two, one_b = lax.optimization_barrier((by_sender, three, two, one_b))
     turned = call(
         turn_rows,
         struct((LAT, OWN, PAD, 2 * CH), BF16),
@@ -191,37 +247,39 @@
     )(by_sender)
     spectrum = lax.all_to_all(turned, ("y", "x"), 0, 0, tiled=True)
 
-    upright = call(
-        turn_legendre,
-        struct((OWN, DEGREES, LAT * PAD), BF16),
-        [pltpu.VMEM((LAT * PAD, 768), F32)],
-        n_in=4,
-    )(*lines)
-    own = call(
-        legendre_sum,
-        struct((DEGREES * OWN * 2, CH), BF16),
-        [
-            pltpu.VMEM((OWN, LAT * PAD, 2 * CH), BF16),
-            pltpu.VMEM((DEGREES * OWN * 2, CH), F32),
-        ],
-        n_in=2,
-    )(spectrum, upright)
-
-    middle = DEGREES * OWN
-    after = along("x", own, -1)
-    before = along("x", own, 1)
-    low = along("y", own[:middle], 1)
-    high = along("y", own[middle:], -1)
-    parts = [(own, 0), (after, 1), (before, 3)]
+    sums = []
+    for span, blocks in enumerate(
+        [(first, one, three, two), (second, one_b, three_b, two_b)]
+    ):
+        degrees = CUTS[span + 1] - CUTS[span]
+        upright = call(
+            turn_legendre,
+            struct((OWN, degrees, LAT * PAD), BF16),
+            [pltpu.VMEM((LAT * PAD, CH), F32)],
+            n_in=SIDE,
+        )(*blocks)
+        found = call(
+            legendre_sum,
+            struct((degrees * OWN * 2, CH), BF16),
+            [
+                pltpu.VMEM((OWN, LAT * PAD, 2 * CH), BF16),
+                pltpu.VMEM((degrees * OWN * 2, CH), F32),
+            ],
+            n_in=2,
+        )(spectrum, upright)
+        sums.append(found)
+
+    parts = []
+    for span, found in enumerate(sums):
+        parts.append((span, 1, along("x", found, -1)))
+        parts.append((span, 3, along("x", found, 1)))
+        parts.append((span, 2, along("y", found, 1 - 2 * span)))
+    parts = [(0, 0, sums[0]), (1, 0, sums[1])] + sorted(parts, key=lambda p: (p[0], p[1] != 2))
     out = jnp.zeros((DEGREES, HELD, 2, CH), BF16)
-    for value, step in parts:
-        value = value.reshape(DEGREES, OWN, 2, CH)
+    for span, step, value in parts:
+        value = value.reshape(-1, OWN, 2, CH)
         at = (colour + step) % SIDE * OWN
-        out = lax.dynamic_update_slice(out, value, (0, at, 0, 0))
-    at = (colour + 2) % SIDE * OWN
-    for value, start in ((low, 0), (high, DEGREES // 2)):
-        value = value.reshape(DEGREES // 2, OWN, 2, CH)
-        out = lax.dynamic_update_slice(out, value, (start, at, 0, 0))
+        out = lax.dynamic_update_slice(out, value, (CUTS[span], at, 0, 0))
     return out
 
 

time: 192 us -> 166 us (0.86)
  the two profiles are of different devices: /device:TPU:24 before, /device:TPU:32 now
where the time goes in v2:
time: 166 us; the launch traced here: 165 us
  starting transfers between devices  89.4 us (54%)
  waiting for transfers between devices  45.8 us (28%)
  local copies, waits for them, and re-layouts  16.9 us (10%)
  Pallas kernels  9.82 us (6%)
  other arithmetic  2.02 us (1%)
    ppermute x9, starting transfers between devices, along(): lax.ppermute(value, axis, [(i, (i + step) % SIDE) for i in range(SIDE)])  31.9 us
    ppermute x6, starting transfers between devices, same_colour(): return lax.ppermute(value, ('y', 'x'), pairs)  25.1 us
    ppermute x6, waiting for transfers between devices, same_colour(): return lax.ppermute(value, ('y', 'x'), pairs)  22.7 us
    ppermute x9, waiting for transfers between devices, along(): lax.ppermute(value, axis, [(i, (i + step) % SIDE) for i in range(SIDE)])  16.7 us
    all_to_all x1, starting transfers between devices, on_device(): row_columns = lax.all_to_all(packed, 'lon', 0, 0, tiled=True)  15.4 us
    all_to_all x1, starting transfers between devices, on_device(): by_sender = lax.all_to_all(returned, 'lon', 0, 0, tiled=True)  12.2 us
    unnamed x28, local copies, waits for them, and re-layouts  9.28 us
    all_to_all x1, waiting for transfers between devices, on_device(): spectrum = lax.all_to_all(turned, ('y', 'x'), 0, 0, tiled=True)  6.37 us
  transfers between devices with their start and end apart: 18, of which 8 were waited for; matrix products, arithmetic and copies ran while one was open for 5% of the time, Pallas kernels for 3%

profile of v2, /device:TPU:32, one launch (start us, length us, event | category | flops | bytes accessed | tf_op | source)
XLA Modules:
  0.0 164.5 jit_solution(4441428492156360911)
XLA Ops:
  0.0 1.0 copy-done.3
  1.1 1.1 shard_map.28
  2.2 15.4 %all-to-all-start = ((bf16[32,72,128]{2,1,0:T(8,128)(2,1)}), bf16[32,72,128]{2,1,0:T(8,128)(2,1)}, u32[]{:S(2)}, u32[]{:S(2)}) async-start(bf16[32,72,128]{2,1,0:T(8,128)(2,1)} %shard_map.28), calls=%async_computation | async-start | bytes 1179648 | tf_op jit(solution)/shard_map/all_to_all | solution.py:212
  17.7 1.2 copy-done.2
  19.2 4.9 %collective-permute-start.2 = (bf16[16,48,128]{2,1,0:T(8,128)(2,1)S(1)}, bf16[16,48,128]{2,1,0:T(8,128)(2,1)S(1)}, u32[]{:S(2)}, u32[]{:S(2)}) collective-permute-start(bf16[16,48,128]{2,1,0:T(8,128)(2,1)S(1)} %get-tuple-element.18), channel_id=1, source_target_pairs={{0,64},{32,96},{64,0},{96,32},{1,65},{33,97},{65,1},{97,33},{2,66}... | collective-permute-start | bytes 589832 | tf_op jit(solution)/shard_map/ppermute | solution.py:193
  24.1 3.0 %collective-permute-start.1 = (bf16[16,48,128]{2,1,0:T(8,128)(2,1)S(1)}, bf16[16,48,128]{2,1,0:T(8,128)(2,1)S(1)}, u32[]{:S(2)}, u32[]{:S(2)}) collective-permute-start(bf16[16,48,128]{2,1,0:T(8,128)(2,1)S(1)} %get-tuple-element.19), channel_id=1, source_target_pairs={{0,96},{32,0},{64,32},{96,64},{1,97},{33,1},{65,33},{97,65},{2,98}... | collective-permute-start | bytes 589832 | tf_op jit(solution)/shard_map/ppermute | solution.py:193
  27.2 2.8 %collective-permute-start = (bf16[16,48,128]{2,1,0:T(8,128)(2,1)S(1)}, bf16[16,48,128]{2,1,0:T(8,128)(2,1)S(1)}, u32[]{:S(2)}, u32[]{:S(2)}) collective-permute-start(bf16[16,48,128]{2,1,0:T(8,128)(2,1)S(1)} %get-tuple-element.17), channel_id=1, source_target_pairs={{0,32},{32,64},{64,96},{96,0},{1,33},{33,65},{65,97},{97,1},{2,34}... | collective-permute-start | bytes 589832 | tf_op jit(solution)/shard_map/ppermute | solution.py:193
  30.1 3.7 %collective-permute-done.1 = bf16[16,48,128]{2,1,0:T(8,128)(2,1)S(1)} collective-permute-done((bf16[16,48,128]{2,1,0:T(8,128)(2,1)S(1)}, bf16[16,48,128]{2,1,0:T(8,128)(2,1)S(1)}, u32[]{:S(2)}, u32[]{:S(2)}) %collective-permute-start.1) | collective-permute-done | bytes 196640 | tf_op jit(solution)/shard_map/ppermute | solution.py:193
  33.9 2.8 %collective-permute-done = bf16[16,48,128]{2,1,0:T(8,128)(2,1)S(1)} collective-permute-done((bf16[16,48,128]{2,1,0:T(8,128)(2,1)S(1)}, bf16[16,48,128]{2,1,0:T(8,128)(2,1)S(1)}, u32[]{:S(2)}, u32[]{:S(2)}) %collective-permute-start) | collective-permute-done | bytes 196640 | tf_op jit(solution)/shard_map/ppermute | solution.py:193
  36.8 3.2 %collective-permute-start.3 = (bf16[4,9,48,128]{3,2,1,0:T(8,128)(2,1)S(1)}, bf16[4,9,48,128]{3,2,1,0:T(8,128)(2,1)S(1)}, u32[]{:S(2)}, u32[]{:S(2)}) collective-permute-start(bf16[4,9,48,128]{3,2,1,0:T(8,128)(2,1)S(1)} %pad_maximum_fusion.refs_0_), channel_id=1, source_target_pairs={{0,192},{32,224},{64,128},{96,160},{128,320},{160,352},{192,256},{... | collective-permute-start | bytes 1327112 | tf_op jit(solution)/shard_map/ppermute | solution.py:202
  40.5 0.7 select_multiply_fusion
  41.2 0.9 shard_map.30.table_ref
  42.1 11.1 %collective-permute-done.3.refs_1_ = bf16[4,9,48,128]{3,2,1,0:T(8,128)(2,1)S(1)} collective-permute-done((bf16[4,9,48,128]{3,2,1,0:T(8,128)(2,1)S(1)}, bf16[4,9,48,128]{3,2,1,0:T(8,128)(2,1)S(1)}, u32[]{:S(2)}, u32[]{:S(2)}) %collective-permute-start.3) | collective-permute-done | bytes 442400 | tf_op jit(solution)/shard_map/ppermute | solution.py:202
  53.2 0.8 copy-done.4
  53.9 2.8 %shard_map.31 = bf16[32,40,128]{2,1,0:T(8,128)(2,1)} custom-call(bf16[32,72,128]{2,1,0:T(8,128)(2,1)} %all-to-all-done.x_ref, bf16[768,1536]{1,0:T(8,128)(2,1)S(1)} %shard_map.30.table_ref), custom_call_target="tpu_custom_call" | custom-call | tf_op jit(solution)/shard_map/pallas_call | solution.py:235
  56.7 12.2 %all-to-all-start.1 = ((bf16[32,40,128]{2,1,0:T(8,128)(2,1)}), bf16[32,40,128]{2,1,0:T(8,128)(2,1)S(1)}, u32[]{:S(2)}, u32[]{:S(2)}) async-start(bf16[32,40,128]{2,1,0:T(8,128)(2,1)} %shard_map.31), calls=%async_computation.1 | async-start | bytes 655360 | tf_op jit(solution)/shard_map/all_to_all | solution.py:241
  68.9 3.6 %collective-permute-start.4 = (bf16[4,9,48,128]{3,2,1,0:T(8,128)(2,1)}, bf16[4,9,48,128]{3,2,1,0:T(8,128)(2,1)S(1)}, u32[]{:S(2)}, u32[]{:S(2)}) collective-permute-start(bf16[4,9,48,128]{3,2,1,0:T(8,128)(2,1)} %copy-done), channel_id=1, source_target_pairs={{0,448},{32,480},{64,384},{96,416},{128,64},{160,96},{192,0},{224,... | collective-permute-start | bytes 1327112 | tf_op jit(solution)/shard_map/ppermute | solution.py:202
  72.5 2.5 %collective-permute-start.5 = (bf16[4,9,48,128]{3,2,1,0:T(8,128)(2,1)}, bf16[4,9,48,128]{3,2,1,0:T(8,128)(2,1)S(1)}, u32[]{:S(2)}, u32[]{:S(2)}) collective-permute-start(bf16[4,9,48,128]{3,2,1,0:T(8,128)(2,1)} %copy-done), channel_id=1, source_target_pairs={{0,256},{32,288},{64,320},{96,352},{128,384},{160,416},{192,448},{... | collective-permute-start | bytes 1327112 | tf_op jit(solution)/shard_map/ppermute | solution.py:202
  75.1 0.9 slice_bitcast_fusion.5
  76.0 0.8 pad_maximum_fusion.1.refs_0_
  76.8 5.5 %collective-permute-start.6 = (bf16[4,7,48,128]{3,2,1,0:T(8,128)(2,1)}, bf16[4,7,48,128]{3,2,1,0:T(8,128)(2,1)S(1)}, u32[]{:S(2)}, u32[]{:S(2)}) collective-permute-start(bf16[4,7,48,128]{3,2,1,0:T(8,128)(2,1)} %pad_maximum_fusion.1.refs_0_), channel_id=1, source_target_pairs={{0,192},{32,224},{64,128},{96,160},{128,320},{160,352},{192,256},{... | collective-permute-start | bytes 1032200 | tf_op jit(solution)/shard_map/ppermute | solution.py:202
  82.3 11.4 %collective-permute-done.6.refs_1_ = bf16[4,7,48,128]{3,2,1,0:T(8,128)(2,1)S(1)} collective-permute-done((bf16[4,7,48,128]{3,2,1,0:T(8,128)(2,1)}, bf16[4,7,48,128]{3,2,1,0:T(8,128)(2,1)S(1)}, u32[]{:S(2)}, u32[]{:S(2)}) %collective-permute-start.6) | collective-permute-done | bytes 344096 | tf_op jit(solution)/shard_map/ppermute | solution.py:202
  93.7 0.7 copy-done.10
  94.4 0.8 copy-done.6
  95.4 0.8 copy-done.8
  96.2 1.3 shard_map.32
  97.6 4.8 %all-to-all-start.2 = ((bf16[16,3,48,256]{3,2,1,0:T(8,128)(2,1)}), bf16[16,3,48,256]{3,2,1,0:T(8,128)(2,1)S(1)}, u32[]{:S(2)}, u32[]{:S(2)}) async-start(bf16[16,3,48,256]{3,2,1,0:T(8,128)(2,1)} %shard_map.32), calls=%async_computation.2 | async-start | bytes 2359296 | tf_op jit(solution)/shard_map/all_to_all | solution.py:248
  102.4 7.4 %collective-permute-start.7 = (bf16[4,7,48,128]{3,2,1,0:T(8,128)(2,1)}, bf16[4,7,48,128]{3,2,1,0:T(8,128)(2,1)}, u32[]{:S(2)}, u32[]{:S(2)}) collective-permute-start(bf16[4,7,48,128]{3,2,1,0:T(8,128)(2,1)} %pad_maximum_fusion.1.refs_0_), channel_id=1, source_target_pairs={{0,448},{32,480},{64,384},{96,416},{128,64},{160,96},{192,0},{224,... | collective-permute-start | bytes 1032200 | tf_op jit(solution)/shard_map/ppermute | solution.py:202
  109.8 2.8 %collective-permute-start.8 = (bf16[4,7,48,128]{3,2,1,0:T(8,128)(2,1)}, bf16[4,7,48,128]{3,2,1,0:T(8,128)(2,1)}, u32[]{:S(2)}, u32[]{:S(2)}) collective-permute-start(bf16[4,7,48,128]{3,2,1,0:T(8,128)(2,1)} %pad_maximum_fusion.1.refs_0_), channel_id=1, source_target_pairs={{0,256},{32,288},{64,320},{96,352},{128,384},{160,416},{192,448},{... | collective-permute-start | bytes 1032200 | tf_op jit(solution)/shard_map/ppermute | solution.py:202
  112.6 1.0 copy-done.5
  113.6 1.0 copy-done.7
  114.6 1.0 copy-done.9
  116.2 6.4 %all-to-all-done.2.s_ref = bf16[16,3,48,256]{3,2,1,0:T(8,128)(2,1)S(1)} async-done(((bf16[16,3,48,256]{3,2,1,0:T(8,128)(2,1)}), bf16[16,3,48,256]{3,2,1,0:T(8,128)(2,1)S(1)}, u32[]{:S(2)}, u32[]{:S(2)}) %all-to-all-start.2) | async-done | bytes 1179680 | tf_op jit(solution)/shard_map/all_to_all | solution.py:248
  122.6 0.7 shard_map.34
  123.2 1.9 %collective-permute-start.9 = (bf16[2304,128]{1,0:T(8,128)(2,1)S(1)}, bf16[2304,128]{1,0:T(8,128)(2,1)S(1)}, u32[]{:S(2)}, u32[]{:S(2)}) collective-permute-start(bf16[2304,128]{1,0:T(8,128)(2,1)S(1)} %shard_map.34), channel_id=1, source_target_pairs={{0,128},{128,256},{256,384},{384,0},{1,129},{129,257},{257,385},{3... | collective-permute-start | bytes 1769480 | tf_op jit(solution)/shard_map/ppermute | solution.py:193
  125.2 2.3 %collective-permute-start.10 = (bf16[2304,128]{1,0:T(8,128)(2,1)S(1)}, bf16[2304,128]{1,0:T(8,128)(2,1)S(1)}, u32[]{:S(2)}, u32[]{:S(2)}) collective-permute-start(bf16[2304,128]{1,0:T(8,128)(2,1)S(1)} %shard_map.34), channel_id=1, source_target_pairs={{0,96},{32,0},{64,32},{96,64},{1,97},{33,1},{65,33},{97,65},{2,98}... | collective-permute-start | bytes 1769480 | tf_op jit(solution)/shard_map/ppermute | solution.py:193
  127.4 3.6 %collective-permute-start.11 = (bf16[2304,128]{1,0:T(8,128)(2,1)S(1)}, bf16[2304,128]{1,0:T(8,128)(2,1)S(1)}, u32[]{:S(2)}, u32[]{:S(2)}) collective-permute-start(bf16[2304,128]{1,0:T(8,128)(2,1)S(1)} %shard_map.34), channel_id=1, source_target_pairs={{0,32},{32,64},{64,96},{96,0},{1,33},{33,65},{65,97},{97,1},{2,34}... | collective-permute-start | bytes 1769480 | tf_op jit(solution)/shard_map/ppermute | solution.py:193
  131.1 1.0 copy-done.11
  132.1 1.6 shard_map.35.p_ref
  133.7 0.6 shard_map.36
  134.3 6.4 %collective-permute-start.12 = (bf16[1728,128]{1,0:T(8,128)(2,1)S(1)}, bf16[1728,128]{1,0:T(8,128)(2,1)S(1)}, u32[]{:S(2)}, u32[]{:S(2)}) collective-permute-start(bf16[1728,128]{1,0:T(8,128)(2,1)S(1)} %shard_map.36), channel_id=1, source_target_pairs={{0,384},{128,0},{256,128},{384,256},{1,385},{129,1},{257,129},{385... | collective-permute-start | bytes 1327112 | tf_op jit(solution)/shard_map/ppermute | solution.py:193
  140.7 5.1 %collective-permute-start.13 = (bf16[1728,128]{1,0:T(8,128)(2,1)S(1)}, bf16[1728,128]{1,0:T(8,128)(2,1)S(1)}, u32[]{:S(2)}, u32[]{:S(2)}) collective-permute-start(bf16[1728,128]{1,0:T(8,128)(2,1)S(1)} %shard_map.36), channel_id=1, source_target_pairs={{0,96},{32,0},{64,32},{96,64},{1,97},{33,1},{65,33},{97,65},{2,98}... | collective-permute-start | bytes 1327112 | tf_op jit(solution)/shard_map/ppermute | solution.py:193
  145.8 2.1 %broadcast_in_dim.38 = bf16[672,12,2,128]{3,2,1,0:T(2,128)(2,1)S(1)} broadcast(bf16[]{:T(256)} %constant.118.clone.1), dimensions={} | broadcast | bytes 4128770 | tf_op jit(solution)/shard_map/broadcast_in_dim | solution.py:278
  147.9 0.5 constant_dynamic-update-slice_fusion.7
  148.9 1.9 %collective-permute-start.14 = (bf16[1728,128]{1,0:T(8,128)(2,1)S(1)}, bf16[1728,128]{1,0:T(8,128)(2,1)S(1)}, u32[]{:S(2)}, u32[]{:S(2)}) collective-permute-start(bf16[1728,128]{1,0:T(8,128)(2,1)S(1)} %shard_map.36), channel_id=1, source_target_pairs={{0,32},{32,64},{64,96},{96,0},{1,33},{33,65},{65,97},{97,1},{2,34}... | collective-permute-start | bytes 1327112 | tf_op jit(solution)/shard_map/ppermute | solution.py:193
  152.9 1.9 %collective-permute-done.13 = bf16[1728,128]{1,0:T(8,128)(2,1)S(1)} collective-permute-done((bf16[1728,128]{1,0:T(8,128)(2,1)S(1)}, bf16[1728,128]{1,0:T(8,128)(2,1)S(1)}, u32[]{:S(2)}, u32[]{:S(2)}) %collective-permute-start.13) | collective-permute-done | bytes 442400 | tf_op jit(solution)/shard_map/ppermute | solution.py:193
  155.2 8.2 %collective-permute-done.14 = bf16[1728,128]{1,0:T(8,128)(2,1)S(1)} collective-permute-done((bf16[1728,128]{1,0:T(8,128)(2,1)S(1)}, bf16[1728,128]{1,0:T(8,128)(2,1)S(1)}, u32[]{:S(2)}, u32[]{:S(2)}) %collective-permute-start.14) | collective-permute-done | bytes 442400 | tf_op jit(solution)/shard_map/ppermute | solution.py:193
  163.4 1.1 constant_dynamic-update-slice_fusion
  (51 shorter events, 4.7 us)
Async XLA Ops:
  0.0 1.1 copy-start.3
  2.2 51.7 %all-to-all-start = ((bf16[32,72,128]{2,1,0:T(8,128)(2,1)}), bf16[32,72,128]{2,1,0:T(8,128)(2,1)}, u32[]{:S(2)}, u32[]{:S(2)}) async-start(bf16[32,72,128]{2,1,0:T(8,128)(2,1)} %shard_map.28), calls=%async_computation | async-start | bytes 1179648 | tf_op jit(solution)/shard_map/all_to_all | solution.py:212
  17.7 1.2 copy-start.2
  19.2 10.9 %collective-permute-start.2 = (bf16[16,48,128]{2,1,0:T(8,128)(2,1)S(1)}, bf16[16,48,128]{2,1,0:T(8,128)(2,1)S(1)}, u32[]{:S(2)}, u32[]{:S(2)}) collective-permute-start(bf16[16,48,128]{2,1,0:T(8,128)(2,1)S(1)} %get-tuple-element.18), channel_id=1, source_target_pairs={{0,64},{32,96},{64,0},{96,32},{1,65},{33,97},{65,1},{97,33},{2,66}... | collective-permute-start | bytes 589832 | tf_op jit(solution)/shard_map/ppermute | solution.py:193
  24.1 9.7 %collective-permute-start.1 = (bf16[16,48,128]{2,1,0:T(8,128)(2,1)S(1)}, bf16[16,48,128]{2,1,0:T(8,128)(2,1)S(1)}, u32[]{:S(2)}, u32[]{:S(2)}) collective-permute-start(bf16[16,48,128]{2,1,0:T(8,128)(2,1)S(1)} %get-tuple-element.19), channel_id=1, source_target_pairs={{0,96},{32,0},{64,32},{96,64},{1,97},{33,1},{65,33},{97,65},{2,98}... | collective-permute-start | bytes 589832 | tf_op jit(solution)/shard_map/ppermute | solution.py:193
  27.2 9.5 %collective-permute-start = (bf16[16,48,128]{2,1,0:T(8,128)(2,1)S(1)}, bf16[16,48,128]{2,1,0:T(8,128)(2,1)S(1)}, u32[]{:S(2)}, u32[]{:S(2)}) collective-permute-start(bf16[16,48,128]{2,1,0:T(8,128)(2,1)S(1)} %get-tuple-element.17), channel_id=1, source_target_pairs={{0,32},{32,64},{64,96},{96,0},{1,33},{33,65},{65,97},{97,1},{2,34}... | collective-permute-start | bytes 589832 | tf_op jit(solution)/shard_map/ppermute | solution.py:193
  36.7 4.5 %copy-start.13 = (bf16[16,48,128]{2,1,0:T(8,128)(2,1)}, bf16[16,48,128]{2,1,0:T(8,128)(2,1)S(1)}, u32[]{:S(2)}) copy-start(bf16[16,48,128]{2,1,0:T(8,128)(2,1)S(1)} %collective-permute-done) | copy-start | bytes 589828
  36.8 4.4 %copy-start = (bf16[4,9,48,128]{3,2,1,0:T(8,128)(2,1)}, bf16[4,9,48,128]{3,2,1,0:T(8,128)(2,1)S(1)}, u32[]{:S(2)}) copy-start(bf16[4,9,48,128]{3,2,1,0:T(8,128)(2,1)S(1)} %pad_maximum_fusion.refs_0_) | copy-start | bytes 1327108
  36.8 16.4 %collective-permute-start.3 = (bf16[4,9,48,128]{3,2,1,0:T(8,128)(2,1)S(1)}, bf16[4,9,48,128]{3,2,1,0:T(8,128)(2,1)S(1)}, u32[]{:S(2)}, u32[]{:S(2)}) collective-permute-start(bf16[4,9,48,128]{3,2,1,0:T(8,128)(2,1)S(1)} %pad_maximum_fusion.refs_0_), channel_id=1, source_target_pairs={{0,192},{32,224},{64,128},{96,160},{128,320},{160,352},{192,256},{... | collective-permute-start | bytes 1327112 | tf_op jit(solution)/shard_map/ppermute | solution.py:202
  53.2 0.8 copy-start.4
  56.7 39.5 %all-to-all-start.1 = ((bf16[32,40,128]{2,1,0:T(8,128)(2,1)}), bf16[32,40,128]{2,1,0:T(8,128)(2,1)S(1)}, u32[]{:S(2)}, u32[]{:S(2)}) async-start(bf16[32,40,128]{2,1,0:T(8,128)(2,1)} %shard_map.31), calls=%async_computation.1 | async-start | bytes 655360 | tf_op jit(solution)/shard_map/all_to_all | solution.py:241
  68.9 43.7 %copy-start.1 = (bf16[4,9,48,128]{3,2,1,0:T(8,128)(2,1)S(1)}, bf16[4,9,48,128]{3,2,1,0:T(8,128)(2,1)}, u32[]{:S(2)}) copy-start(bf16[4,9,48,128]{3,2,1,0:T(8,128)(2,1)} %copy-done) | copy-start | bytes 1327108
  68.9 25.5 %collective-permute-start.4 = (bf16[4,9,48,128]{3,2,1,0:T(8,128)(2,1)}, bf16[4,9,48,128]{3,2,1,0:T(8,128)(2,1)S(1)}, u32[]{:S(2)}, u32[]{:S(2)}) collective-permute-start(bf16[4,9,48,128]{3,2,1,0:T(8,128)(2,1)} %copy-done), channel_id=1, source_target_pairs={{0,448},{32,480},{64,384},{96,416},{128,64},{160,96},{192,0},{224,... | collective-permute-start | bytes 1327112 | tf_op jit(solution)/shard_map/ppermute | solution.py:202
  72.5 22.9 %collective-permute-start.5 = (bf16[4,9,48,128]{3,2,1,0:T(8,128)(2,1)}, bf16[4,9,48,128]{3,2,1,0:T(8,128)(2,1)S(1)}, u32[]{:S(2)}, u32[]{:S(2)}) collective-permute-start(bf16[4,9,48,128]{3,2,1,0:T(8,128)(2,1)} %copy-done), channel_id=1, source_target_pairs={{0,256},{32,288},{64,320},{96,352},{128,384},{160,416},{192,448},{... | collective-permute-start | bytes 1327112 | tf_op jit(solution)/shard_map/ppermute | solution.py:202
  76.8 16.9 %collective-permute-start.6 = (bf16[4,7,48,128]{3,2,1,0:T(8,128)(2,1)}, bf16[4,7,48,128]{3,2,1,0:T(8,128)(2,1)S(1)}, u32[]{:S(2)}, u32[]{:S(2)}) collective-permute-start(bf16[4,7,48,128]{3,2,1,0:T(8,128)(2,1)} %pad_maximum_fusion.1.refs_0_), channel_id=1, source_target_pairs={{0,192},{32,224},{64,128},{96,160},{128,320},{160,352},{192,256},{... | collective-permute-start | bytes 1032200 | tf_op jit(solution)/shard_map/ppermute | solution.py:202
  93.7 0.7 copy-start.10
  94.4 0.8 copy-start.6
  95.4 0.8 copy-start.8
  97.6 25.0 %all-to-all-start.2 = ((bf16[16,3,48,256]{3,2,1,0:T(8,128)(2,1)}), bf16[16,3,48,256]{3,2,1,0:T(8,128)(2,1)S(1)}, u32[]{:S(2)}, u32[]{:S(2)}) async-start(bf16[16,3,48,256]{3,2,1,0:T(8,128)(2,1)} %shard_map.32), calls=%async_computation.2 | async-start | bytes 2359296 | tf_op jit(solution)/shard_map/all_to_all | solution.py:248
  102.4 28.7 %collective-permute-start.7 = (bf16[4,7,48,128]{3,2,1,0:T(8,128)(2,1)}, bf16[4,7,48,128]{3,2,1,0:T(8,128)(2,1)}, u32[]{:S(2)}, u32[]{:S(2)}) collective-permute-start(bf16[4,7,48,128]{3,2,1,0:T(8,128)(2,1)} %pad_maximum_fusion.1.refs_0_), channel_id=1, source_target_pairs={{0,448},{32,480},{64,384},{96,416},{128,64},{160,96},{192,0},{224,... | collective-permute-start | bytes 1032200 | tf_op jit(solution)/shard_map/ppermute | solution.py:202
  109.8 21.3 %collective-permute-start.8 = (bf16[4,7,48,128]{3,2,1,0:T(8,128)(2,1)}, bf16[4,7,48,128]{3,2,1,0:T(8,128)(2,1)}, u32[]{:S(2)}, u32[]{:S(2)}) collective-permute-start(bf16[4,7,48,128]{3,2,1,0:T(8,128)(2,1)} %pad_maximum_fusion.1.refs_0_), channel_id=1, source_target_pairs={{0,256},{32,288},{64,320},{96,352},{128,384},{160,416},{192,448},{... | collective-permute-start | bytes 1032200 | tf_op jit(solution)/shard_map/ppermute | solution.py:202
  112.6 1.0 copy-start.5
  113.6 1.0 copy-start.7
  114.6 1.0 copy-start.9
  123.2 25.6 %collective-permute-start.9 = (bf16[2304,128]{1,0:T(8,128)(2,1)S(1)}, bf16[2304,128]{1,0:T(8,128)(2,1)S(1)}, u32[]{:S(2)}, u32[]{:S(2)}) collective-permute-start(bf16[2304,128]{1,0:T(8,128)(2,1)S(1)} %shard_map.34), channel_id=1, source_target_pairs={{0,128},{128,256},{256,384},{384,0},{1,129},{129,257},{257,385},{3... | collective-permute-start | bytes 1769480 | tf_op jit(solution)/shard_map/ppermute | solution.py:193
  125.2 26.2 %collective-permute-start.10 = (bf16[2304,128]{1,0:T(8,128)(2,1)S(1)}, bf16[2304,128]{1,0:T(8,128)(2,1)S(1)}, u32[]{:S(2)}, u32[]{:S(2)}) collective-permute-start(bf16[2304,128]{1,0:T(8,128)(2,1)S(1)} %shard_map.34), channel_id=1, source_target_pairs={{0,96},{32,0},{64,32},{96,64},{1,97},{33,1},{65,33},{97,65},{2,98}... | collective-permute-start | bytes 1769480 | tf_op jit(solution)/shard_map/ppermute | solution.py:193
  127.4 24.5 %collective-permute-start.11 = (bf16[2304,128]{1,0:T(8,128)(2,1)S(1)}, bf16[2304,128]{1,0:T(8,128)(2,1)S(1)}, u32[]{:S(2)}, u32[]{:S(2)}) collective-permute-start(bf16[2304,128]{1,0:T(8,128)(2,1)S(1)} %shard_map.34), channel_id=1, source_target_pairs={{0,32},{32,64},{64,96},{96,0},{1,33},{33,65},{65,97},{97,1},{2,34}... | collective-permute-start | bytes 1769480 | tf_op jit(solution)/shard_map/ppermute | solution.py:193
  131.1 1.0 copy-start.11
  134.3 18.2 %collective-permute-start.12 = (bf16[1728,128]{1,0:T(8,128)(2,1)S(1)}, bf16[1728,128]{1,0:T(8,128)(2,1)S(1)}, u32[]{:S(2)}, u32[]{:S(2)}) collective-permute-start(bf16[1728,128]{1,0:T(8,128)(2,1)S(1)} %shard_map.36), channel_id=1, source_target_pairs={{0,384},{128,0},{256,128},{384,256},{1,385},{129,1},{257,129},{385... | collective-permute-start | bytes 1327112 | tf_op jit(solution)/shard_map/ppermute | solution.py:193
  140.7 14.1 %collective-permute-start.13 = (bf16[1728,128]{1,0:T(8,128)(2,1)S(1)}, bf16[1728,128]{1,0:T(8,128)(2,1)S(1)}, u32[]{:S(2)}, u32[]{:S(2)}) collective-permute-start(bf16[1728,128]{1,0:T(8,128)(2,1)S(1)} %shard_map.36), channel_id=1, source_target_pairs={{0,96},{32,0},{64,32},{96,64},{1,97},{33,1},{65,33},{97,65},{2,98}... | collective-permute-start | bytes 1327112 | tf_op jit(solution)/shard_map/ppermute | solution.py:193
  148.9 14.6 %collective-permute-start.14 = (bf16[1728,128]{1,0:T(8,128)(2,1)S(1)}, bf16[1728,128]{1,0:T(8,128)(2,1)S(1)}, u32[]{:S(2)}, u32[]{:S(2)}) collective-permute-start(bf16[1728,128]{1,0:T(8,128)(2,1)S(1)} %shard_map.36), channel_id=1, source_target_pairs={{0,32},{32,64},{64,96},{96,0},{1,33},{33,65},{65,97},{97,1},{2,34}... | collective-permute-start | bytes 1327112 | tf_op jit(solution)/shard_map/ppermute | solution.py:193
  155.2 8.2 %copy-start.12 = (bf16[672,12,2,128]{3,2,1,0:T(2,128)(2,1)}, bf16[672,12,2,128]{3,2,1,0:T(2,128)(2,1)S(1)}, u32[]{:S(2)}) copy-start(bf16[672,12,2,128]{3,2,1,0:T(2,128)(2,1)S(1)} %constant_dynamic-update-slice_fusion.1) | copy-start | bytes 12386308

commit v3 on v2

--- a/solution.py
+++ b/solution.py
@@ -23,12 +23,15 @@
 F32, BF16 = jnp.float32, jnp.bfloat16
 HOPS = (0, 1, 3, 2)
 SHIFTS = (0, 1, 3, 2)
-VMEM_LIMIT = 20 * 1024 * 1024
-CUTS = (0, 384, DEGREES)
-TILES = (9, 7)
-
-
-def call(body, out_shape, scratch=(), n_in=1):
+MIB = 1024 * 1024
+FULL = DEGREES // CH
+TAIL = DEGREES % CH
+TILES = OWN * FULL + 1
+
+LONG = pl.CostEstimate(flops=10**11, transcendentals=0, bytes_accessed=10**9)
+
+
+def call(body, out_shape, scratch=(), n_in=1, vmem=8, cost=None):
     whole = pl.BlockSpec(memory_space=pltpu.VMEM)
     many = isinstance(out_shape, list)
     return pl.pallas_call(
@@ -37,7 +40,8 @@
         in_specs=[whole] * n_in,
         out_specs=[whole] * len(out_shape) if many else whole,
         scratch_shapes=list(scratch),
-        compiler_params=pltpu.CompilerParams(vmem_limit_bytes=VMEM_LIMIT),
+        cost_estimate=cost,
+        compiler_params=pltpu.CompilerParams(vmem_limit_bytes=vmem * MIB),
     )
 
 
@@ -111,42 +115,35 @@
     lon = lax.axis_index("lon")
     wide[...] = jnp.zeros_like(wide)
     degree = lax.broadcasted_iota(jnp.int32, (ROWS, DEGREES), 1)
-    end = DEGREES // CH
-    cut = CUTS[1] // CH
     for colour in range(SIDE):
         tails = jnp.zeros((PAD, CH), F32)
         for place in range(OWN):
             order = colour * OWN + place
             value = legendre_ref[order].astype(F32)
             wide[0:ROWS, 0:DEGREES] = jnp.where(degree >= lon * HELD + order, value, 0.0)
-            for tile in range(end):
-                if tile < cut:
-                    at = place * cut + tile
-                else:
-                    at = TILES[0] + place * (end - cut) + tile - cut
+            for tile in range(FULL):
                 lanes = slice(tile * CH, (tile + 1) * CH)
-                out_ref[colour, at] = wide[:, lanes].astype(BF16)
-            tail = wide[:, end * CH : (end + 1) * CH]
-            tails += pltpu.roll(tail, place * (DEGREES - end * CH), 1)
-        out_ref[colour, sum(TILES) - 1] = tails.astype(BF16)
+                out_ref[colour, place * FULL + tile] = wide[:, lanes].astype(BF16)
+            tail = wide[:, FULL * CH : (FULL + 1) * CH]
+            tails += pltpu.roll(tail, place * TAIL, 1)
+        out_ref[colour, TILES - 1] = tails.astype(BF16)
 
 
 def turn_legendre(*refs):
     *parts, out_ref, tall = refs
-    degrees = out_ref.shape[1]
-    full, size = degrees // CH, degrees % CH
-    for tile in range(parts[0].shape[1]):
+    for tile in range(TILES):
         for hop, part in enumerate(parts):
             for shift in range(SIDE):
                 at = (hop * SIDE + shift) * PAD
                 tall[at : at + PAD, :] = part[shift, tile].astype(F32)
         turned = tall[...].T.astype(BF16)
-        place, at = tile // full, tile % full * CH
-        if place < OWN:
+        if tile == TILES - 1:
+            for place in range(OWN):
+                rows = slice(place * TAIL, (place + 1) * TAIL)
+                out_ref[place, FULL * CH : DEGREES, :] = turned[rows]
+        else:
+            place, at = tile // FULL, tile % FULL * CH
             out_ref[place, at : at + CH, :] = turned
-        else:
-            for place in range(OWN):
-                out_ref[place, full * CH :, :] = turned[place * size : (place + 1) * size]
 
 
 def legendre_sum(s_ref, p_ref, out_ref, gathered, spread):
@@ -161,7 +158,7 @@
     for place in range(OWN):
         found = jnp.dot(p_ref[place], gathered[place], preferred_element_type=F32)
         for part in range(2):
-            rows = pl.ds(2 * place + part, p_ref.shape[1], stride=2 * OWN)
+            rows = pl.ds(2 * place + part, DEGREES, stride=2 * OWN)
             spread[rows, :] = found[:, part * CH : (part + 1) * CH]
     out_ref[...] = spread[...].astype(BF16)
 
@@ -213,8 +210,8 @@
 
     masked = call(
         pack_legendre,
-        struct((SIDE, sum(TILES), PAD, CH), BF16),
-        [pltpu.VMEM((PAD, 768), F32)],
+        struct((SIDE, TILES, PAD, CH), BF16),
+        [pltpu.VMEM((PAD, (FULL + 1) * CH), F32)],
     )(legendre)
     line = [lax.dynamic_index_in_dim(masked, colour, 0, keepdims=False)]
     for step in SHIFTS[1:]:
@@ -225,12 +222,17 @@
         struct((2 * ORDERS, LON * PAD), BF16),
         [pltpu.VMEM((LON * PAD, 2 * ORDERS), F32)],
         n_in=4,
+        vmem=16,
     )(*fourier_factors())
-    first = jnp.stack([part[: TILES[0]] for part in line])
-    second = jnp.stack([part[TILES[0] :] for part in line])
-    one, three, two = (same_colour(first, step) for step in HOPS[1:])
-    one_b, three_b, two_b = (same_colour(second, step) for step in HOPS[1:])
-    row_columns, one = lax.optimization_barrier((row_columns, one))
+    line = jnp.stack(line)
+    lines = [line] + [same_colour(line, step) for step in HOPS[1:]]
+    upright = call(
+        turn_legendre,
+        struct((OWN, DEGREES, LAT * PAD), BF16),
+        [pltpu.VMEM((LAT * PAD, CH), F32)],
+        n_in=SIDE,
+        cost=LONG,
+    )(*lines)
 
     returned = call(
         spectrum_rows,
@@ -239,7 +241,7 @@
         n_in=2,
     )(row_columns, table)
     by_sender = lax.all_to_all(returned, "lon", 0, 0, tiled=True)
-    by_sender, three, two, one_b = lax.optimization_barrier((by_sender, three, two, one_b))
+    by_sender, upright = lax.optimization_barrier((by_sender, upright))
     turned = call(
         turn_rows,
         struct((LAT, OWN, PAD, 2 * CH), BF16),
@@ -247,39 +249,27 @@
     )(by_sender)
     spectrum = lax.all_to_all(turned, ("y", "x"), 0, 0, tiled=True)
 
-    sums = []
-    for span, blocks in enumerate(
-        [(first, one, three, two), (second, one_b, three_b, two_b)]
-    ):
-        degrees = CUTS[span + 1] - CUTS[span]
-        upright = call(
-            turn_legendre,
-            struct((OWN, degrees, LAT * PAD), BF16),
-            [pltpu.VMEM((LAT * PAD, CH), F32)],
-            n_in=SIDE,
-        )(*blocks)
-        found = call(
-            legendre_sum,
-            struct((degrees * OWN * 2, CH), BF16),
-            [
-                pltpu.VMEM((OWN, LAT * PAD, 2 * CH), BF16),
-                pltpu.VMEM((degrees * OWN * 2, CH), F32),
-            ],
-            n_in=2,
-        )(spectrum, upright)
-        sums.append(found)
-
-    parts = []
-    for span, found in enumerate(sums):
-        parts.append((span, 1, along("x", found, -1)))
-        parts.append((span, 3, along("x", found, 1)))
-        parts.append((span, 2, along("y", found, 1 - 2 * span)))
-    parts = [(0, 0, sums[0]), (1, 0, sums[1])] + sorted(parts, key=lambda p: (p[0], p[1] != 2))
+    middle = DEGREES * OWN
+    own = call(
+        legendre_sum,
+        struct((2 * middle, CH), BF16),
+        [
+            pltpu.VMEM((OWN, LAT * PAD, 2 * CH), BF16),
+            pltpu.VMEM((2 * middle, CH), F32),
+        ],
+        n_in=2,
+    )(spectrum, upright)
+
+    after = along("x", own, -1)
+    before = along("x", own, 1)
+    low = along("y", own[:middle], 1)
+    high = along("y", own[middle:], -1)
+    parts = [(own, 0, 0), (low, 2, 0), (high, 2, DEGREES // 2), (after, 1, 0), (before, 3, 0)]
     out = jnp.zeros((DEGREES, HELD, 2, CH), BF16)
-    for span, step, value in parts:
+    for value, step, start in parts:
         value = value.reshape(-1, OWN, 2, CH)
         at = (colour + step) % SIDE * OWN
-        out = lax.dynamic_update_slice(out, value, (CUTS[span], at, 0, 0))
+        out = lax.dynamic_update_slice(out, value, (start, at, 0, 0))
     return out
 
 

time: 166 us -> 147 us (0.89)
  the two profiles are of different devices: /device:TPU:32 before, /device:TPU:24 now
where the time goes in v3:
time: 147 us; the launch traced here: 146 us
  starting transfers between devices  58.5 us (40%)
  waiting for transfers between devices  39.4 us (27%)
  blocking collectives  22.9 us (16%)
  local copies, waits for them, and re-layouts  14.9 us (10%)
  Pallas kernels  8.14 us (6%)
  other arithmetic  2.16 us (1%)
    ppermute x7, starting transfers between devices, along(): lax.ppermute(value, axis, [(i, (i + step) % SIDE) for i in range(SIDE)])  23 us
    all_to_all x1, blocking collectives, on_device(): spectrum = lax.all_to_all(turned, ('y', 'x'), 0, 0, tiled=True)  22.9 us
    ppermute x3, waiting for transfers between devices, same_colour(): return lax.ppermute(value, ('y', 'x'), pairs)  19.2 us
    all_to_all x1, starting transfers between devices, on_device(): row_columns = lax.all_to_all(packed, 'lon', 0, 0, tiled=True)  15.5 us
    ppermute x7, waiting for transfers between devices, along(): lax.ppermute(value, axis, [(i, (i + step) % SIDE) for i in range(SIDE)])  14.8 us
    ppermute x3, starting transfers between devices, same_colour(): return lax.ppermute(value, ('y', 'x'), pairs)  11.4 us
    all_to_all x1, starting transfers between devices, on_device(): by_sender = lax.all_to_all(returned, 'lon', 0, 0, tiled=True)  8.62 us
    dynamic_update_slice x5, local copies, waits for them, and re-layouts, on_device(): out = lax.dynamic_update_slice(out, value, (start, at, 0, 0))  6.59 us
  transfers between devices with their start and end apart: 12, of which 9 were waited for; matrix products, arithmetic and copies ran while one was open for 7% of the time, Pallas kernels for 4%

profile of v3, /device:TPU:24, one launch (start us, length us, event | category | flops | bytes accessed | tf_op | source)
XLA Modules:
  0.0 146.4 jit_solution(4045139392912987821)
XLA Ops:
  0.0 1.0 copy-done.3
  1.1 1.2 shard_map.28
  2.2 15.5 %all-to-all-start = ((bf16[32,72,128]{2,1,0:T(8,128)(2,1)}), bf16[32,72,128]{2,1,0:T(8,128)(2,1)S(1)}, u32[]{:S(2)}, u32[]{:S(2)}) async-start(bf16[32,72,128]{2,1,0:T(8,128)(2,1)} %shard_map.28), calls=%async_computation | async-start | bytes 1179648 | tf_op jit(solution)/shard_map/all_to_all | solution.py:209
  17.8 0.0 copy-start.2
  17.8 1.2 copy-done.2
  18.9 0.3 shard_map.31
  19.2 0.1 constant_dynamic-slice_fusion
  19.3 3.4 %collective-permute-start = (bf16[16,48,128]{2,1,0:T(8,128)(2,1)S(1)}, bf16[16,48,128]{2,1,0:T(8,128)(2,1)S(1)}, u32[]{:S(2)}, u32[]{:S(2)}) collective-permute-start(bf16[16,48,128]{2,1,0:T(8,128)(2,1)S(1)} %get-tuple-element.14), channel_id=1, source_target_pairs={{0,32},{32,64},{64,96},{96,0},{1,33},{33,65},{65,97},{97,1},{2,34}... | collective-permute-start | bytes 589832 | tf_op jit(solution)/shard_map/ppermute | solution.py:190
  22.7 3.7 %collective-permute-start.1 = (bf16[16,48,128]{2,1,0:T(8,128)(2,1)S(1)}, bf16[16,48,128]{2,1,0:T(8,128)(2,1)S(1)}, u32[]{:S(2)}, u32[]{:S(2)}) collective-permute-start(bf16[16,48,128]{2,1,0:T(8,128)(2,1)S(1)} %get-tuple-element.13), channel_id=1, source_target_pairs={{0,96},{32,0},{64,32},{96,64},{1,97},{33,1},{65,33},{97,65},{2,98}... | collective-permute-start | bytes 589832 | tf_op jit(solution)/shard_map/ppermute | solution.py:190
  26.4 3.7 %collective-permute-start.2 = (bf16[16,48,128]{2,1,0:T(8,128)(2,1)S(1)}, bf16[16,48,128]{2,1,0:T(8,128)(2,1)S(1)}, u32[]{:S(2)}, u32[]{:S(2)}) collective-permute-start(bf16[16,48,128]{2,1,0:T(8,128)(2,1)S(1)} %get-tuple-element.12), channel_id=1, source_target_pairs={{0,64},{32,96},{64,0},{96,32},{1,65},{33,97},{65,1},{97,33},{2,66}... | collective-permute-start | bytes 589832 | tf_op jit(solution)/shard_map/ppermute | solution.py:190
  30.1 0.0 collective-permute-done
  30.1 4.8 %collective-permute-done.1 = bf16[16,48,128]{2,1,0:T(8,128)(2,1)S(1)} collective-permute-done((bf16[16,48,128]{2,1,0:T(8,128)(2,1)S(1)}, bf16[16,48,128]{2,1,0:T(8,128)(2,1)S(1)}, u32[]{:S(2)}, u32[]{:S(2)}) %collective-permute-start.1) | collective-permute-done | bytes 196640 | tf_op jit(solution)/shard_map/ppermute | solution.py:190
  34.9 1.4 collective-permute-done.2
  36.3 1.0 pad_maximum_fusion.refs_0_
  37.3 3.4 %collective-permute-start.3 = (bf16[4,16,48,128]{3,2,1,0:T(8,128)(2,1)}, bf16[4,16,48,128]{3,2,1,0:T(8,128)(2,1)}, u32[]{:S(2)}, u32[]{:S(2)}) collective-permute-start(bf16[4,16,48,128]{3,2,1,0:T(8,128)(2,1)} %pad_maximum_fusion.refs_0_), channel_id=1, source_target_pairs={{0,192},{32,224},{64,128},{96,160},{128,320},{160,352},{192,256},{... | collective-permute-start | bytes 2359304 | tf_op jit(solution)/shard_map/ppermute | solution.py:199
  40.7 4.9 %collective-permute-start.4 = (bf16[4,16,48,128]{3,2,1,0:T(8,128)(2,1)}, bf16[4,16,48,128]{3,2,1,0:T(8,128)(2,1)}, u32[]{:S(2)}, u32[]{:S(2)}) collective-permute-start(bf16[4,16,48,128]{3,2,1,0:T(8,128)(2,1)} %pad_maximum_fusion.refs_0_), channel_id=1, source_target_pairs={{0,448},{32,480},{64,384},{96,416},{128,64},{160,96},{192,0},{224,... | collective-permute-start | bytes 2359304 | tf_op jit(solution)/shard_map/ppermute | solution.py:199
  45.5 3.1 %collective-permute-start.5 = (bf16[4,16,48,128]{3,2,1,0:T(8,128)(2,1)}, bf16[4,16,48,128]{3,2,1,0:T(8,128)(2,1)}, u32[]{:S(2)}, u32[]{:S(2)}) collective-permute-start(bf16[4,16,48,128]{3,2,1,0:T(8,128)(2,1)} %pad_maximum_fusion.refs_0_), channel_id=1, source_target_pairs={{0,256},{32,288},{64,320},{96,352},{128,384},{160,416},{192,448},{... | collective-permute-start | bytes 2359304 | tf_op jit(solution)/shard_map/ppermute | solution.py:199
  48.7 0.5 fusion.9
  49.2 0.7 select_multiply_fusion
  49.9 0.9 shard_map.29.table_ref
  50.8 3.4 %all-to-all-done.x_ref = bf16[32,72,128]{2,1,0:T(8,128)(2,1)S(1)} async-done(((bf16[32,72,128]{2,1,0:T(8,128)(2,1)}), bf16[32,72,128]{2,1,0:T(8,128)(2,1)S(1)}, u32[]{:S(2)}, u32[]{:S(2)}) %all-to-all-start) | async-done | bytes 589856 | tf_op jit(solution)/shard_map/all_to_all | solution.py:209
  54.2 1.7 %shard_map.30 = bf16[32,40,128]{2,1,0:T(8,128)(2,1)} custom-call(bf16[32,72,128]{2,1,0:T(8,128)(2,1)S(1)} %all-to-all-done.x_ref, bf16[768,1536]{1,0:T(8,128)(2,1)S(1)} %shard_map.29.table_ref), custom_call_target="tpu_custom_call" | custom-call | tf_op jit(solution)/shard_map/pallas_call | solution.py:237
  55.9 8.6 %all-to-all-start.1 = ((bf16[32,40,128]{2,1,0:T(8,128)(2,1)}), bf16[32,40,128]{2,1,0:T(8,128)(2,1)S(1)}, u32[]{:S(2)}, u32[]{:S(2)}) async-start(bf16[32,40,128]{2,1,0:T(8,128)(2,1)} %shard_map.30), calls=%async_computation.1 | async-start | bytes 655360 | tf_op jit(solution)/shard_map/all_to_all | solution.py:243
  64.6 13.4 %collective-permute-done.4.refs_2_ = bf16[4,16,48,128]{3,2,1,0:T(8,128)(2,1)} collective-permute-done((bf16[4,16,48,128]{3,2,1,0:T(8,128)(2,1)}, bf16[4,16,48,128]{3,2,1,0:T(8,128)(2,1)}, u32[]{:S(2)}, u32[]{:S(2)}) %collective-permute-start.4) | collective-permute-done | bytes 786464 | tf_op jit(solution)/shard_map/ppermute | solution.py:199
  77.9 5.9 %collective-permute-done.5.refs_3_ = bf16[4,16,48,128]{3,2,1,0:T(8,128)(2,1)} collective-permute-done((bf16[4,16,48,128]{3,2,1,0:T(8,128)(2,1)}, bf16[4,16,48,128]{3,2,1,0:T(8,128)(2,1)}, u32[]{:S(2)}, u32[]{:S(2)}) %collective-permute-start.5) | collective-permute-done | bytes 786464 | tf_op jit(solution)/shard_map/ppermute | solution.py:199
  83.8 2.7 %shard_map.32.p_ref = bf16[3,672,768]{2,1,0:T(8,128)(2,1)S(1)} custom-call(bf16[4,16,48,128]{3,2,1,0:T(8,128)(2,1)} %pad_maximum_fusion.refs_0_, bf16[4,16,48,128]{3,2,1,0:T(8,128)(2,1)} %collective-permute-done.3.refs_1_, bf16[4,16,48,128]{3,2,1,0:T(8,128)(2,1)} %collective-permute-done.4.refs_2_, bf16[4,16,48,128]{3,2,1,0:T(8,128)(2,1)} %collective-permute-done.5.refs_3_), custom_call_target="tpu_custom_call" | custom-call | flops 99999997952 | bytes 1000000000 | tf_op jit(solution)/shard_map/pallas_call | solution.py:229
  86.5 0.0 copy-start
  86.5 1.6 %copy-done = bf16[3,672,768]{2,1,0:T(8,128)(2,1)} copy-done((bf16[3,672,768]{2,1,0:T(8,128)(2,1)}, bf16[3,672,768]{2,1,0:T(8,128)(2,1)S(1)}, u32[]{:S(2)}) %copy-start) | copy-done | bytes 3096600
  88.2 1.9 %all-to-all-done.1.r_ref = bf16[32,40,128]{2,1,0:T(8,128)(2,1)S(1)} async-done(((bf16[32,40,128]{2,1,0:T(8,128)(2,1)}), bf16[32,40,128]{2,1,0:T(8,128)(2,1)S(1)}, u32[]{:S(2)}, u32[]{:S(2)}) %all-to-all-start.1) | async-done | bytes 327712 | tf_op jit(solution)/shard_map/all_to_all | solution.py:243
  90.0 0.3 shard_map.33
  90.4 22.9 %all_to_all.15.s_ref = bf16[16,3,48,256]{3,2,1,0:T(8,128)(2,1)S(1)} all-to-all(bf16[16,3,48,256]{3,2,1,0:T(8,128)(2,1)S(1)} %shard_map.33), channel_id=1, replica_groups=mesh['y'=4,'x'=4,'lon'=32] {'y','x'}, dimensions={0} | all-to-all | bytes 2359296 | tf_op jit(solution)/shard_map/all_to_all | solution.py:250
  113.3 1.1 shard_map.34
  114.4 3.1 %collective-permute-start.8 = (bf16[4032,128]{1,0:T(8,128)(2,1)S(1)}, bf16[4032,128]{1,0:T(8,128)(2,1)S(1)}, u32[]{:S(2)}, u32[]{:S(2)}) collective-permute-start(bf16[4032,128]{1,0:T(8,128)(2,1)S(1)} %shard_map.34), channel_id=1, source_target_pairs={{0,96},{32,0},{64,32},{96,64},{1,97},{33,1},{65,33},{97,65},{2,98}... | collective-permute-start | bytes 3096584 | tf_op jit(solution)/shard_map/ppermute | solution.py:190
  117.5 2.7 %collective-permute-start.9 = (bf16[4032,128]{1,0:T(8,128)(2,1)S(1)}, bf16[4032,128]{1,0:T(8,128)(2,1)S(1)}, u32[]{:S(2)}, u32[]{:S(2)}) collective-permute-start(bf16[4032,128]{1,0:T(8,128)(2,1)S(1)} %shard_map.34), channel_id=1, source_target_pairs={{0,32},{32,64},{64,96},{96,0},{1,33},{33,65},{65,97},{97,1},{2,34}... | collective-permute-start | bytes 3096584 | tf_op jit(solution)/shard_map/ppermute | solution.py:190
  120.2 1.0 fusion.33
  121.3 4.3 %collective-permute-start.6 = (bf16[2016,128]{1,0:T(8,128)(2,1)}, bf16[2016,128]{1,0:T(8,128)(2,1)}, u32[]{:S(2)}, u32[]{:S(2)}) collective-permute-start(bf16[2016,128]{1,0:T(8,128)(2,1)} %get-tuple-element.10), channel_id=1, source_target_pairs={{0,128},{128,256},{256,384},{384,0},{1,129},{129,257},{257,385},{3... | collective-permute-start | bytes 1548296 | tf_op jit(solution)/shard_map/ppermute | solution.py:190
  125.6 2.1 %collective-permute-start.7 = (bf16[2016,128]{1,0:T(8,128)(2,1)}, bf16[2016,128]{1,0:T(8,128)(2,1)}, u32[]{:S(2)}, u32[]{:S(2)}) collective-permute-start(bf16[2016,128]{1,0:T(8,128)(2,1)} %get-tuple-element.9), channel_id=1, source_target_pairs={{0,384},{128,0},{256,128},{384,256},{1,385},{129,1},{257,129},{385... | collective-permute-start | bytes 1548296 | tf_op jit(solution)/shard_map/ppermute | solution.py:190
  127.7 2.1 %broadcast_in_dim.38 = bf16[672,12,2,128]{3,2,1,0:T(2,128)(2,1)S(1)} broadcast(bf16[]{:T(256)} %constant.112.clone.1), dimensions={} | broadcast | bytes 4128770 | tf_op jit(solution)/shard_map/broadcast_in_dim | solution.py:268
  129.9 0.9 constant_dynamic-update-slice_fusion.4
  130.8 4.4 %collective-permute-done.6 = bf16[2016,128]{1,0:T(8,128)(2,1)} collective-permute-done((bf16[2016,128]{1,0:T(8,128)(2,1)}, bf16[2016,128]{1,0:T(8,128)(2,1)}, u32[]{:S(2)}, u32[]{:S(2)}) %collective-permute-start.6) | collective-permute-done | bytes 516128 | tf_op jit(solution)/shard_map/ppermute | solution.py:190
  135.3 1.5 %constant_dynamic-update-slice_fusion.3 = bf16[672,12,2,128]{3,2,1,0:T(2,128)(2,1)S(1)} fusion(bf16[672,12,2,128]{3,2,1,0:T(2,128)(2,1)S(1)} %constant_dynamic-update-slice_fusion.4, bf16[336,3,2,128]{3,2,1,0:T(2,128)(2,1)} %bitcast.7, s32[]{:T(128)S(6)} %select_n.168), kind=kLoop, calls=%fused_computation.53 | loop fusion | bytes 1032196 | tf_op jit(solution)/shard_map/dynamic_update_slice | solution.py:272
  136.8 3.4 %collective-permute-done.7 = bf16[2016,128]{1,0:T(8,128)(2,1)} collective-permute-done((bf16[2016,128]{1,0:T(8,128)(2,1)}, bf16[2016,128]{1,0:T(8,128)(2,1)}, u32[]{:S(2)}, u32[]{:S(2)}) %collective-permute-start.7) | collective-permute-done | bytes 516128 | tf_op jit(solution)/shard_map/ppermute | solution.py:190
  140.2 1.5 %constant_dynamic-update-slice_fusion.2 = bf16[672,12,2,128]{3,2,1,0:T(2,128)(2,1)S(1)} fusion(bf16[672,12,2,128]{3,2,1,0:T(2,128)(2,1)S(1)} %constant_dynamic-update-slice_fusion.3, bf16[336,3,2,128]{3,2,1,0:T(2,128)(2,1)} %bitcast.8, s32[]{:T(128)S(6)} %select_n.168), kind=kLoop, calls=%fused_computation.52 | loop fusion | bytes 1032196 | tf_op jit(solution)/shard_map/dynamic_update_slice | solution.py:272
  141.7 0.9 constant_dynamic-update-slice_fusion.1
  142.7 0.0 copy-start.4
  142.7 0.8 collective-permute-done.9
  143.5 1.2 copy-done.4
  144.7 1.7 %constant_dynamic-update-slice_fusion = bf16[672,12,2,128]{3,2,1,0:T(2,128)(2,1)} fusion(bf16[672,12,2,128]{3,2,1,0:T(2,128)(2,1)} %copy-done.4, bf16[672,3,2,128]{3,2,1,0:T(2,128)(2,1)S(1)} %bitcast.15, s32[]{:T(128)S(6)} %select_n.170), kind=kLoop, calls=%fused_computation.50 | loop fusion | bytes 2064388 | tf_op jit(solution)/shard_map/dynamic_update_slice | solution.py:272
  (9 shorter events, 0.1 us)
Async XLA Ops:
  0.0 1.1 copy-start.3
  2.2 52.0 %all-to-all-start = ((bf16[32,72,128]{2,1,0:T(8,128)(2,1)}), bf16[32,72,128]{2,1,0:T(8,128)(2,1)S(1)}, u32[]{:S(2)}, u32[]{:S(2)}) async-start(bf16[32,72,128]{2,1,0:T(8,128)(2,1)} %shard_map.28), calls=%async_computation | async-start | bytes 1179648 | tf_op jit(solution)/shard_map/all_to_all | solution.py:209
  17.8 1.2 copy-start.2
  19.3 10.8 %collective-permute-start = (bf16[16,48,128]{2,1,0:T(8,128)(2,1)S(1)}, bf16[16,48,128]{2,1,0:T(8,128)(2,1)S(1)}, u32[]{:S(2)}, u32[]{:S(2)}) collective-permute-start(bf16[16,48,128]{2,1,0:T(8,128)(2,1)S(1)} %get-tuple-element.14), channel_id=1, source_target_pairs={{0,32},{32,64},{64,96},{96,0},{1,33},{33,65},{65,97},{97,1},{2,34}... | collective-permute-start | bytes 589832 | tf_op jit(solution)/shard_map/ppermute | solution.py:190
  22.7 12.2 %collective-permute-start.1 = (bf16[16,48,128]{2,1,0:T(8,128)(2,1)S(1)}, bf16[16,48,128]{2,1,0:T(8,128)(2,1)S(1)}, u32[]{:S(2)}, u32[]{:S(2)}) collective-permute-start(bf16[16,48,128]{2,1,0:T(8,128)(2,1)S(1)} %get-tuple-element.13), channel_id=1, source_target_pairs={{0,96},{32,0},{64,32},{96,64},{1,97},{33,1},{65,33},{97,65},{2,98}... | collective-permute-start | bytes 589832 | tf_op jit(solution)/shard_map/ppermute | solution.py:190
  26.4 9.9 %collective-permute-start.2 = (bf16[16,48,128]{2,1,0:T(8,128)(2,1)S(1)}, bf16[16,48,128]{2,1,0:T(8,128)(2,1)S(1)}, u32[]{:S(2)}, u32[]{:S(2)}) collective-permute-start(bf16[16,48,128]{2,1,0:T(8,128)(2,1)S(1)} %get-tuple-element.12), channel_id=1, source_target_pairs={{0,64},{32,96},{64,0},{96,32},{1,65},{33,97},{65,1},{97,33},{2,66}... | collective-permute-start | bytes 589832 | tf_op jit(solution)/shard_map/ppermute | solution.py:190
  37.3 27.3 %collective-permute-start.3 = (bf16[4,16,48,128]{3,2,1,0:T(8,128)(2,1)}, bf16[4,16,48,128]{3,2,1,0:T(8,128)(2,1)}, u32[]{:S(2)}, u32[]{:S(2)}) collective-permute-start(bf16[4,16,48,128]{3,2,1,0:T(8,128)(2,1)} %pad_maximum_fusion.refs_0_), channel_id=1, source_target_pairs={{0,192},{32,224},{64,128},{96,160},{128,320},{160,352},{192,256},{... | collective-permute-start | bytes 2359304 | tf_op jit(solution)/shard_map/ppermute | solution.py:199
  40.7 37.3 %collective-permute-start.4 = (bf16[4,16,48,128]{3,2,1,0:T(8,128)(2,1)}, bf16[4,16,48,128]{3,2,1,0:T(8,128)(2,1)}, u32[]{:S(2)}, u32[]{:S(2)}) collective-permute-start(bf16[4,16,48,128]{3,2,1,0:T(8,128)(2,1)} %pad_maximum_fusion.refs_0_), channel_id=1, source_target_pairs={{0,448},{32,480},{64,384},{96,416},{128,64},{160,96},{192,0},{224,... | collective-permute-start | bytes 2359304 | tf_op jit(solution)/shard_map/ppermute | solution.py:199
  45.5 38.3 %collective-permute-start.5 = (bf16[4,16,48,128]{3,2,1,0:T(8,128)(2,1)}, bf16[4,16,48,128]{3,2,1,0:T(8,128)(2,1)}, u32[]{:S(2)}, u32[]{:S(2)}) collective-permute-start(bf16[4,16,48,128]{3,2,1,0:T(8,128)(2,1)} %pad_maximum_fusion.refs_0_), channel_id=1, source_target_pairs={{0,256},{32,288},{64,320},{96,352},{128,384},{160,416},{192,448},{... | collective-permute-start | bytes 2359304 | tf_op jit(solution)/shard_map/ppermute | solution.py:199
  55.9 34.1 %all-to-all-start.1 = ((bf16[32,40,128]{2,1,0:T(8,128)(2,1)}), bf16[32,40,128]{2,1,0:T(8,128)(2,1)S(1)}, u32[]{:S(2)}, u32[]{:S(2)}) async-start(bf16[32,40,128]{2,1,0:T(8,128)(2,1)} %shard_map.30), calls=%async_computation.1 | async-start | bytes 655360 | tf_op jit(solution)/shard_map/all_to_all | solution.py:243
  86.5 1.7 %copy-start = (bf16[3,672,768]{2,1,0:T(8,128)(2,1)}, bf16[3,672,768]{2,1,0:T(8,128)(2,1)S(1)}, u32[]{:S(2)}) copy-start(bf16[3,672,768]{2,1,0:T(8,128)(2,1)S(1)} %shard_map.32.p_ref) | copy-start | bytes 9289732
  90.0 23.3 %copy-start.1 = (bf16[3,672,768]{2,1,0:T(8,128)(2,1)S(1)}, bf16[3,672,768]{2,1,0:T(8,128)(2,1)}, u32[]{:S(2)}) copy-start(bf16[3,672,768]{2,1,0:T(8,128)(2,1)} %copy-done) | copy-start | bytes 9289732
  114.4 27.4 %collective-permute-start.8 = (bf16[4032,128]{1,0:T(8,128)(2,1)S(1)}, bf16[4032,128]{1,0:T(8,128)(2,1)S(1)}, u32[]{:S(2)}, u32[]{:S(2)}) collective-permute-start(bf16[4032,128]{1,0:T(8,128)(2,1)S(1)} %shard_map.34), channel_id=1, source_target_pairs={{0,96},{32,0},{64,32},{96,64},{1,97},{33,1},{65,33},{97,65},{2,98}... | collective-permute-start | bytes 3096584 | tf_op jit(solution)/shard_map/ppermute | solution.py:190
  117.5 25.9 %collective-permute-start.9 = (bf16[4032,128]{1,0:T(8,128)(2,1)S(1)}, bf16[4032,128]{1,0:T(8,128)(2,1)S(1)}, u32[]{:S(2)}, u32[]{:S(2)}) collective-permute-start(bf16[4032,128]{1,0:T(8,128)(2,1)S(1)} %shard_map.34), channel_id=1, source_target_pairs={{0,32},{32,64},{64,96},{96,0},{1,33},{33,65},{65,97},{97,1},{2,34}... | collective-permute-start | bytes 3096584 | tf_op jit(solution)/shard_map/ppermute | solution.py:190
  121.3 14.0 %collective-permute-start.6 = (bf16[2016,128]{1,0:T(8,128)(2,1)}, bf16[2016,128]{1,0:T(8,128)(2,1)}, u32[]{:S(2)}, u32[]{:S(2)}) collective-permute-start(bf16[2016,128]{1,0:T(8,128)(2,1)} %get-tuple-element.10), channel_id=1, source_target_pairs={{0,128},{128,256},{256,384},{384,0},{1,129},{129,257},{257,385},{3... | collective-permute-start | bytes 1548296 | tf_op jit(solution)/shard_map/ppermute | solution.py:190
  125.6 14.7 %collective-permute-start.7 = (bf16[2016,128]{1,0:T(8,128)(2,1)}, bf16[2016,128]{1,0:T(8,128)(2,1)}, u32[]{:S(2)}, u32[]{:S(2)}) collective-permute-start(bf16[2016,128]{1,0:T(8,128)(2,1)} %get-tuple-element.9), channel_id=1, source_target_pairs={{0,384},{128,0},{256,128},{384,256},{1,385},{129,1},{257,129},{385... | collective-permute-start | bytes 1548296 | tf_op jit(solution)/shard_map/ppermute | solution.py:190
  142.7 2.0 %copy-start.4 = (bf16[672,12,2,128]{3,2,1,0:T(2,128)(2,1)}, bf16[672,12,2,128]{3,2,1,0:T(2,128)(2,1)S(1)}, u32[]{:S(2)}) copy-start(bf16[672,12,2,128]{3,2,1,0:T(2,128)(2,1)S(1)} %constant_dynamic-update-slice_fusion.1) | copy-start | bytes 12386308

commit v4 on v3

--- a/solution.py
+++ b/solution.py
@@ -22,7 +22,7 @@
 BACK = 40
 F32, BF16 = jnp.float32, jnp.bfloat16
 HOPS = (0, 1, 3, 2)
-SHIFTS = (0, 1, 3, 2)
+NEAR = ((0, 0), (-1, 0), (0, -1), (0, 1))
 MIB = 1024 * 1024
 FULL = DEGREES // CH
 TAIL = DEGREES % CH
@@ -149,9 +149,9 @@
 def legendre_sum(s_ref, p_ref, out_ref, gathered, spread):
     y, x = lax.axis_index("y"), lax.axis_index("x")
     for hop, step in enumerate(HOPS):
-        row = lax.rem(y + (SIDE - step), SIDE)
-        for shift in range(SIDE):
-            column = lax.rem(x + (3 * SIDE - 2 * step - SHIFTS[shift]), SIDE)
+        for shift, (rows, columns) in enumerate(NEAR):
+            row = lax.rem(y + (2 * SIDE - step + rows), SIDE)
+            column = lax.rem(x + (3 * SIDE - 2 * step + columns), SIDE)
             at = (hop * SIDE + shift) * PAD
             for place in range(OWN):
                 gathered[place, at : at + PAD, :] = s_ref[row * SIDE + column, place]
@@ -214,9 +214,11 @@
         [pltpu.VMEM((PAD, (FULL + 1) * CH), F32)],
     )(legendre)
     line = [lax.dynamic_index_in_dim(masked, colour, 0, keepdims=False)]
-    for step in SHIFTS[1:]:
-        theirs = lax.dynamic_index_in_dim(masked, (colour + step) % SIDE, 0, keepdims=False)
-        line.append(along("x", theirs, step))
+    for rows, columns in NEAR[1:]:
+        theirs = (colour - 2 * rows - columns) % SIDE
+        theirs = lax.dynamic_index_in_dim(masked, theirs, 0, keepdims=False)
+        line.append(along("y" if rows else "x", theirs, -rows - columns))
+    line = jnp.stack(line)
     table = call(
         fourier_table,
         struct((2 * ORDERS, LON * PAD), BF16),
@@ -224,7 +226,7 @@
         n_in=4,
         vmem=16,
     )(*fourier_factors())
-    line = jnp.stack(line)
+    line, table = lax.optimization_barrier((line, table))
     lines = [line] + [same_colour(line, step) for step in HOPS[1:]]
     upright = call(
         turn_legendre,

time: 147 us -> 144 us (0.980)
  starting transfers between devices: 58.5 us -> 54.4 us
    all_to_all x1, starting transfers between devices: 8.62 us -> 4.85 us  [on_device(): by_sender = lax.all_to_all(returned, 'lon', 0, 0, tiled=True)]
    all_to_all x1, waiting for transfers between devices: 3.44 us -> 7.21 us  [on_device(): row_columns = lax.all_to_all(packed, 'lon', 0, 0, tiled=True)]
    ppermute x7, waiting for transfers between devices: 14.8 us -> 11.3 us  [along(): lax.ppermute(value, axis, [(i, (i + step) % SIDE) for i in range(SIDE)])]
    ppermute x7, starting transfers between devices: 23 us -> 21.4 us  [along(): lax.ppermute(value, axis, [(i, (i + step) % SIDE) for i in range(SIDE)])]
where the time goes in v4:
time: 144 us; the launch traced here: 143 us
  starting transfers between devices  54.4 us (38%)
  waiting for transfers between devices  39.6 us (28%)
  blocking collectives  23.6 us (16%)
  local copies, waits for them, and re-layouts  14.9 us (10%)
  Pallas kernels  8.15 us (6%)
  other arithmetic  2.16 us (2%)
    all_to_all x1, blocking collectives, on_device(): spectrum = lax.all_to_all(turned, ('y', 'x'), 0, 0, tiled=True)  23.6 us
    ppermute x7, starting transfers between devices, along(): lax.ppermute(value, axis, [(i, (i + step) % SIDE) for i in range(SIDE)])  21.4 us
    ppermute x3, waiting for transfers between devices, same_colour(): return lax.ppermute(value, ('y', 'x'), pairs)  20.1 us
    all_to_all x1, starting transfers between devices, on_device(): row_columns = lax.all_to_all(packed, 'lon', 0, 0, tiled=True)  15.5 us
    ppermute x3, starting transfers between devices, same_colour(): return lax.ppermute(value, ('y', 'x'), pairs)  12.7 us
    ppermute x7, waiting for transfers between devices, along(): lax.ppermute(value, axis, [(i, (i + step) % SIDE) for i in range(SIDE)])  11.3 us
    all_to_all x1, waiting for transfers between devices, on_device(): row_columns = lax.all_to_all(packed, 'lon', 0, 0, tiled=True)  7.21 us
    dynamic_update_slice x5, local copies, waits for them, and re-layouts, on_device(): out = lax.dynamic_update_slice(out, value, (start, at, 0, 0))  6.59 us
  transfers between devices with their start and end apart: 12, of which 9 were waited for; matrix products, arithmetic and copies ran while one was open for 7% of the time, Pallas kernels for 4%

profile of v4, /device:TPU:24, one launch (start us, length us, event | category | flops | bytes accessed | tf_op | source)
XLA Modules:
  0.0 143.3 jit_solution(17527413815316332882)
XLA Ops:
  0.0 1.0 copy-done.3
  1.1 1.2 shard_map.28
  2.2 15.5 %all-to-all-start = ((bf16[32,72,128]{2,1,0:T(8,128)(2,1)}), bf16[32,72,128]{2,1,0:T(8,128)(2,1)S(1)}, u32[]{:S(2)}, u32[]{:S(2)}) async-start(bf16[32,72,128]{2,1,0:T(8,128)(2,1)} %shard_map.28), calls=%async_computation | async-start | bytes 1179648 | tf_op jit(solution)/shard_map/all_to_all | solution.py:209
  17.8 0.0 copy-start.2
  17.8 1.2 copy-done.2
  18.9 0.3 shard_map.29
  19.2 0.1 constant_dynamic-slice_fusion
  19.3 2.1 %collective-permute-start = (bf16[16,48,128]{2,1,0:T(8,128)(2,1)S(1)}, bf16[16,48,128]{2,1,0:T(8,128)(2,1)S(1)}, u32[]{:S(2)}, u32[]{:S(2)}) collective-permute-start(bf16[16,48,128]{2,1,0:T(8,128)(2,1)S(1)} %get-tuple-element.18), channel_id=1, source_target_pairs={{0,128},{128,256},{256,384},{384,0},{1,129},{129,257},{257,385},{3... | collective-permute-start | bytes 589832 | tf_op jit(solution)/shard_map/ppermute | solution.py:190
  21.5 3.4 %collective-permute-start.1 = (bf16[16,48,128]{2,1,0:T(8,128)(2,1)S(1)}, bf16[16,48,128]{2,1,0:T(8,128)(2,1)S(1)}, u32[]{:S(2)}, u32[]{:S(2)}) collective-permute-start(bf16[16,48,128]{2,1,0:T(8,128)(2,1)S(1)} %get-tuple-element.17), channel_id=1, source_target_pairs={{0,32},{32,64},{64,96},{96,0},{1,33},{33,65},{65,97},{97,1},{2,34}... | collective-permute-start | bytes 589832 | tf_op jit(solution)/shard_map/ppermute | solution.py:190
  24.9 3.7 %collective-permute-start.2 = (bf16[16,48,128]{2,1,0:T(8,128)(2,1)S(1)}, bf16[16,48,128]{2,1,0:T(8,128)(2,1)S(1)}, u32[]{:S(2)}, u32[]{:S(2)}) collective-permute-start(bf16[16,48,128]{2,1,0:T(8,128)(2,1)S(1)} %get-tuple-element.16), channel_id=1, source_target_pairs={{0,96},{32,0},{64,32},{96,64},{1,97},{33,1},{65,33},{97,65},{2,98}... | collective-permute-start | bytes 589832 | tf_op jit(solution)/shard_map/ppermute | solution.py:190
  28.6 0.7 select_multiply_fusion
  29.2 0.5 fusion.9
  29.7 0.9 shard_map.30.table_ref
  30.6 0.8 collective-permute-done.1
  31.4 1.9 %collective-permute-done.2 = bf16[16,48,128]{2,1,0:T(8,128)(2,1)S(1)} collective-permute-done((bf16[16,48,128]{2,1,0:T(8,128)(2,1)S(1)}, bf16[16,48,128]{2,1,0:T(8,128)(2,1)S(1)}, u32[]{:S(2)}, u32[]{:S(2)}) %collective-permute-start.2) | collective-permute-done | bytes 196640 | tf_op jit(solution)/shard_map/ppermute | solution.py:190
  33.3 1.0 pad_maximum_fusion.refs_0_
  34.3 5.6 %collective-permute-start.3 = (bf16[4,16,48,128]{3,2,1,0:T(8,128)(2,1)}, bf16[4,16,48,128]{3,2,1,0:T(8,128)(2,1)}, u32[]{:S(2)}, u32[]{:S(2)}) collective-permute-start(bf16[4,16,48,128]{3,2,1,0:T(8,128)(2,1)} %pad_maximum_fusion.refs_0_), channel_id=1, source_target_pairs={{0,192},{32,224},{64,128},{96,160},{128,320},{160,352},{192,256},{... | collective-permute-start | bytes 2359304 | tf_op jit(solution)/shard_map/ppermute | solution.py:199
  39.9 2.7 %collective-permute-start.4 = (bf16[4,16,48,128]{3,2,1,0:T(8,128)(2,1)}, bf16[4,16,48,128]{3,2,1,0:T(8,128)(2,1)}, u32[]{:S(2)}, u32[]{:S(2)}) collective-permute-start(bf16[4,16,48,128]{3,2,1,0:T(8,128)(2,1)} %pad_maximum_fusion.refs_0_), channel_id=1, source_target_pairs={{0,448},{32,480},{64,384},{96,416},{128,64},{160,96},{192,0},{224,... | collective-permute-start | bytes 2359304 | tf_op jit(solution)/shard_map/ppermute | solution.py:199
  42.6 4.4 %collective-permute-start.5 = (bf16[4,16,48,128]{3,2,1,0:T(8,128)(2,1)}, bf16[4,16,48,128]{3,2,1,0:T(8,128)(2,1)}, u32[]{:S(2)}, u32[]{:S(2)}) collective-permute-start(bf16[4,16,48,128]{3,2,1,0:T(8,128)(2,1)} %pad_maximum_fusion.refs_0_), channel_id=1, source_target_pairs={{0,256},{32,288},{64,320},{96,352},{128,384},{160,416},{192,448},{... | collective-permute-start | bytes 2359304 | tf_op jit(solution)/shard_map/ppermute | solution.py:199
  47.0 7.2 %all-to-all-done.x_ref = bf16[32,72,128]{2,1,0:T(8,128)(2,1)S(1)} async-done(((bf16[32,72,128]{2,1,0:T(8,128)(2,1)}), bf16[32,72,128]{2,1,0:T(8,128)(2,1)S(1)}, u32[]{:S(2)}, u32[]{:S(2)}) %all-to-all-start) | async-done | bytes 589856 | tf_op jit(solution)/shard_map/all_to_all | solution.py:209
  54.2 1.7 %shard_map.31 = bf16[32,40,128]{2,1,0:T(8,128)(2,1)} custom-call(bf16[32,72,128]{2,1,0:T(8,128)(2,1)S(1)} %all-to-all-done.x_ref, bf16[768,1536]{1,0:T(8,128)(2,1)S(1)} %shard_map.30.table_ref), custom_call_target="tpu_custom_call" | custom-call | tf_op jit(solution)/shard_map/pallas_call | solution.py:239
  55.9 4.8 %all-to-all-start.1 = ((bf16[32,40,128]{2,1,0:T(8,128)(2,1)}), bf16[32,40,128]{2,1,0:T(8,128)(2,1)S(1)}, u32[]{:S(2)}, u32[]{:S(2)}) async-start(bf16[32,40,128]{2,1,0:T(8,128)(2,1)} %shard_map.31), calls=%async_computation.1 | async-start | bytes 655360 | tf_op jit(solution)/shard_map/all_to_all | solution.py:245
  60.8 0.0 collective-permute-done.3.refs_1_
  60.8 15.2 %collective-permute-done.4.refs_2_ = bf16[4,16,48,128]{3,2,1,0:T(8,128)(2,1)} collective-permute-done((bf16[4,16,48,128]{3,2,1,0:T(8,128)(2,1)}, bf16[4,16,48,128]{3,2,1,0:T(8,128)(2,1)}, u32[]{:S(2)}, u32[]{:S(2)}) %collective-permute-start.4) | collective-permute-done | bytes 786464 | tf_op jit(solution)/shard_map/ppermute | solution.py:199
  76.0 5.0 %collective-permute-done.5.refs_3_ = bf16[4,16,48,128]{3,2,1,0:T(8,128)(2,1)} collective-permute-done((bf16[4,16,48,128]{3,2,1,0:T(8,128)(2,1)}, bf16[4,16,48,128]{3,2,1,0:T(8,128)(2,1)}, u32[]{:S(2)}, u32[]{:S(2)}) %collective-permute-start.5) | collective-permute-done | bytes 786464 | tf_op jit(solution)/shard_map/ppermute | solution.py:199
  80.9 2.7 %shard_map.32.p_ref = bf16[3,672,768]{2,1,0:T(8,128)(2,1)S(1)} custom-call(bf16[4,16,48,128]{3,2,1,0:T(8,128)(2,1)} %pad_maximum_fusion.refs_0_, bf16[4,16,48,128]{3,2,1,0:T(8,128)(2,1)} %collective-permute-done.3.refs_1_, bf16[4,16,48,128]{3,2,1,0:T(8,128)(2,1)} %collective-permute-done.4.refs_2_, bf16[4,16,48,128]{3,2,1,0:T(8,128)(2,1)} %collective-permute-done.5.refs_3_), custom_call_target="tpu_custom_call" | custom-call | flops 99999997952 | bytes 1000000000 | tf_op jit(solution)/shard_map/pallas_call | solution.py:231
  83.7 0.0 copy-start
  83.7 1.6 %copy-done = bf16[3,672,768]{2,1,0:T(8,128)(2,1)} copy-done((bf16[3,672,768]{2,1,0:T(8,128)(2,1)}, bf16[3,672,768]{2,1,0:T(8,128)(2,1)S(1)}, u32[]{:S(2)}) %copy-start) | copy-done | bytes 3096600
  85.3 1.0 all-to-all-done.1.r_ref
  86.3 0.3 shard_map.33
  86.6 23.6 %all_to_all.15.s_ref = bf16[16,3,48,256]{3,2,1,0:T(8,128)(2,1)S(1)} all-to-all(bf16[16,3,48,256]{3,2,1,0:T(8,128)(2,1)S(1)} %shard_map.33), channel_id=1, replica_groups=mesh['y'=4,'x'=4,'lon'=32] {'y','x'}, dimensions={0} | all-to-all | bytes 2359296 | tf_op jit(solution)/shard_map/all_to_all | solution.py:252
  110.2 1.1 shard_map.34
  111.3 3.1 %collective-permute-start.8 = (bf16[4032,128]{1,0:T(8,128)(2,1)S(1)}, bf16[4032,128]{1,0:T(8,128)(2,1)S(1)}, u32[]{:S(2)}, u32[]{:S(2)}) collective-permute-start(bf16[4032,128]{1,0:T(8,128)(2,1)S(1)} %shard_map.34), channel_id=1, source_target_pairs={{0,96},{32,0},{64,32},{96,64},{1,97},{33,1},{65,33},{97,65},{2,98}... | collective-permute-start | bytes 3096584 | tf_op jit(solution)/shard_map/ppermute | solution.py:190
  114.4 2.7 %collective-permute-start.9 = (bf16[4032,128]{1,0:T(8,128)(2,1)S(1)}, bf16[4032,128]{1,0:T(8,128)(2,1)S(1)}, u32[]{:S(2)}, u32[]{:S(2)}) collective-permute-start(bf16[4032,128]{1,0:T(8,128)(2,1)S(1)} %shard_map.34), channel_id=1, source_target_pairs={{0,32},{32,64},{64,96},{96,0},{1,33},{33,65},{65,97},{97,1},{2,34}... | collective-permute-start | bytes 3096584 | tf_op jit(solution)/shard_map/ppermute | solution.py:190
  117.1 1.0 fusion.33
  118.2 4.3 %collective-permute-start.6 = (bf16[2016,128]{1,0:T(8,128)(2,1)}, bf16[2016,128]{1,0:T(8,128)(2,1)}, u32[]{:S(2)}, u32[]{:S(2)}) collective-permute-start(bf16[2016,128]{1,0:T(8,128)(2,1)} %get-tuple-element.14), channel_id=1, source_target_pairs={{0,128},{128,256},{256,384},{384,0},{1,129},{129,257},{257,385},{3... | collective-permute-start | bytes 1548296 | tf_op jit(solution)/shard_map/ppermute | solution.py:190
  122.5 2.1 %collective-permute-start.7 = (bf16[2016,128]{1,0:T(8,128)(2,1)}, bf16[2016,128]{1,0:T(8,128)(2,1)}, u32[]{:S(2)}, u32[]{:S(2)}) collective-permute-start(bf16[2016,128]{1,0:T(8,128)(2,1)} %get-tuple-element.13), channel_id=1, source_target_pairs={{0,384},{128,0},{256,128},{384,256},{1,385},{129,1},{257,129},{385... | collective-permute-start | bytes 1548296 | tf_op jit(solution)/shard_map/ppermute | solution.py:190
  124.6 2.1 %broadcast_in_dim.38 = bf16[672,12,2,128]{3,2,1,0:T(2,128)(2,1)S(1)} broadcast(bf16[]{:T(256)} %constant.119.clone.1), dimensions={} | broadcast | bytes 4128770 | tf_op jit(solution)/shard_map/broadcast_in_dim | solution.py:270
  126.8 0.9 constant_dynamic-update-slice_fusion.4
  127.7 4.4 %collective-permute-done.6 = bf16[2016,128]{1,0:T(8,128)(2,1)} collective-permute-done((bf16[2016,128]{1,0:T(8,128)(2,1)}, bf16[2016,128]{1,0:T(8,128)(2,1)}, u32[]{:S(2)}, u32[]{:S(2)}) %collective-permute-start.6) | collective-permute-done | bytes 516128 | tf_op jit(solution)/shard_map/ppermute | solution.py:190
  132.2 1.5 %constant_dynamic-update-slice_fusion.3 = bf16[672,12,2,128]{3,2,1,0:T(2,128)(2,1)S(1)} fusion(bf16[672,12,2,128]{3,2,1,0:T(2,128)(2,1)S(1)} %constant_dynamic-update-slice_fusion.4, bf16[336,3,2,128]{3,2,1,0:T(2,128)(2,1)} %bitcast.7, s32[]{:T(128)S(6)} %select_n.170), kind=kLoop, calls=%fused_computation.53 | loop fusion | bytes 1032196 | tf_op jit(solution)/shard_map/dynamic_update_slice | solution.py:274
  133.7 3.4 %collective-permute-done.7 = bf16[2016,128]{1,0:T(8,128)(2,1)} collective-permute-done((bf16[2016,128]{1,0:T(8,128)(2,1)}, bf16[2016,128]{1,0:T(8,128)(2,1)}, u32[]{:S(2)}, u32[]{:S(2)}) %collective-permute-start.7) | collective-permute-done | bytes 516128 | tf_op jit(solution)/shard_map/ppermute | solution.py:190
  137.1 1.5 %constant_dynamic-update-slice_fusion.2 = bf16[672,12,2,128]{3,2,1,0:T(2,128)(2,1)S(1)} fusion(bf16[672,12,2,128]{3,2,1,0:T(2,128)(2,1)S(1)} %constant_dynamic-update-slice_fusion.3, bf16[336,3,2,128]{3,2,1,0:T(2,128)(2,1)} %bitcast.8, s32[]{:T(128)S(6)} %select_n.170), kind=kLoop, calls=%fused_computation.52 | loop fusion | bytes 1032196 | tf_op jit(solution)/shard_map/dynamic_update_slice | solution.py:274
  138.6 0.9 constant_dynamic-update-slice_fusion.1
  139.6 0.0 copy-start.4
  139.6 0.8 collective-permute-done.9
  140.4 1.2 copy-done.4
  141.6 1.7 %constant_dynamic-update-slice_fusion = bf16[672,12,2,128]{3,2,1,0:T(2,128)(2,1)} fusion(bf16[672,12,2,128]{3,2,1,0:T(2,128)(2,1)} %copy-done.4, bf16[672,3,2,128]{3,2,1,0:T(2,128)(2,1)S(1)} %bitcast.15, s32[]{:T(128)S(6)} %select_n.173), kind=kLoop, calls=%fused_computation.50 | loop fusion | bytes 2064388 | tf_op jit(solution)/shard_map/dynamic_update_slice | solution.py:274
  (9 shorter events, 0.1 us)
Async XLA Ops:
  0.0 1.1 copy-start.3
  2.2 52.0 %all-to-all-start = ((bf16[32,72,128]{2,1,0:T(8,128)(2,1)}), bf16[32,72,128]{2,1,0:T(8,128)(2,1)S(1)}, u32[]{:S(2)}, u32[]{:S(2)}) async-start(bf16[32,72,128]{2,1,0:T(8,128)(2,1)} %shard_map.28), calls=%async_computation | async-start | bytes 1179648 | tf_op jit(solution)/shard_map/all_to_all | solution.py:209
  17.8 1.2 copy-start.2
  19.3 11.3 %collective-permute-start = (bf16[16,48,128]{2,1,0:T(8,128)(2,1)S(1)}, bf16[16,48,128]{2,1,0:T(8,128)(2,1)S(1)}, u32[]{:S(2)}, u32[]{:S(2)}) collective-permute-start(bf16[16,48,128]{2,1,0:T(8,128)(2,1)S(1)} %get-tuple-element.18), channel_id=1, source_target_pairs={{0,128},{128,256},{256,384},{384,0},{1,129},{129,257},{257,385},{3... | collective-permute-start | bytes 589832 | tf_op jit(solution)/shard_map/ppermute | solution.py:190
  21.5 10.0 %collective-permute-start.1 = (bf16[16,48,128]{2,1,0:T(8,128)(2,1)S(1)}, bf16[16,48,128]{2,1,0:T(8,128)(2,1)S(1)}, u32[]{:S(2)}, u32[]{:S(2)}) collective-permute-start(bf16[16,48,128]{2,1,0:T(8,128)(2,1)S(1)} %get-tuple-element.17), channel_id=1, source_target_pairs={{0,32},{32,64},{64,96},{96,0},{1,33},{33,65},{65,97},{97,1},{2,34}... | collective-permute-start | bytes 589832 | tf_op jit(solution)/shard_map/ppermute | solution.py:190
  24.9 8.5 %collective-permute-start.2 = (bf16[16,48,128]{2,1,0:T(8,128)(2,1)S(1)}, bf16[16,48,128]{2,1,0:T(8,128)(2,1)S(1)}, u32[]{:S(2)}, u32[]{:S(2)}) collective-permute-start(bf16[16,48,128]{2,1,0:T(8,128)(2,1)S(1)} %get-tuple-element.16), channel_id=1, source_target_pairs={{0,96},{32,0},{64,32},{96,64},{1,97},{33,1},{65,33},{97,65},{2,98}... | collective-permute-start | bytes 589832 | tf_op jit(solution)/shard_map/ppermute | solution.py:190
  34.3 26.5 %collective-permute-start.3 = (bf16[4,16,48,128]{3,2,1,0:T(8,128)(2,1)}, bf16[4,16,48,128]{3,2,1,0:T(8,128)(2,1)}, u32[]{:S(2)}, u32[]{:S(2)}) collective-permute-start(bf16[4,16,48,128]{3,2,1,0:T(8,128)(2,1)} %pad_maximum_fusion.refs_0_), channel_id=1, source_target_pairs={{0,192},{32,224},{64,128},{96,160},{128,320},{160,352},{192,256},{... | collective-permute-start | bytes 2359304 | tf_op jit(solution)/shard_map/ppermute | solution.py:199
  39.9 36.1 %collective-permute-start.4 = (bf16[4,16,48,128]{3,2,1,0:T(8,128)(2,1)}, bf16[4,16,48,128]{3,2,1,0:T(8,128)(2,1)}, u32[]{:S(2)}, u32[]{:S(2)}) collective-permute-start(bf16[4,16,48,128]{3,2,1,0:T(8,128)(2,1)} %pad_maximum_fusion.refs_0_), channel_id=1, source_target_pairs={{0,448},{32,480},{64,384},{96,416},{128,64},{160,96},{192,0},{224,... | collective-permute-start | bytes 2359304 | tf_op jit(solution)/shard_map/ppermute | solution.py:199
  42.6 38.4 %collective-permute-start.5 = (bf16[4,16,48,128]{3,2,1,0:T(8,128)(2,1)}, bf16[4,16,48,128]{3,2,1,0:T(8,128)(2,1)}, u32[]{:S(2)}, u32[]{:S(2)}) collective-permute-start(bf16[4,16,48,128]{3,2,1,0:T(8,128)(2,1)} %pad_maximum_fusion.refs_0_), channel_id=1, source_target_pairs={{0,256},{32,288},{64,320},{96,352},{128,384},{160,416},{192,448},{... | collective-permute-start | bytes 2359304 | tf_op jit(solution)/shard_map/ppermute | solution.py:199
  55.9 30.3 %all-to-all-start.1 = ((bf16[32,40,128]{2,1,0:T(8,128)(2,1)}), bf16[32,40,128]{2,1,0:T(8,128)(2,1)S(1)}, u32[]{:S(2)}, u32[]{:S(2)}) async-start(bf16[32,40,128]{2,1,0:T(8,128)(2,1)} %shard_map.31), calls=%async_computation.1 | async-start | bytes 655360 | tf_op jit(solution)/shard_map/all_to_all | solution.py:245
  83.7 1.7 %copy-start = (bf16[3,672,768]{2,1,0:T(8,128)(2,1)}, bf16[3,672,768]{2,1,0:T(8,128)(2,1)S(1)}, u32[]{:S(2)}) copy-start(bf16[3,672,768]{2,1,0:T(8,128)(2,1)S(1)} %shard_map.32.p_ref) | copy-start | bytes 9289732
  86.3 23.9 %copy-start.1 = (bf16[3,672,768]{2,1,0:T(8,128)(2,1)S(1)}, bf16[3,672,768]{2,1,0:T(8,128)(2,1)}, u32[]{:S(2)}) copy-start(bf16[3,672,768]{2,1,0:T(8,128)(2,1)} %copy-done) | copy-start | bytes 9289732
  111.3 27.4 %collective-permute-start.8 = (bf16[4032,128]{1,0:T(8,128)(2,1)S(1)}, bf16[4032,128]{1,0:T(8,128)(2,1)S(1)}, u32[]{:S(2)}, u32[]{:S(2)}) collective-permute-start(bf16[4032,128]{1,0:T(8,128)(2,1)S(1)} %shard_map.34), channel_id=1, source_target_pairs={{0,96},{32,0},{64,32},{96,64},{1,97},{33,1},{65,33},{97,65},{2,98}... | collective-permute-start | bytes 3096584 | tf_op jit(solution)/shard_map/ppermute | solution.py:190
  114.4 25.9 %collective-permute-start.9 = (bf16[4032,128]{1,0:T(8,128)(2,1)S(1)}, bf16[4032,128]{1,0:T(8,128)(2,1)S(1)}, u32[]{:S(2)}, u32[]{:S(2)}) collective-permute-start(bf16[4032,128]{1,0:T(8,128)(2,1)S(1)} %shard_map.34), channel_id=1, source_target_pairs={{0,32},{32,64},{64,96},{96,0},{1,33},{33,65},{65,97},{97,1},{2,34}... | collective-permute-start | bytes 3096584 | tf_op jit(solution)/shard_map/ppermute | solution.py:190
  118.2 14.0 %collective-permute-start.6 = (bf16[2016,128]{1,0:T(8,128)(2,1)}, bf16[2016,128]{1,0:T(8,128)(2,1)}, u32[]{:S(2)}, u32[]{:S(2)}) collective-permute-start(bf16[2016,128]{1,0:T(8,128)(2,1)} %get-tuple-element.14), channel_id=1, source_target_pairs={{0,128},{128,256},{256,384},{384,0},{1,129},{129,257},{257,385},{3... | collective-permute-start | bytes 1548296 | tf_op jit(solution)/shard_map/ppermute | solution.py:190
  122.5 14.7 %collective-permute-start.7 = (bf16[2016,128]{1,0:T(8,128)(2,1)}, bf16[2016,128]{1,0:T(8,128)(2,1)}, u32[]{:S(2)}, u32[]{:S(2)}) collective-permute-start(bf16[2016,128]{1,0:T(8,128)(2,1)} %get-tuple-element.13), channel_id=1, source_target_pairs={{0,384},{128,0},{256,128},{384,256},{1,385},{129,1},{257,129},{385... | collective-permute-start | bytes 1548296 | tf_op jit(solution)/shard_map/ppermute | solution.py:190
  139.6 2.0 %copy-start.4 = (bf16[672,12,2,128]{3,2,1,0:T(2,128)(2,1)}, bf16[672,12,2,128]{3,2,1,0:T(2,128)(2,1)S(1)}, u32[]{:S(2)}) copy-start(bf16[672,12,2,128]{3,2,1,0:T(2,128)(2,1)S(1)} %constant_dynamic-update-slice_fusion.1) | copy-start | bytes 12386308

commit v5 on v4

--- a/solution.py
+++ b/solution.py
@@ -18,10 +18,11 @@
 HELD = ORDERS // LON
 OWN = HELD // SIDE
 EXTRA = ROWS - LON
-SENT = PAD + PAD // 2
-BACK = 40
+HALF = (COLS + 1) // 2
+SENT = COLS + HALF
+BACK = 36
 F32, BF16 = jnp.float32, jnp.bfloat16
-HOPS = (0, 1, 3, 2)
+HOPS = (0, 3, 1, 2)
 NEAR = ((0, 0), (-1, 0), (0, -1), (0, 1))
 MIB = 1024 * 1024
 FULL = DEGREES // CH
@@ -49,47 +50,51 @@
     return lax.broadcasted_iota(jnp.int32, shape, len(shape) - 1) < CH // 2
 
 
-def pack_rows(grad_ref, out_ref, rows):
+def pack_rows(grad_ref, out_ref, rows, flat):
+    rows[...] = jnp.zeros_like(rows)
+    left = left_half((HALF, CH))
+    for d in range(2 * EXTRA, LON):
+        flat[d * SENT + COLS : (d + 1) * SENT, :] = jnp.zeros((HALF, CH), F32)
+    for row in range(ROWS):
+        if row < LON:
+            flat[row * SENT : row * SENT + COLS, :] = grad_ref[row].astype(F32)
+        else:
+            rows[0:COLS, :] = grad_ref[row].astype(F32)
+            early, late = rows[0:HALF, :], rows[HALF : 2 * HALF, :]
+            first = jnp.where(left, early, pltpu.roll(late, CH // 2, 1))
+            second = jnp.where(left, pltpu.roll(early, CH // 2, 1), late)
+            at = 2 * (row - LON) * SENT
+            flat[at + COLS : at + SENT, :] = first
+            flat[at + SENT + COLS : at + 2 * SENT, :] = second
+    out_ref[...] = flat[...].astype(BF16)
+
+
+def spectrum_rows(x_ref, table_ref, out_ref, both, flat, got, rows):
+    got[0 : LON * SENT, :] = x_ref[...].astype(F32)
+    got[LON * SENT :, :] = jnp.zeros_like(got[LON * SENT :, :])
     rows[...] = jnp.zeros_like(rows)
     half = PAD // 2
     left = left_half((half, CH))
     for d in range(LON):
-        rows[0:COLS, :] = grad_ref[d].astype(F32)
-        out_ref[d, 0:PAD, :] = rows[...].astype(BF16)
-    for extra in range(EXTRA):
-        rows[0:COLS, :] = grad_ref[LON + extra].astype(F32)
-        early, late = rows[0:half, :], rows[half:PAD, :]
-        first = jnp.where(left, early, pltpu.roll(late, CH // 2, 1))
-        second = jnp.where(left, pltpu.roll(early, CH // 2, 1), late)
-        out_ref[2 * extra, PAD:SENT, :] = first.astype(BF16)
-        out_ref[2 * extra + 1, PAD:SENT, :] = second.astype(BF16)
-    for d in range(2 * EXTRA, LON):
-        out_ref[d, PAD:SENT, :] = jnp.zeros((half, CH), BF16)
-
-
-def spectrum_rows(x_ref, table_ref, out_ref, both):
-    half = PAD // 2
-    left = left_half((half, CH))
-    for d in range(LON):
         at = d * PAD
-        both[at : at + PAD, 0:CH] = x_ref[d, 0:PAD, :]
-        packed = x_ref[d, PAD:SENT, :].astype(F32)
-        early = jnp.where(left, packed, 0.0)
-        late = jnp.where(left, pltpu.roll(packed, CH // 2, 1), 0.0)
-        both[at : at + PAD, CH : 2 * CH] = jnp.concatenate([early, late], 0).astype(BF16)
+        both[at : at + PAD, 0:CH] = got[d * SENT : d * SENT + PAD, :].astype(BF16)
+        packed = got[d * SENT + COLS : d * SENT + COLS + half, :]
+        rows[0:half, :] = jnp.where(left, packed, 0.0)
+        rows[HALF : HALF + half, :] = jnp.where(left, pltpu.roll(packed, CH // 2, 1), 0.0)
+        both[at : at + PAD, CH : 2 * CH] = rows[...].astype(BF16)
     n = 2 * HELD
     found = jnp.dot(table_ref[...], both[...], preferred_element_type=F32)
-    left8 = left_half((8, CH))
     for d in range(LON):
-        whole = found[d * n : (d + 1) * n, 0:CH]
+        at = d * BACK
+        flat[at : at + n, :] = found[d * n : (d + 1) * n, 0:CH]
         part = found[d * n : (d + 1) * n, CH : 2 * CH]
-        mixed = jnp.where(left8, part[0:8], pltpu.roll(part[16:24], CH // 2, 1))
-        out_ref[d] = jnp.concatenate([whole, mixed, part[8:16]], 0).astype(BF16)
+        high = pltpu.roll(part, CH // 2, 1)[HELD:n]
+        flat[at + n : at + BACK, :] = jnp.where(left_half((HELD, CH)), part[0:HELD], high)
+    out_ref[...] = flat[...].astype(BF16)
 
 
 def turn_rows(r_ref, out_ref, flat):
-    for d in range(LON):
-        flat[d * BACK : (d + 1) * BACK, :] = r_ref[d].astype(F32)
+    flat[...] = r_ref[...].astype(F32)
     n = 2 * HELD
     left = left_half((16, CH))
     for order in range(HELD):
@@ -98,10 +103,10 @@
             i = part * HELD + order
             lanes = slice(part * CH, (part + 1) * CH)
             main = flat[pl.ds(i, LON, stride=BACK), :]
-            at = n + (i if i < 16 else i - 16)
+            at = n + i % HELD
             even = flat[pl.ds(at, 16, stride=2 * BACK), :]
             odd = flat[pl.ds(BACK + at, 16, stride=2 * BACK), :]
-            if i < 16:
+            if part == 0:
                 rest = jnp.where(left, even, pltpu.roll(odd, CH // 2, 1))
             else:
                 rest = jnp.where(left, pltpu.roll(even, CH // 2, 1), odd)
@@ -204,9 +209,12 @@
     struct = jax.ShapeDtypeStruct
 
     packed = call(
-        pack_rows, struct((LON, SENT, CH), BF16), [pltpu.VMEM((PAD, CH), F32)]
+        pack_rows,
+        struct((LON * SENT, CH), BF16),
+        [pltpu.VMEM((PAD, CH), F32), pltpu.VMEM((LON * SENT, CH), F32)],
     )(grad_field)
-    row_columns = lax.all_to_all(packed, "lon", 0, 0, tiled=True)
+    packed = packed.reshape(LON, SENT // 2, 2, CH)
+    row_columns = lax.all_to_all(packed, "lon", 0, 0, tiled=True).reshape(LON * SENT, CH)
 
     masked = call(
         pack_legendre,
@@ -238,11 +246,17 @@
 
     returned = call(
         spectrum_rows,
-        struct((LON, BACK, CH), BF16),
-        [pltpu.VMEM((LON * PAD, 2 * CH), BF16)],
+        struct((LON * BACK, CH), BF16),
+        [
+            pltpu.VMEM((LON * PAD, 2 * CH), BF16),
+            pltpu.VMEM((LON * BACK, CH), F32),
+            pltpu.VMEM((LON * SENT + 8, CH), F32),
+            pltpu.VMEM((PAD, CH), F32),
+        ],
         n_in=2,
     )(row_columns, table)
-    by_sender = lax.all_to_all(returned, "lon", 0, 0, tiled=True)
+    returned = returned.reshape(LON, BACK // 2, 2, CH)
+    by_sender = lax.all_to_all(returned, "lon", 0, 0, tiled=True).reshape(LON * BACK, CH)
     by_sender, upright = lax.optimization_barrier((by_sender, upright))
     turned = call(
         turn_rows,

time: 144 us -> 142 us (0.986)
  waiting for transfers between devices: 39.6 us -> 35.4 us
    ppermute x3, waiting for transfers between devices: 20.1 us -> 14.4 us  [same_colour(): return lax.ppermute(value, ('y', 'x'), pairs)]
    all_to_all x2, waiting for transfers between devices: 8.16 us -> 11.2 us  [the longest x1 5.83 us: on_device(): lax.all_to_all(packed, 'lon', 0, 0, tiled=True).reshape(LON * SENT, CH)]
    ppermute x7, waiting for transfers between devices: 11.3 us -> 9.8 us  [along(): lax.ppermute(value, axis, [(i, (i + step) % SIDE) for i in range(SIDE)])]
where the time goes in v5:
time: 142 us; the launch traced here: 141 us
  starting transfers between devices  55.7 us (39%)
  waiting for transfers between devices  35.4 us (25%)
  blocking collectives  23.6 us (17%)
  local copies, waits for them, and re-layouts  15.4 us (11%)
  Pallas kernels  8.11 us (6%)
  other arithmetic  2.16 us (2%)
    all_to_all x1, blocking collectives, on_device(): spectrum = lax.all_to_all(turned, ('y', 'x'), 0, 0, tiled=True)  23.6 us
    ppermute x7, starting transfers between devices, along(): lax.ppermute(value, axis, [(i, (i + step) % SIDE) for i in range(SIDE)])  21.3 us
    all_to_all x1, starting transfers between devices, on_device(): lax.all_to_all(packed, 'lon', 0, 0, tiled=True).reshape(LON * SENT, CH)  15.5 us
    ppermute x3, waiting for transfers between devices, same_colour(): return lax.ppermute(value, ('y', 'x'), pairs)  14.4 us
    ppermute x3, starting transfers between devices, same_colour(): return lax.ppermute(value, ('y', 'x'), pairs)  12.7 us
    ppermute x7, waiting for transfers between devices, along(): lax.ppermute(value, axis, [(i, (i + step) % SIDE) for i in range(SIDE)])  9.8 us
    dynamic_update_slice x5, local copies, waits for them, and re-layouts, on_device(): out = lax.dynamic_update_slice(out, value, (start, at, 0, 0))  6.59 us
    all_to_all x1, starting transfers between devices, on_device(): lax.all_to_all(returned, 'lon', 0, 0, tiled=True).reshape(LON * BACK, CH)  6.23 us
  transfers between devices with their start and end apart: 12, of which 9 were waited for; matrix products, arithmetic and copies ran while one was open for 7% of the time, Pallas kernels for 4%

profile of v5, /device:TPU:24, one launch (start us, length us, event | category | flops | bytes accessed | tf_op | source)
XLA Modules:
  0.0 140.8 jit_solution(7099480628597906694)
XLA Ops:
  0.0 1.0 copy-done.3
  1.1 1.0 shard_map.28
  2.1 15.5 %all-to-all-start = ((bf16[32,34,2,128]{3,2,1,0:T(2,128)(2,1)}), bf16[32,34,2,128]{3,2,1,0:T(2,128)(2,1)S(1)}, u32[]{:S(2)}, u32[]{:S(2)}) async-start(bf16[32,34,2,128]{3,2,1,0:T(2,128)(2,1)} %bitcast), calls=%async_computation | async-start | bytes 1114112 | tf_op jit(solution)/shard_map/all_to_all | solution.py:217
  17.6 0.0 copy-start.2
  17.7 1.2 copy-done.2
  18.8 0.3 shard_map.29
  19.1 0.1 constant_dynamic-slice_fusion
  19.2 2.1 %collective-permute-start = (bf16[16,48,128]{2,1,0:T(8,128)(2,1)S(1)}, bf16[16,48,128]{2,1,0:T(8,128)(2,1)S(1)}, u32[]{:S(2)}, u32[]{:S(2)}) collective-permute-start(bf16[16,48,128]{2,1,0:T(8,128)(2,1)S(1)} %get-tuple-element.18), channel_id=1, source_target_pairs={{0,128},{128,256},{256,384},{384,0},{1,129},{129,257},{257,385},{3... | collective-permute-start | bytes 589832 | tf_op jit(solution)/shard_map/ppermute | solution.py:195
  21.3 3.4 %collective-permute-start.1 = (bf16[16,48,128]{2,1,0:T(8,128)(2,1)S(1)}, bf16[16,48,128]{2,1,0:T(8,128)(2,1)S(1)}, u32[]{:S(2)}, u32[]{:S(2)}) collective-permute-start(bf16[16,48,128]{2,1,0:T(8,128)(2,1)S(1)} %get-tuple-element.17), channel_id=1, source_target_pairs={{0,32},{32,64},{64,96},{96,0},{1,33},{33,65},{65,97},{97,1},{2,34}... | collective-permute-start | bytes 589832 | tf_op jit(solution)/shard_map/ppermute | solution.py:195
  24.7 3.7 %collective-permute-start.2 = (bf16[16,48,128]{2,1,0:T(8,128)(2,1)S(1)}, bf16[16,48,128]{2,1,0:T(8,128)(2,1)S(1)}, u32[]{:S(2)}, u32[]{:S(2)}) collective-permute-start(bf16[16,48,128]{2,1,0:T(8,128)(2,1)S(1)} %get-tuple-element.16), channel_id=1, source_target_pairs={{0,96},{32,0},{64,32},{96,64},{1,97},{33,1},{65,33},{97,65},{2,98}... | collective-permute-start | bytes 589832 | tf_op jit(solution)/shard_map/ppermute | solution.py:195
  28.5 0.7 select_multiply_fusion
  29.1 0.5 fusion.9
  29.6 0.9 shard_map.30.table_ref
  30.5 0.8 collective-permute-done.1
  31.3 1.9 %collective-permute-done.2 = bf16[16,48,128]{2,1,0:T(8,128)(2,1)S(1)} collective-permute-done((bf16[16,48,128]{2,1,0:T(8,128)(2,1)S(1)}, bf16[16,48,128]{2,1,0:T(8,128)(2,1)S(1)}, u32[]{:S(2)}, u32[]{:S(2)}) %collective-permute-start.2) | collective-permute-done | bytes 196640 | tf_op jit(solution)/shard_map/ppermute | solution.py:195
  33.2 1.0 pad_maximum_fusion.refs_0_
  34.2 5.8 %collective-permute-start.3 = (bf16[4,16,48,128]{3,2,1,0:T(8,128)(2,1)}, bf16[4,16,48,128]{3,2,1,0:T(8,128)(2,1)}, u32[]{:S(2)}, u32[]{:S(2)}) collective-permute-start(bf16[4,16,48,128]{3,2,1,0:T(8,128)(2,1)} %pad_maximum_fusion.refs_0_), channel_id=1, source_target_pairs={{0,448},{32,480},{64,384},{96,416},{128,64},{160,96},{192,0},{224,... | collective-permute-start | bytes 2359304 | tf_op jit(solution)/shard_map/ppermute | solution.py:204
  40.0 3.6 %collective-permute-start.4 = (bf16[4,16,48,128]{3,2,1,0:T(8,128)(2,1)}, bf16[4,16,48,128]{3,2,1,0:T(8,128)(2,1)}, u32[]{:S(2)}, u32[]{:S(2)}) collective-permute-start(bf16[4,16,48,128]{3,2,1,0:T(8,128)(2,1)} %pad_maximum_fusion.refs_0_), channel_id=1, source_target_pairs={{0,192},{32,224},{64,128},{96,160},{128,320},{160,352},{192,256},{... | collective-permute-start | bytes 2359304 | tf_op jit(solution)/shard_map/ppermute | solution.py:204
  43.7 3.2 %collective-permute-start.5 = (bf16[4,16,48,128]{3,2,1,0:T(8,128)(2,1)}, bf16[4,16,48,128]{3,2,1,0:T(8,128)(2,1)}, u32[]{:S(2)}, u32[]{:S(2)}) collective-permute-start(bf16[4,16,48,128]{3,2,1,0:T(8,128)(2,1)} %pad_maximum_fusion.refs_0_), channel_id=1, source_target_pairs={{0,256},{32,288},{64,320},{96,352},{128,384},{160,416},{192,448},{... | collective-permute-start | bytes 2359304 | tf_op jit(solution)/shard_map/ppermute | solution.py:204
  46.9 5.8 %all-to-all-done = bf16[32,34,2,128]{3,2,1,0:T(2,128)(2,1)S(1)} async-done(((bf16[32,34,2,128]{3,2,1,0:T(2,128)(2,1)}), bf16[32,34,2,128]{3,2,1,0:T(2,128)(2,1)S(1)}, u32[]{:S(2)}, u32[]{:S(2)}) %all-to-all-start) | async-done | bytes 557088 | tf_op jit(solution)/shard_map/all_to_all | solution.py:217
  52.7 1.9 %shard_map.31 = bf16[1152,128]{1,0:T(8,128)(2,1)} custom-call(bf16[2176,128]{1,0:T(8,128)(2,1)S(1)} %bitcast.19, bf16[768,1536]{1,0:T(8,128)(2,1)S(1)} %shard_map.30.table_ref), custom_call_target="tpu_custom_call" | custom-call | tf_op jit(solution)/shard_map/pallas_call | solution.py:247
  54.6 6.2 %all-to-all-start.1 = ((bf16[32,18,2,128]{3,2,1,0:T(2,128)(2,1)}), bf16[32,18,2,128]{3,2,1,0:T(2,128)(2,1)S(1)}, u32[]{:S(2)}, u32[]{:S(2)}) async-start(bf16[32,18,2,128]{3,2,1,0:T(2,128)(2,1)} %bitcast.8), calls=%async_computation.1 | async-start | bytes 589824 | tf_op jit(solution)/shard_map/all_to_all | solution.py:259
  60.8 0.0 collective-permute-done.3.refs_1_
  60.8 13.7 %collective-permute-done.4.refs_2_ = bf16[4,16,48,128]{3,2,1,0:T(8,128)(2,1)} collective-permute-done((bf16[4,16,48,128]{3,2,1,0:T(8,128)(2,1)}, bf16[4,16,48,128]{3,2,1,0:T(8,128)(2,1)}, u32[]{:S(2)}, u32[]{:S(2)}) %collective-permute-start.4) | collective-permute-done | bytes 786464 | tf_op jit(solution)/shard_map/ppermute | solution.py:204
  74.5 0.7 collective-permute-done.5.refs_3_
  75.2 2.7 %shard_map.32.p_ref = bf16[3,672,768]{2,1,0:T(8,128)(2,1)S(1)} custom-call(bf16[4,16,48,128]{3,2,1,0:T(8,128)(2,1)} %pad_maximum_fusion.refs_0_, bf16[4,16,48,128]{3,2,1,0:T(8,128)(2,1)} %collective-permute-done.3.refs_1_, bf16[4,16,48,128]{3,2,1,0:T(8,128)(2,1)} %collective-permute-done.4.refs_2_, bf16[4,16,48,128]{3,2,1,0:T(8,128)(2,1)} %collective-permute-done.5.refs_3_), custom_call_target="tpu_custom_call" | custom-call | flops 99999997952 | bytes 1000000000 | tf_op jit(solution)/shard_map/pallas_call | solution.py:239
  77.9 0.0 copy-start
  77.9 1.6 %copy-done = bf16[3,672,768]{2,1,0:T(8,128)(2,1)} copy-done((bf16[3,672,768]{2,1,0:T(8,128)(2,1)}, bf16[3,672,768]{2,1,0:T(8,128)(2,1)S(1)}, u32[]{:S(2)}) %copy-start) | copy-done | bytes 3096600
  79.6 5.4 %all-to-all-done.1 = bf16[32,18,2,128]{3,2,1,0:T(2,128)(2,1)S(1)} async-done(((bf16[32,18,2,128]{3,2,1,0:T(2,128)(2,1)}), bf16[32,18,2,128]{3,2,1,0:T(2,128)(2,1)S(1)}, u32[]{:S(2)}, u32[]{:S(2)}) %all-to-all-start.1) | async-done | bytes 294944 | tf_op jit(solution)/shard_map/all_to_all | solution.py:259
  85.0 0.3 shard_map.33
  85.2 23.6 %all_to_all.15.s_ref = bf16[16,3,48,256]{3,2,1,0:T(8,128)(2,1)S(1)} all-to-all(bf16[16,3,48,256]{3,2,1,0:T(8,128)(2,1)S(1)} %shard_map.33), channel_id=1, replica_groups=mesh['y'=4,'x'=4,'lon'=32] {'y','x'}, dimensions={0} | all-to-all | bytes 2359296 | tf_op jit(solution)/shard_map/all_to_all | solution.py:266
  108.9 1.1 shard_map.34
  109.9 2.9 %collective-permute-start.8 = (bf16[4032,128]{1,0:T(8,128)(2,1)S(1)}, bf16[4032,128]{1,0:T(8,128)(2,1)S(1)}, u32[]{:S(2)}, u32[]{:S(2)}) collective-permute-start(bf16[4032,128]{1,0:T(8,128)(2,1)S(1)} %shard_map.34), channel_id=1, source_target_pairs={{0,96},{32,0},{64,32},{96,64},{1,97},{33,1},{65,33},{97,65},{2,98}... | collective-permute-start | bytes 3096584 | tf_op jit(solution)/shard_map/ppermute | solution.py:195
  112.9 2.9 %collective-permute-start.9 = (bf16[4032,128]{1,0:T(8,128)(2,1)S(1)}, bf16[4032,128]{1,0:T(8,128)(2,1)S(1)}, u32[]{:S(2)}, u32[]{:S(2)}) collective-permute-start(bf16[4032,128]{1,0:T(8,128)(2,1)S(1)} %shard_map.34), channel_id=1, source_target_pairs={{0,32},{32,64},{64,96},{96,0},{1,33},{33,65},{65,97},{97,1},{2,34}... | collective-permute-start | bytes 3096584 | tf_op jit(solution)/shard_map/ppermute | solution.py:195
  115.8 1.0 fusion.33
  116.8 4.2 %collective-permute-start.6 = (bf16[2016,128]{1,0:T(8,128)(2,1)}, bf16[2016,128]{1,0:T(8,128)(2,1)}, u32[]{:S(2)}, u32[]{:S(2)}) collective-permute-start(bf16[2016,128]{1,0:T(8,128)(2,1)} %get-tuple-element.14), channel_id=1, source_target_pairs={{0,128},{128,256},{256,384},{384,0},{1,129},{129,257},{257,385},{3... | collective-permute-start | bytes 1548296 | tf_op jit(solution)/shard_map/ppermute | solution.py:195
  121.0 2.1 %collective-permute-start.7 = (bf16[2016,128]{1,0:T(8,128)(2,1)}, bf16[2016,128]{1,0:T(8,128)(2,1)}, u32[]{:S(2)}, u32[]{:S(2)}) collective-permute-start(bf16[2016,128]{1,0:T(8,128)(2,1)} %get-tuple-element.13), channel_id=1, source_target_pairs={{0,384},{128,0},{256,128},{384,256},{1,385},{129,1},{257,129},{385... | collective-permute-start | bytes 1548296 | tf_op jit(solution)/shard_map/ppermute | solution.py:195
  123.2 2.1 %broadcast_in_dim.38 = bf16[672,12,2,128]{3,2,1,0:T(2,128)(2,1)S(1)} broadcast(bf16[]{:T(256)} %constant.119.clone.1), dimensions={} | broadcast | bytes 4128770 | tf_op jit(solution)/shard_map/broadcast_in_dim | solution.py:284
  125.3 0.9 constant_dynamic-update-slice_fusion.4
  126.3 3.1 %collective-permute-done.6 = bf16[2016,128]{1,0:T(8,128)(2,1)} collective-permute-done((bf16[2016,128]{1,0:T(8,128)(2,1)}, bf16[2016,128]{1,0:T(8,128)(2,1)}, u32[]{:S(2)}, u32[]{:S(2)}) %collective-permute-start.6) | collective-permute-done | bytes 516128 | tf_op jit(solution)/shard_map/ppermute | solution.py:195
  129.4 1.5 %constant_dynamic-update-slice_fusion.3 = bf16[672,12,2,128]{3,2,1,0:T(2,128)(2,1)S(1)} fusion(bf16[672,12,2,128]{3,2,1,0:T(2,128)(2,1)S(1)} %constant_dynamic-update-slice_fusion.4, bf16[336,3,2,128]{3,2,1,0:T(2,128)(2,1)} %bitcast.11, s32[]{:T(128)S(6)} %select_n.170), kind=kLoop, calls=%fused_computation.53 | loop fusion | bytes 1032196 | tf_op jit(solution)/shard_map/dynamic_update_slice | solution.py:288
  130.9 3.7 %collective-permute-done.7 = bf16[2016,128]{1,0:T(8,128)(2,1)} collective-permute-done((bf16[2016,128]{1,0:T(8,128)(2,1)}, bf16[2016,128]{1,0:T(8,128)(2,1)}, u32[]{:S(2)}, u32[]{:S(2)}) %collective-permute-start.7) | collective-permute-done | bytes 516128 | tf_op jit(solution)/shard_map/ppermute | solution.py:195
  134.7 1.5 %constant_dynamic-update-slice_fusion.2 = bf16[672,12,2,128]{3,2,1,0:T(2,128)(2,1)S(1)} fusion(bf16[672,12,2,128]{3,2,1,0:T(2,128)(2,1)S(1)} %constant_dynamic-update-slice_fusion.3, bf16[336,3,2,128]{3,2,1,0:T(2,128)(2,1)} %bitcast.12, s32[]{:T(128)S(6)} %select_n.170), kind=kLoop, calls=%fused_computation.52 | loop fusion | bytes 1032196 | tf_op jit(solution)/shard_map/dynamic_update_slice | solution.py:288
  136.2 0.9 constant_dynamic-update-slice_fusion.1
  137.2 0.0 copy-start.4
  137.2 0.2 collective-permute-done.9
  137.4 1.7 %copy-done.4 = bf16[672,12,2,128]{3,2,1,0:T(2,128)(2,1)} copy-done((bf16[672,12,2,128]{3,2,1,0:T(2,128)(2,1)}, bf16[672,12,2,128]{3,2,1,0:T(2,128)(2,1)S(1)}, u32[]{:S(2)}) %copy-start.4) | copy-done | bytes 4128792
  139.1 1.7 %constant_dynamic-update-slice_fusion = bf16[672,12,2,128]{3,2,1,0:T(2,128)(2,1)} fusion(bf16[672,12,2,128]{3,2,1,0:T(2,128)(2,1)} %copy-done.4, bf16[672,3,2,128]{3,2,1,0:T(2,128)(2,1)S(1)} %bitcast.21, s32[]{:T(128)S(6)} %select_n.173), kind=kLoop, calls=%fused_computation.50 | loop fusion | bytes 2064388 | tf_op jit(solution)/shard_map/dynamic_update_slice | solution.py:288
  (9 shorter events, 0.1 us)
Async XLA Ops:
  0.0 1.1 copy-start.3
  2.1 50.6 %all-to-all-start = ((bf16[32,34,2,128]{3,2,1,0:T(2,128)(2,1)}), bf16[32,34,2,128]{3,2,1,0:T(2,128)(2,1)S(1)}, u32[]{:S(2)}, u32[]{:S(2)}) async-start(bf16[32,34,2,128]{3,2,1,0:T(2,128)(2,1)} %bitcast), calls=%async_computation | async-start | bytes 1114112 | tf_op jit(solution)/shard_map/all_to_all | solution.py:217
  17.6 1.2 copy-start.2
  19.2 11.3 %collective-permute-start = (bf16[16,48,128]{2,1,0:T(8,128)(2,1)S(1)}, bf16[16,48,128]{2,1,0:T(8,128)(2,1)S(1)}, u32[]{:S(2)}, u32[]{:S(2)}) collective-permute-start(bf16[16,48,128]{2,1,0:T(8,128)(2,1)S(1)} %get-tuple-element.18), channel_id=1, source_target_pairs={{0,128},{128,256},{256,384},{384,0},{1,129},{129,257},{257,385},{3... | collective-permute-start | bytes 589832 | tf_op jit(solution)/shard_map/ppermute | solution.py:195
  21.3 10.0 %collective-permute-start.1 = (bf16[16,48,128]{2,1,0:T(8,128)(2,1)S(1)}, bf16[16,48,128]{2,1,0:T(8,128)(2,1)S(1)}, u32[]{:S(2)}, u32[]{:S(2)}) collective-permute-start(bf16[16,48,128]{2,1,0:T(8,128)(2,1)S(1)} %get-tuple-element.17), channel_id=1, source_target_pairs={{0,32},{32,64},{64,96},{96,0},{1,33},{33,65},{65,97},{97,1},{2,34}... | collective-permute-start | bytes 589832 | tf_op jit(solution)/shard_map/ppermute | solution.py:195
  24.7 8.5 %collective-permute-start.2 = (bf16[16,48,128]{2,1,0:T(8,128)(2,1)S(1)}, bf16[16,48,128]{2,1,0:T(8,128)(2,1)S(1)}, u32[]{:S(2)}, u32[]{:S(2)}) collective-permute-start(bf16[16,48,128]{2,1,0:T(8,128)(2,1)S(1)} %get-tuple-element.16), channel_id=1, source_target_pairs={{0,96},{32,0},{64,32},{96,64},{1,97},{33,1},{65,33},{97,65},{2,98}... | collective-permute-start | bytes 589832 | tf_op jit(solution)/shard_map/ppermute | solution.py:195
  34.2 26.7 %collective-permute-start.3 = (bf16[4,16,48,128]{3,2,1,0:T(8,128)(2,1)}, bf16[4,16,48,128]{3,2,1,0:T(8,128)(2,1)}, u32[]{:S(2)}, u32[]{:S(2)}) collective-permute-start(bf16[4,16,48,128]{3,2,1,0:T(8,128)(2,1)} %pad_maximum_fusion.refs_0_), channel_id=1, source_target_pairs={{0,448},{32,480},{64,384},{96,416},{128,64},{160,96},{192,0},{224,... | collective-permute-start | bytes 2359304 | tf_op jit(solution)/shard_map/ppermute | solution.py:204
  40.0 34.5 %collective-permute-start.4 = (bf16[4,16,48,128]{3,2,1,0:T(8,128)(2,1)}, bf16[4,16,48,128]{3,2,1,0:T(8,128)(2,1)}, u32[]{:S(2)}, u32[]{:S(2)}) collective-permute-start(bf16[4,16,48,128]{3,2,1,0:T(8,128)(2,1)} %pad_maximum_fusion.refs_0_), channel_id=1, source_target_pairs={{0,192},{32,224},{64,128},{96,160},{128,320},{160,352},{192,256},{... | collective-permute-start | bytes 2359304 | tf_op jit(solution)/shard_map/ppermute | solution.py:204
  43.7 31.6 %collective-permute-start.5 = (bf16[4,16,48,128]{3,2,1,0:T(8,128)(2,1)}, bf16[4,16,48,128]{3,2,1,0:T(8,128)(2,1)}, u32[]{:S(2)}, u32[]{:S(2)}) collective-permute-start(bf16[4,16,48,128]{3,2,1,0:T(8,128)(2,1)} %pad_maximum_fusion.refs_0_), channel_id=1, source_target_pairs={{0,256},{32,288},{64,320},{96,352},{128,384},{160,416},{192,448},{... | collective-permute-start | bytes 2359304 | tf_op jit(solution)/shard_map/ppermute | solution.py:204
  54.6 30.4 %all-to-all-start.1 = ((bf16[32,18,2,128]{3,2,1,0:T(2,128)(2,1)}), bf16[32,18,2,128]{3,2,1,0:T(2,128)(2,1)S(1)}, u32[]{:S(2)}, u32[]{:S(2)}) async-start(bf16[32,18,2,128]{3,2,1,0:T(2,128)(2,1)} %bitcast.8), calls=%async_computation.1 | async-start | bytes 589824 | tf_op jit(solution)/shard_map/all_to_all | solution.py:259
  77.9 1.7 %copy-start = (bf16[3,672,768]{2,1,0:T(8,128)(2,1)}, bf16[3,672,768]{2,1,0:T(8,128)(2,1)S(1)}, u32[]{:S(2)}) copy-start(bf16[3,672,768]{2,1,0:T(8,128)(2,1)S(1)} %shard_map.32.p_ref) | copy-start | bytes 9289732
  85.0 23.9 %copy-start.1 = (bf16[3,672,768]{2,1,0:T(8,128)(2,1)S(1)}, bf16[3,672,768]{2,1,0:T(8,128)(2,1)}, u32[]{:S(2)}) copy-start(bf16[3,672,768]{2,1,0:T(8,128)(2,1)} %copy-done) | copy-start | bytes 9289732
  109.9 26.2 %collective-permute-start.8 = (bf16[4032,128]{1,0:T(8,128)(2,1)S(1)}, bf16[4032,128]{1,0:T(8,128)(2,1)S(1)}, u32[]{:S(2)}, u32[]{:S(2)}) collective-permute-start(bf16[4032,128]{1,0:T(8,128)(2,1)S(1)} %shard_map.34), channel_id=1, source_target_pairs={{0,96},{32,0},{64,32},{96,64},{1,97},{33,1},{65,33},{97,65},{2,98}... | collective-permute-start | bytes 3096584 | tf_op jit(solution)/shard_map/ppermute | solution.py:195
  112.9 24.6 %collective-permute-start.9 = (bf16[4032,128]{1,0:T(8,128)(2,1)S(1)}, bf16[4032,128]{1,0:T(8,128)(2,1)S(1)}, u32[]{:S(2)}, u32[]{:S(2)}) collective-permute-start(bf16[4032,128]{1,0:T(8,128)(2,1)S(1)} %shard_map.34), channel_id=1, source_target_pairs={{0,32},{32,64},{64,96},{96,0},{1,33},{33,65},{65,97},{97,1},{2,34}... | collective-permute-start | bytes 3096584 | tf_op jit(solution)/shard_map/ppermute | solution.py:195
  116.8 12.6 %collective-permute-start.6 = (bf16[2016,128]{1,0:T(8,128)(2,1)}, bf16[2016,128]{1,0:T(8,128)(2,1)}, u32[]{:S(2)}, u32[]{:S(2)}) collective-permute-start(bf16[2016,128]{1,0:T(8,128)(2,1)} %get-tuple-element.14), channel_id=1, source_target_pairs={{0,128},{128,256},{256,384},{384,0},{1,129},{129,257},{257,385},{3... | collective-permute-start | bytes 1548296 | tf_op jit(solution)/shard_map/ppermute | solution.py:195
  121.0 13.6 %collective-permute-start.7 = (bf16[2016,128]{1,0:T(8,128)(2,1)}, bf16[2016,128]{1,0:T(8,128)(2,1)}, u32[]{:S(2)}, u32[]{:S(2)}) collective-permute-start(bf16[2016,128]{1,0:T(8,128)(2,1)} %get-tuple-element.13), channel_id=1, source_target_pairs={{0,384},{128,0},{256,128},{384,256},{1,385},{129,1},{257,129},{385... | collective-permute-start | bytes 1548296 | tf_op jit(solution)/shard_map/ppermute | solution.py:195
  137.2 2.0 %copy-start.4 = (bf16[672,12,2,128]{3,2,1,0:T(2,128)(2,1)}, bf16[672,12,2,128]{3,2,1,0:T(2,128)(2,1)S(1)}, u32[]{:S(2)}) copy-start(bf16[672,12,2,128]{3,2,1,0:T(2,128)(2,1)S(1)} %constant_dynamic-update-slice_fusion.1) | copy-start | bytes 12386308

commit v6 on v5

--- a/solution.py
+++ b/solution.py
@@ -20,6 +20,7 @@
 EXTRA = ROWS - LON
 HALF = (COLS + 1) // 2
 SENT = COLS + HALF
+LEAD = 40
 BACK = 36
 F32, BF16 = jnp.float32, jnp.bfloat16
 HOPS = (0, 3, 1, 2)
@@ -70,15 +71,15 @@
 
 
 def spectrum_rows(x_ref, table_ref, out_ref, both, flat, got, rows):
-    got[0 : LON * SENT, :] = x_ref[...].astype(F32)
-    got[LON * SENT :, :] = jnp.zeros_like(got[LON * SENT :, :])
+    got[...] = jnp.zeros_like(got)
     rows[...] = jnp.zeros_like(rows)
     half = PAD // 2
     left = left_half((half, CH))
     for d in range(LON):
         at = d * PAD
-        both[at : at + PAD, 0:CH] = got[d * SENT : d * SENT + PAD, :].astype(BF16)
-        packed = got[d * SENT + COLS : d * SENT + COLS + half, :]
+        both[at : at + PAD, 0:CH] = x_ref[d * SENT : d * SENT + PAD, :]
+        got[0 : SENT - LEAD, :] = x_ref[d * SENT + LEAD : (d + 1) * SENT, :].astype(F32)
+        packed = got[COLS - LEAD : COLS - LEAD + half, :]
         rows[0:half, :] = jnp.where(left, packed, 0.0)
         rows[HALF : HALF + half, :] = jnp.where(left, pltpu.roll(packed, CH // 2, 1), 0.0)
         both[at : at + PAD, CH : 2 * CH] = rows[...].astype(BF16)
@@ -250,7 +251,7 @@
         [
             pltpu.VMEM((LON * PAD, 2 * CH), BF16),
             pltpu.VMEM((LON * BACK, CH), F32),
-            pltpu.VMEM((LON * SENT + 8, CH), F32),
+            pltpu.VMEM((PAD, CH), F32),
             pltpu.VMEM((PAD, CH), F32),
         ],
         n_in=2,

time: 142 us -> 142 us (level)
  no operation moved by 1% of the time
where the time goes in v6:
time: 142 us; the launch traced here: 141 us
  starting transfers between devices  55.7 us (39%)
  waiting for transfers between devices  35.4 us (25%)
  blocking collectives  23.7 us (17%)
  local copies, waits for them, and re-layouts  15.4 us (11%)
  Pallas kernels  8.12 us (6%)
  other arithmetic  2.16 us (2%)
    all_to_all x1, blocking collectives, on_device(): spectrum = lax.all_to_all(turned, ('y', 'x'), 0, 0, tiled=True)  23.7 us
    ppermute x7, starting transfers between devices, along(): lax.ppermute(value, axis, [(i, (i + step) % SIDE) for i in range(SIDE)])  21.3 us
    all_to_all x1, starting transfers between devices, on_device(): lax.all_to_all(packed, 'lon', 0, 0, tiled=True).reshape(LON * SENT, CH)  15.5 us
    ppermute x3, waiting for transfers between devices, same_colour(): return lax.ppermute(value, ('y', 'x'), pairs)  14.4 us
    ppermute x3, starting transfers between devices, same_colour(): return lax.ppermute(value, ('y', 'x'), pairs)  12.7 us
    ppermute x7, waiting for transfers between devices, along(): lax.ppermute(value, axis, [(i, (i + step) % SIDE) for i in range(SIDE)])  9.8 us
    dynamic_update_slice x5, local copies, waits for them, and re-layouts, on_device(): out = lax.dynamic_update_slice(out, value, (start, at, 0, 0))  6.59 us
    all_to_all x1, starting transfers between devices, on_device(): lax.all_to_all(returned, 'lon', 0, 0, tiled=True).reshape(LON * BACK, CH)  6.23 us
  transfers between devices with their start and end apart: 12, of which 9 were waited for; matrix products, arithmetic and copies ran while one was open for 7% of the time, Pallas kernels for 4%

profile of v6, /device:TPU:24, one launch (start us, length us, event | category | flops | bytes accessed | tf_op | source)
XLA Modules:
  0.0 140.8 jit_solution(78966937411361301)
XLA Ops:
  0.0 1.0 copy-done.3
  1.1 1.0 shard_map.28
  2.1 15.5 %all-to-all-start = ((bf16[32,34,2,128]{3,2,1,0:T(2,128)(2,1)}), bf16[32,34,2,128]{3,2,1,0:T(2,128)(2,1)S(1)}, u32[]{:S(2)}, u32[]{:S(2)}) async-start(bf16[32,34,2,128]{3,2,1,0:T(2,128)(2,1)} %bitcast), calls=%async_computation | async-start | bytes 1114112 | tf_op jit(solution)/shard_map/all_to_all | solution.py:218
  17.6 0.0 copy-start.2
  17.7 1.2 copy-done.2
  18.8 0.3 shard_map.29
  19.1 0.1 constant_dynamic-slice_fusion
  19.2 2.1 %collective-permute-start = (bf16[16,48,128]{2,1,0:T(8,128)(2,1)S(1)}, bf16[16,48,128]{2,1,0:T(8,128)(2,1)S(1)}, u32[]{:S(2)}, u32[]{:S(2)}) collective-permute-start(bf16[16,48,128]{2,1,0:T(8,128)(2,1)S(1)} %get-tuple-element.18), channel_id=1, source_target_pairs={{0,128},{128,256},{256,384},{384,0},{1,129},{129,257},{257,385},{3... | collective-permute-start | bytes 589832 | tf_op jit(solution)/shard_map/ppermute | solution.py:196
  21.3 3.4 %collective-permute-start.1 = (bf16[16,48,128]{2,1,0:T(8,128)(2,1)S(1)}, bf16[16,48,128]{2,1,0:T(8,128)(2,1)S(1)}, u32[]{:S(2)}, u32[]{:S(2)}) collective-permute-start(bf16[16,48,128]{2,1,0:T(8,128)(2,1)S(1)} %get-tuple-element.17), channel_id=1, source_target_pairs={{0,32},{32,64},{64,96},{96,0},{1,33},{33,65},{65,97},{97,1},{2,34}... | collective-permute-start | bytes 589832 | tf_op jit(solution)/shard_map/ppermute | solution.py:196
  24.7 3.7 %collective-permute-start.2 = (bf16[16,48,128]{2,1,0:T(8,128)(2,1)S(1)}, bf16[16,48,128]{2,1,0:T(8,128)(2,1)S(1)}, u32[]{:S(2)}, u32[]{:S(2)}) collective-permute-start(bf16[16,48,128]{2,1,0:T(8,128)(2,1)S(1)} %get-tuple-element.16), channel_id=1, source_target_pairs={{0,96},{32,0},{64,32},{96,64},{1,97},{33,1},{65,33},{97,65},{2,98}... | collective-permute-start | bytes 589832 | tf_op jit(solution)/shard_map/ppermute | solution.py:196
  28.5 0.7 select_multiply_fusion
  29.1 0.5 fusion.9
  29.6 0.9 shard_map.30.table_ref
  30.5 0.8 collective-permute-done.1
  31.3 1.9 %collective-permute-done.2 = bf16[16,48,128]{2,1,0:T(8,128)(2,1)S(1)} collective-permute-done((bf16[16,48,128]{2,1,0:T(8,128)(2,1)S(1)}, bf16[16,48,128]{2,1,0:T(8,128)(2,1)S(1)}, u32[]{:S(2)}, u32[]{:S(2)}) %collective-permute-start.2) | collective-permute-done | bytes 196640 | tf_op jit(solution)/shard_map/ppermute | solution.py:196
  33.2 1.0 pad_maximum_fusion.refs_0_
  34.2 5.8 %collective-permute-start.3 = (bf16[4,16,48,128]{3,2,1,0:T(8,128)(2,1)}, bf16[4,16,48,128]{3,2,1,0:T(8,128)(2,1)}, u32[]{:S(2)}, u32[]{:S(2)}) collective-permute-start(bf16[4,16,48,128]{3,2,1,0:T(8,128)(2,1)} %pad_maximum_fusion.refs_0_), channel_id=1, source_target_pairs={{0,448},{32,480},{64,384},{96,416},{128,64},{160,96},{192,0},{224,... | collective-permute-start | bytes 2359304 | tf_op jit(solution)/shard_map/ppermute | solution.py:205
  40.0 3.6 %collective-permute-start.4 = (bf16[4,16,48,128]{3,2,1,0:T(8,128)(2,1)}, bf16[4,16,48,128]{3,2,1,0:T(8,128)(2,1)}, u32[]{:S(2)}, u32[]{:S(2)}) collective-permute-start(bf16[4,16,48,128]{3,2,1,0:T(8,128)(2,1)} %pad_maximum_fusion.refs_0_), channel_id=1, source_target_pairs={{0,192},{32,224},{64,128},{96,160},{128,320},{160,352},{192,256},{... | collective-permute-start | bytes 2359304 | tf_op jit(solution)/shard_map/ppermute | solution.py:205
  43.7 3.2 %collective-permute-start.5 = (bf16[4,16,48,128]{3,2,1,0:T(8,128)(2,1)}, bf16[4,16,48,128]{3,2,1,0:T(8,128)(2,1)}, u32[]{:S(2)}, u32[]{:S(2)}) collective-permute-start(bf16[4,16,48,128]{3,2,1,0:T(8,128)(2,1)} %pad_maximum_fusion.refs_0_), channel_id=1, source_target_pairs={{0,256},{32,288},{64,320},{96,352},{128,384},{160,416},{192,448},{... | collective-permute-start | bytes 2359304 | tf_op jit(solution)/shard_map/ppermute | solution.py:205
  46.9 5.8 %all-to-all-done = bf16[32,34,2,128]{3,2,1,0:T(2,128)(2,1)S(1)} async-done(((bf16[32,34,2,128]{3,2,1,0:T(2,128)(2,1)}), bf16[32,34,2,128]{3,2,1,0:T(2,128)(2,1)S(1)}, u32[]{:S(2)}, u32[]{:S(2)}) %all-to-all-start) | async-done | bytes 557088 | tf_op jit(solution)/shard_map/all_to_all | solution.py:218
  52.7 1.9 %shard_map.31 = bf16[1152,128]{1,0:T(8,128)(2,1)} custom-call(bf16[2176,128]{1,0:T(8,128)(2,1)S(1)} %bitcast.19, bf16[768,1536]{1,0:T(8,128)(2,1)S(1)} %shard_map.30.table_ref), custom_call_target="tpu_custom_call" | custom-call | tf_op jit(solution)/shard_map/pallas_call | solution.py:248
  54.6 6.2 %all-to-all-start.1 = ((bf16[32,18,2,128]{3,2,1,0:T(2,128)(2,1)}), bf16[32,18,2,128]{3,2,1,0:T(2,128)(2,1)S(1)}, u32[]{:S(2)}, u32[]{:S(2)}) async-start(bf16[32,18,2,128]{3,2,1,0:T(2,128)(2,1)} %bitcast.8), calls=%async_computation.1 | async-start | bytes 589824 | tf_op jit(solution)/shard_map/all_to_all | solution.py:260
  60.8 0.0 collective-permute-done.3.refs_1_
  60.8 13.7 %collective-permute-done.4.refs_2_ = bf16[4,16,48,128]{3,2,1,0:T(8,128)(2,1)} collective-permute-done((bf16[4,16,48,128]{3,2,1,0:T(8,128)(2,1)}, bf16[4,16,48,128]{3,2,1,0:T(8,128)(2,1)}, u32[]{:S(2)}, u32[]{:S(2)}) %collective-permute-start.4) | collective-permute-done | bytes 786464 | tf_op jit(solution)/shard_map/ppermute | solution.py:205
  74.5 0.7 collective-permute-done.5.refs_3_
  75.2 2.7 %shard_map.32.p_ref = bf16[3,672,768]{2,1,0:T(8,128)(2,1)S(1)} custom-call(bf16[4,16,48,128]{3,2,1,0:T(8,128)(2,1)} %pad_maximum_fusion.refs_0_, bf16[4,16,48,128]{3,2,1,0:T(8,128)(2,1)} %collective-permute-done.3.refs_1_, bf16[4,16,48,128]{3,2,1,0:T(8,128)(2,1)} %collective-permute-done.4.refs_2_, bf16[4,16,48,128]{3,2,1,0:T(8,128)(2,1)} %collective-permute-done.5.refs_3_), custom_call_target="tpu_custom_call" | custom-call | flops 99999997952 | bytes 1000000000 | tf_op jit(solution)/shard_map/pallas_call | solution.py:240
  77.9 0.0 copy-start
  77.9 1.6 %copy-done = bf16[3,672,768]{2,1,0:T(8,128)(2,1)} copy-done((bf16[3,672,768]{2,1,0:T(8,128)(2,1)}, bf16[3,672,768]{2,1,0:T(8,128)(2,1)S(1)}, u32[]{:S(2)}) %copy-start) | copy-done | bytes 3096600
  79.6 5.4 %all-to-all-done.1 = bf16[32,18,2,128]{3,2,1,0:T(2,128)(2,1)S(1)} async-done(((bf16[32,18,2,128]{3,2,1,0:T(2,128)(2,1)}), bf16[32,18,2,128]{3,2,1,0:T(2,128)(2,1)S(1)}, u32[]{:S(2)}, u32[]{:S(2)}) %all-to-all-start.1) | async-done | bytes 294944 | tf_op jit(solution)/shard_map/all_to_all | solution.py:260
  85.0 0.3 shard_map.33
  85.2 23.7 %all_to_all.15.s_ref = bf16[16,3,48,256]{3,2,1,0:T(8,128)(2,1)S(1)} all-to-all(bf16[16,3,48,256]{3,2,1,0:T(8,128)(2,1)S(1)} %shard_map.33), channel_id=1, replica_groups=mesh['y'=4,'x'=4,'lon'=32] {'y','x'}, dimensions={0} | all-to-all | bytes 2359296 | tf_op jit(solution)/shard_map/all_to_all | solution.py:267
  108.9 1.1 shard_map.34
  110.0 2.9 %collective-permute-start.8 = (bf16[4032,128]{1,0:T(8,128)(2,1)S(1)}, bf16[4032,128]{1,0:T(8,128)(2,1)S(1)}, u32[]{:S(2)}, u32[]{:S(2)}) collective-permute-start(bf16[4032,128]{1,0:T(8,128)(2,1)S(1)} %shard_map.34), channel_id=1, source_target_pairs={{0,96},{32,0},{64,32},{96,64},{1,97},{33,1},{65,33},{97,65},{2,98}... | collective-permute-start | bytes 3096584 | tf_op jit(solution)/shard_map/ppermute | solution.py:196
  112.9 3.0 %collective-permute-start.9 = (bf16[4032,128]{1,0:T(8,128)(2,1)S(1)}, bf16[4032,128]{1,0:T(8,128)(2,1)S(1)}, u32[]{:S(2)}, u32[]{:S(2)}) collective-permute-start(bf16[4032,128]{1,0:T(8,128)(2,1)S(1)} %shard_map.34), channel_id=1, source_target_pairs={{0,32},{32,64},{64,96},{96,0},{1,33},{33,65},{65,97},{97,1},{2,34}... | collective-permute-start | bytes 3096584 | tf_op jit(solution)/shard_map/ppermute | solution.py:196
  115.8 1.0 fusion.33
  116.9 4.2 %collective-permute-start.6 = (bf16[2016,128]{1,0:T(8,128)(2,1)}, bf16[2016,128]{1,0:T(8,128)(2,1)}, u32[]{:S(2)}, u32[]{:S(2)}) collective-permute-start(bf16[2016,128]{1,0:T(8,128)(2,1)} %get-tuple-element.14), channel_id=1, source_target_pairs={{0,128},{128,256},{256,384},{384,0},{1,129},{129,257},{257,385},{3... | collective-permute-start | bytes 1548296 | tf_op jit(solution)/shard_map/ppermute | solution.py:196
  121.1 2.1 %collective-permute-start.7 = (bf16[2016,128]{1,0:T(8,128)(2,1)}, bf16[2016,128]{1,0:T(8,128)(2,1)}, u32[]{:S(2)}, u32[]{:S(2)}) collective-permute-start(bf16[2016,128]{1,0:T(8,128)(2,1)} %get-tuple-element.13), channel_id=1, source_target_pairs={{0,384},{128,0},{256,128},{384,256},{1,385},{129,1},{257,129},{385... | collective-permute-start | bytes 1548296 | tf_op jit(solution)/shard_map/ppermute | solution.py:196
  123.2 2.1 %broadcast_in_dim.38 = bf16[672,12,2,128]{3,2,1,0:T(2,128)(2,1)S(1)} broadcast(bf16[]{:T(256)} %constant.119.clone.1), dimensions={} | broadcast | bytes 4128770 | tf_op jit(solution)/shard_map/broadcast_in_dim | solution.py:285
  125.4 0.9 constant_dynamic-update-slice_fusion.4
  126.3 3.1 %collective-permute-done.6 = bf16[2016,128]{1,0:T(8,128)(2,1)} collective-permute-done((bf16[2016,128]{1,0:T(8,128)(2,1)}, bf16[2016,128]{1,0:T(8,128)(2,1)}, u32[]{:S(2)}, u32[]{:S(2)}) %collective-permute-start.6) | collective-permute-done | bytes 516128 | tf_op jit(solution)/shard_map/ppermute | solution.py:196
  129.4 1.5 %constant_dynamic-update-slice_fusion.3 = bf16[672,12,2,128]{3,2,1,0:T(2,128)(2,1)S(1)} fusion(bf16[672,12,2,128]{3,2,1,0:T(2,128)(2,1)S(1)} %constant_dynamic-update-slice_fusion.4, bf16[336,3,2,128]{3,2,1,0:T(2,128)(2,1)} %bitcast.11, s32[]{:T(128)S(6)} %select_n.170), kind=kLoop, calls=%fused_computation.53 | loop fusion | bytes 1032196 | tf_op jit(solution)/shard_map/dynamic_update_slice | solution.py:289
  131.0 3.7 %collective-permute-done.7 = bf16[2016,128]{1,0:T(8,128)(2,1)} collective-permute-done((bf16[2016,128]{1,0:T(8,128)(2,1)}, bf16[2016,128]{1,0:T(8,128)(2,1)}, u32[]{:S(2)}, u32[]{:S(2)}) %collective-permute-start.7) | collective-permute-done | bytes 516128 | tf_op jit(solution)/shard_map/ppermute | solution.py:196
  134.7 1.5 %constant_dynamic-update-slice_fusion.2 = bf16[672,12,2,128]{3,2,1,0:T(2,128)(2,1)S(1)} fusion(bf16[672,12,2,128]{3,2,1,0:T(2,128)(2,1)S(1)} %constant_dynamic-update-slice_fusion.3, bf16[336,3,2,128]{3,2,1,0:T(2,128)(2,1)} %bitcast.12, s32[]{:T(128)S(6)} %select_n.170), kind=kLoop, calls=%fused_computation.52 | loop fusion | bytes 1032196 | tf_op jit(solution)/shard_map/dynamic_update_slice | solution.py:289
  136.2 0.9 constant_dynamic-update-slice_fusion.1
  137.2 0.0 copy-start.4
  137.2 0.2 collective-permute-done.9
  137.4 1.7 %copy-done.4 = bf16[672,12,2,128]{3,2,1,0:T(2,128)(2,1)} copy-done((bf16[672,12,2,128]{3,2,1,0:T(2,128)(2,1)}, bf16[672,12,2,128]{3,2,1,0:T(2,128)(2,1)S(1)}, u32[]{:S(2)}) %copy-start.4) | copy-done | bytes 4128792
  139.2 1.7 %constant_dynamic-update-slice_fusion = bf16[672,12,2,128]{3,2,1,0:T(2,128)(2,1)} fusion(bf16[672,12,2,128]{3,2,1,0:T(2,128)(2,1)} %copy-done.4, bf16[672,3,2,128]{3,2,1,0:T(2,128)(2,1)S(1)} %bitcast.21, s32[]{:T(128)S(6)} %select_n.173), kind=kLoop, calls=%fused_computation.50 | loop fusion | bytes 2064388 | tf_op jit(solution)/shard_map/dynamic_update_slice | solution.py:289
  (9 shorter events, 0.1 us)
Async XLA Ops:
  0.0 1.1 copy-start.3
  2.1 50.6 %all-to-all-start = ((bf16[32,34,2,128]{3,2,1,0:T(2,128)(2,1)}), bf16[32,34,2,128]{3,2,1,0:T(2,128)(2,1)S(1)}, u32[]{:S(2)}, u32[]{:S(2)}) async-start(bf16[32,34,2,128]{3,2,1,0:T(2,128)(2,1)} %bitcast), calls=%async_computation | async-start | bytes 1114112 | tf_op jit(solution)/shard_map/all_to_all | solution.py:218
  17.6 1.2 copy-start.2
  19.2 11.3 %collective-permute-start = (bf16[16,48,128]{2,1,0:T(8,128)(2,1)S(1)}, bf16[16,48,128]{2,1,0:T(8,128)(2,1)S(1)}, u32[]{:S(2)}, u32[]{:S(2)}) collective-permute-start(bf16[16,48,128]{2,1,0:T(8,128)(2,1)S(1)} %get-tuple-element.18), channel_id=1, source_target_pairs={{0,128},{128,256},{256,384},{384,0},{1,129},{129,257},{257,385},{3... | collective-permute-start | bytes 589832 | tf_op jit(solution)/shard_map/ppermute | solution.py:196
  21.3 10.0 %collective-permute-start.1 = (bf16[16,48,128]{2,1,0:T(8,128)(2,1)S(1)}, bf16[16,48,128]{2,1,0:T(8,128)(2,1)S(1)}, u32[]{:S(2)}, u32[]{:S(2)}) collective-permute-start(bf16[16,48,128]{2,1,0:T(8,128)(2,1)S(1)} %get-tuple-element.17), channel_id=1, source_target_pairs={{0,32},{32,64},{64,96},{96,0},{1,33},{33,65},{65,97},{97,1},{2,34}... | collective-permute-start | bytes 589832 | tf_op jit(solution)/shard_map/ppermute | solution.py:196
  24.7 8.5 %collective-permute-start.2 = (bf16[16,48,128]{2,1,0:T(8,128)(2,1)S(1)}, bf16[16,48,128]{2,1,0:T(8,128)(2,1)S(1)}, u32[]{:S(2)}, u32[]{:S(2)}) collective-permute-start(bf16[16,48,128]{2,1,0:T(8,128)(2,1)S(1)} %get-tuple-element.16), channel_id=1, source_target_pairs={{0,96},{32,0},{64,32},{96,64},{1,97},{33,1},{65,33},{97,65},{2,98}... | collective-permute-start | bytes 589832 | tf_op jit(solution)/shard_map/ppermute | solution.py:196
  34.2 26.7 %collective-permute-start.3 = (bf16[4,16,48,128]{3,2,1,0:T(8,128)(2,1)}, bf16[4,16,48,128]{3,2,1,0:T(8,128)(2,1)}, u32[]{:S(2)}, u32[]{:S(2)}) collective-permute-start(bf16[4,16,48,128]{3,2,1,0:T(8,128)(2,1)} %pad_maximum_fusion.refs_0_), channel_id=1, source_target_pairs={{0,448},{32,480},{64,384},{96,416},{128,64},{160,96},{192,0},{224,... | collective-permute-start | bytes 2359304 | tf_op jit(solution)/shard_map/ppermute | solution.py:205
  40.0 34.5 %collective-permute-start.4 = (bf16[4,16,48,128]{3,2,1,0:T(8,128)(2,1)}, bf16[4,16,48,128]{3,2,1,0:T(8,128)(2,1)}, u32[]{:S(2)}, u32[]{:S(2)}) collective-permute-start(bf16[4,16,48,128]{3,2,1,0:T(8,128)(2,1)} %pad_maximum_fusion.refs_0_), channel_id=1, source_target_pairs={{0,192},{32,224},{64,128},{96,160},{128,320},{160,352},{192,256},{... | collective-permute-start | bytes 2359304 | tf_op jit(solution)/shard_map/ppermute | solution.py:205
  43.7 31.6 %collective-permute-start.5 = (bf16[4,16,48,128]{3,2,1,0:T(8,128)(2,1)}, bf16[4,16,48,128]{3,2,1,0:T(8,128)(2,1)}, u32[]{:S(2)}, u32[]{:S(2)}) collective-permute-start(bf16[4,16,48,128]{3,2,1,0:T(8,128)(2,1)} %pad_maximum_fusion.refs_0_), channel_id=1, source_target_pairs={{0,256},{32,288},{64,320},{96,352},{128,384},{160,416},{192,448},{... | collective-permute-start | bytes 2359304 | tf_op jit(solution)/shard_map/ppermute | solution.py:205
  54.6 30.4 %all-to-all-start.1 = ((bf16[32,18,2,128]{3,2,1,0:T(2,128)(2,1)}), bf16[32,18,2,128]{3,2,1,0:T(2,128)(2,1)S(1)}, u32[]{:S(2)}, u32[]{:S(2)}) async-start(bf16[32,18,2,128]{3,2,1,0:T(2,128)(2,1)} %bitcast.8), calls=%async_computation.1 | async-start | bytes 589824 | tf_op jit(solution)/shard_map/all_to_all | solution.py:260
  77.9 1.7 %copy-start = (bf16[3,672,768]{2,1,0:T(8,128)(2,1)}, bf16[3,672,768]{2,1,0:T(8,128)(2,1)S(1)}, u32[]{:S(2)}) copy-start(bf16[3,672,768]{2,1,0:T(8,128)(2,1)S(1)} %shard_map.32.p_ref) | copy-start | bytes 9289732
  85.0 23.9 %copy-start.1 = (bf16[3,672,768]{2,1,0:T(8,128)(2,1)S(1)}, bf16[3,672,768]{2,1,0:T(8,128)(2,1)}, u32[]{:S(2)}) copy-start(bf16[3,672,768]{2,1,0:T(8,128)(2,1)} %copy-done) | copy-start | bytes 9289732
  110.0 26.2 %collective-permute-start.8 = (bf16[4032,128]{1,0:T(8,128)(2,1)S(1)}, bf16[4032,128]{1,0:T(8,128)(2,1)S(1)}, u32[]{:S(2)}, u32[]{:S(2)}) collective-permute-start(bf16[4032,128]{1,0:T(8,128)(2,1)S(1)} %shard_map.34), channel_id=1, source_target_pairs={{0,96},{32,0},{64,32},{96,64},{1,97},{33,1},{65,33},{97,65},{2,98}... | collective-permute-start | bytes 3096584 | tf_op jit(solution)/shard_map/ppermute | solution.py:196
  112.9 24.6 %collective-permute-start.9 = (bf16[4032,128]{1,0:T(8,128)(2,1)S(1)}, bf16[4032,128]{1,0:T(8,128)(2,1)S(1)}, u32[]{:S(2)}, u32[]{:S(2)}) collective-permute-start(bf16[4032,128]{1,0:T(8,128)(2,1)S(1)} %shard_map.34), channel_id=1, source_target_pairs={{0,32},{32,64},{64,96},{96,0},{1,33},{33,65},{65,97},{97,1},{2,34}... | collective-permute-start | bytes 3096584 | tf_op jit(solution)/shard_map/ppermute | solution.py:196
  116.9 12.6 %collective-permute-start.6 = (bf16[2016,128]{1,0:T(8,128)(2,1)}, bf16[2016,128]{1,0:T(8,128)(2,1)}, u32[]{:S(2)}, u32[]{:S(2)}) collective-permute-start(bf16[2016,128]{1,0:T(8,128)(2,1)} %get-tuple-element.14), channel_id=1, source_target_pairs={{0,128},{128,256},{256,384},{384,0},{1,129},{129,257},{257,385},{3... | collective-permute-start | bytes 1548296 | tf_op jit(solution)/shard_map/ppermute | solution.py:196
  121.1 13.6 %collective-permute-start.7 = (bf16[2016,128]{1,0:T(8,128)(2,1)}, bf16[2016,128]{1,0:T(8,128)(2,1)}, u32[]{:S(2)}, u32[]{:S(2)}) collective-permute-start(bf16[2016,128]{1,0:T(8,128)(2,1)} %get-tuple-element.13), channel_id=1, source_target_pairs={{0,384},{128,0},{256,128},{384,256},{1,385},{129,1},{257,129},{385... | collective-permute-start | bytes 1548296 | tf_op jit(solution)/shard_map/ppermute | solution.py:196
  137.2 2.0 %copy-start.4 = (bf16[672,12,2,128]{3,2,1,0:T(2,128)(2,1)}, bf16[672,12,2,128]{3,2,1,0:T(2,128)(2,1)S(1)}, u32[]{:S(2)}) copy-start(bf16[672,12,2,128]{3,2,1,0:T(2,128)(2,1)S(1)} %constant_dynamic-update-slice_fusion.1) | copy-start | bytes 12386308

commit v7 on v6

--- a/solution.py
+++ b/solution.py
@@ -136,20 +136,28 @@
 
 
 def turn_legendre(*refs):
-    *parts, out_ref, tall = refs
-    for tile in range(TILES):
+    *parts, out_ref, turned, tall, done = refs
+    copies = [
+        pltpu.make_async_copy(turned.at[place], out_ref.at[place], done.at[place])
+        for place in range(OWN)
+    ]
+    for tile in [TILES - 1] + list(range(TILES - 1)):
         for hop, part in enumerate(parts):
             for shift in range(SIDE):
                 at = (hop * SIDE + shift) * PAD
                 tall[at : at + PAD, :] = part[shift, tile].astype(F32)
-        turned = tall[...].T.astype(BF16)
+        found = tall[...].T.astype(BF16)
         if tile == TILES - 1:
             for place in range(OWN):
                 rows = slice(place * TAIL, (place + 1) * TAIL)
-                out_ref[place, FULL * CH : DEGREES, :] = turned[rows]
+                turned[place, FULL * CH : DEGREES, :] = found[rows]
         else:
             place, at = tile // FULL, tile % FULL * CH
-            out_ref[place, at : at + CH, :] = turned
+            turned[place, at : at + CH, :] = found
+            if tile % FULL == FULL - 1:
+                copies[place].start()
+    for copy in copies:
+        copy.wait()
 
 
 def legendre_sum(s_ref, p_ref, out_ref, gathered, spread):
@@ -237,12 +245,19 @@
     )(*fourier_factors())
     line, table = lax.optimization_barrier((line, table))
     lines = [line] + [same_colour(line, step) for step in HOPS[1:]]
-    upright = call(
+    whole = pl.BlockSpec(memory_space=pltpu.VMEM)
+    upright = pl.pallas_call(
         turn_legendre,
-        struct((OWN, DEGREES, LAT * PAD), BF16),
-        [pltpu.VMEM((LAT * PAD, CH), F32)],
-        n_in=SIDE,
-        cost=LONG,
+        out_shape=struct((OWN, DEGREES, LAT * PAD), BF16),
+        in_specs=[whole] * SIDE,
+        out_specs=pl.BlockSpec(memory_space=pltpu.HBM),
+        scratch_shapes=[
+            pltpu.VMEM((OWN, DEGREES, LAT * PAD), BF16),
+            pltpu.VMEM((LAT * PAD, CH), F32),
+            pltpu.SemaphoreType.DMA((OWN,)),
+        ],
+        cost_estimate=LONG,
+        compiler_params=pltpu.CompilerParams(vmem_limit_bytes=12 * MIB),
     )(*lines)
 
     returned = call(

time: 142 us -> 140 us (0.986)
  waiting for transfers between devices: 35.4 us -> 33.1 us
  transfers between devices with their start and end apart: 12 -> 12, of which waited for: 9 -> 9; matrix products, arithmetic and copies ran while one was open for 7% -> 7% of each run, Pallas kernels for 4% -> 5%
where the time goes in v7:
time: 140 us
  starting transfers between devices  55.8 us (40%)
  waiting for transfers between devices  33.1 us (24%)
  blocking collectives  23.4 us (17%)
  local copies, waits for them, and re-layouts  15.3 us (11%)
  Pallas kernels  9.45 us (7%)
  other arithmetic  2.16 us (2%)
    all_to_all x1, blocking collectives, on_device(): spectrum = lax.all_to_all(turned, ('y', 'x'), 0, 0, tiled=True)  23.4 us
    ppermute x7, starting transfers between devices, along(): lax.ppermute(value, axis, [(i, (i + step) % SIDE) for i in range(SIDE)])  21.4 us
    all_to_all x1, starting transfers between devices, on_device(): lax.all_to_all(packed, 'lon', 0, 0, tiled=True).reshape(LON * SENT, CH)  15.5 us
    ppermute x3, waiting for transfers between devices, same_colour(): return lax.ppermute(value, ('y', 'x'), pairs)  14.4 us
    ppermute x3, starting transfers between devices, same_colour(): return lax.ppermute(value, ('y', 'x'), pairs)  12.7 us
    ppermute x7, waiting for transfers between devices, along(): lax.ppermute(value, axis, [(i, (i + step) % SIDE) for i in range(SIDE)])  8.81 us
    dynamic_update_slice x5, local copies, waits for them, and re-layouts, on_device(): out = lax.dynamic_update_slice(out, value, (start, at, 0, 0))  6.59 us
    all_to_all x1, starting transfers between devices, on_device(): lax.all_to_all(returned, 'lon', 0, 0, tiled=True).reshape(LON * BACK, CH)  6.23 us
  transfers between devices with their start and end apart: 12, of which 9 were waited for; matrix products, arithmetic and copies ran while one was open for 7% of the time, Pallas kernels for 5%

profile of v7, /device:TPU:24, one launch (start us, length us, event | category | flops | bytes accessed | tf_op | source)
XLA Modules:
  0.0 139.5 jit_solution(2063389192935225798)
XLA Ops:
  0.0 1.0 copy-done.3
  1.1 1.0 shard_map.28
  2.1 15.5 %all-to-all-start = ((bf16[32,34,2,128]{3,2,1,0:T(2,128)(2,1)}), bf16[32,34,2,128]{3,2,1,0:T(2,128)(2,1)S(1)}, u32[]{:S(2)}, u32[]{:S(2)}) async-start(bf16[32,34,2,128]{3,2,1,0:T(2,128)(2,1)} %bitcast), calls=%async_computation | async-start | bytes 1114112 | tf_op jit(solution)/shard_map/all_to_all | solution.py:226
  17.6 0.0 copy-start.2
  17.7 1.2 copy-done.2
  18.8 0.3 shard_map.29
  19.1 0.1 constant_dynamic-slice_fusion
  19.2 2.1 %collective-permute-start = (bf16[16,48,128]{2,1,0:T(8,128)(2,1)S(1)}, bf16[16,48,128]{2,1,0:T(8,128)(2,1)S(1)}, u32[]{:S(2)}, u32[]{:S(2)}) collective-permute-start(bf16[16,48,128]{2,1,0:T(8,128)(2,1)S(1)} %get-tuple-element.18), channel_id=1, source_target_pairs={{0,128},{128,256},{256,384},{384,0},{1,129},{129,257},{257,385},{3... | collective-permute-start | bytes 589832 | tf_op jit(solution)/shard_map/ppermute | solution.py:204
  21.3 3.4 %collective-permute-start.1 = (bf16[16,48,128]{2,1,0:T(8,128)(2,1)S(1)}, bf16[16,48,128]{2,1,0:T(8,128)(2,1)S(1)}, u32[]{:S(2)}, u32[]{:S(2)}) collective-permute-start(bf16[16,48,128]{2,1,0:T(8,128)(2,1)S(1)} %get-tuple-element.17), channel_id=1, source_target_pairs={{0,32},{32,64},{64,96},{96,0},{1,33},{33,65},{65,97},{97,1},{2,34}... | collective-permute-start | bytes 589832 | tf_op jit(solution)/shard_map/ppermute | solution.py:204
  24.7 3.7 %collective-permute-start.2 = (bf16[16,48,128]{2,1,0:T(8,128)(2,1)S(1)}, bf16[16,48,128]{2,1,0:T(8,128)(2,1)S(1)}, u32[]{:S(2)}, u32[]{:S(2)}) collective-permute-start(bf16[16,48,128]{2,1,0:T(8,128)(2,1)S(1)} %get-tuple-element.16), channel_id=1, source_target_pairs={{0,96},{32,0},{64,32},{96,64},{1,97},{33,1},{65,33},{97,65},{2,98}... | collective-permute-start | bytes 589832 | tf_op jit(solution)/shard_map/ppermute | solution.py:204
  28.5 0.7 select_multiply_fusion
  29.1 0.5 fusion.9
  29.6 0.9 shard_map.30.table_ref
  30.5 0.8 collective-permute-done.1
  31.3 1.9 %collective-permute-done.2 = bf16[16,48,128]{2,1,0:T(8,128)(2,1)S(1)} collective-permute-done((bf16[16,48,128]{2,1,0:T(8,128)(2,1)S(1)}, bf16[16,48,128]{2,1,0:T(8,128)(2,1)S(1)}, u32[]{:S(2)}, u32[]{:S(2)}) %collective-permute-start.2) | collective-permute-done | bytes 196640 | tf_op jit(solution)/shard_map/ppermute | solution.py:204
  33.2 1.0 pad_maximum_fusion.refs_0_
  34.2 5.8 %collective-permute-start.3 = (bf16[4,16,48,128]{3,2,1,0:T(8,128)(2,1)}, bf16[4,16,48,128]{3,2,1,0:T(8,128)(2,1)}, u32[]{:S(2)}, u32[]{:S(2)}) collective-permute-start(bf16[4,16,48,128]{3,2,1,0:T(8,128)(2,1)} %pad_maximum_fusion.refs_0_), channel_id=1, source_target_pairs={{0,448},{32,480},{64,384},{96,416},{128,64},{160,96},{192,0},{224,... | collective-permute-start | bytes 2359304 | tf_op jit(solution)/shard_map/ppermute | solution.py:213
  40.0 3.6 %collective-permute-start.4 = (bf16[4,16,48,128]{3,2,1,0:T(8,128)(2,1)}, bf16[4,16,48,128]{3,2,1,0:T(8,128)(2,1)}, u32[]{:S(2)}, u32[]{:S(2)}) collective-permute-start(bf16[4,16,48,128]{3,2,1,0:T(8,128)(2,1)} %pad_maximum_fusion.refs_0_), channel_id=1, source_target_pairs={{0,192},{32,224},{64,128},{96,160},{128,320},{160,352},{192,256},{... | collective-permute-start | bytes 2359304 | tf_op jit(solution)/shard_map/ppermute | solution.py:213
  43.7 3.2 %collective-permute-start.5 = (bf16[4,16,48,128]{3,2,1,0:T(8,128)(2,1)}, bf16[4,16,48,128]{3,2,1,0:T(8,128)(2,1)}, u32[]{:S(2)}, u32[]{:S(2)}) collective-permute-start(bf16[4,16,48,128]{3,2,1,0:T(8,128)(2,1)} %pad_maximum_fusion.refs_0_), channel_id=1, source_target_pairs={{0,256},{32,288},{64,320},{96,352},{128,384},{160,416},{192,448},{... | collective-permute-start | bytes 2359304 | tf_op jit(solution)/shard_map/ppermute | solution.py:213
  46.9 5.8 %all-to-all-done = bf16[32,34,2,128]{3,2,1,0:T(2,128)(2,1)S(1)} async-done(((bf16[32,34,2,128]{3,2,1,0:T(2,128)(2,1)}), bf16[32,34,2,128]{3,2,1,0:T(2,128)(2,1)S(1)}, u32[]{:S(2)}, u32[]{:S(2)}) %all-to-all-start) | async-done | bytes 557088 | tf_op jit(solution)/shard_map/all_to_all | solution.py:226
  52.7 1.9 %shard_map.31 = bf16[1152,128]{1,0:T(8,128)(2,1)} custom-call(bf16[2176,128]{1,0:T(8,128)(2,1)S(1)} %bitcast.19, bf16[768,1536]{1,0:T(8,128)(2,1)S(1)} %shard_map.30.table_ref), custom_call_target="tpu_custom_call" | custom-call | tf_op jit(solution)/shard_map/pallas_call | solution.py:263
  54.6 6.2 %all-to-all-start.1 = ((bf16[32,18,2,128]{3,2,1,0:T(2,128)(2,1)}), bf16[32,18,2,128]{3,2,1,0:T(2,128)(2,1)S(1)}, u32[]{:S(2)}, u32[]{:S(2)}) async-start(bf16[32,18,2,128]{3,2,1,0:T(2,128)(2,1)} %bitcast.8), calls=%async_computation.1 | async-start | bytes 589824 | tf_op jit(solution)/shard_map/all_to_all | solution.py:275
  60.8 0.0 collective-permute-done.3.refs_1_
  60.8 13.7 %collective-permute-done.4.refs_2_ = bf16[4,16,48,128]{3,2,1,0:T(8,128)(2,1)} collective-permute-done((bf16[4,16,48,128]{3,2,1,0:T(8,128)(2,1)}, bf16[4,16,48,128]{3,2,1,0:T(8,128)(2,1)}, u32[]{:S(2)}, u32[]{:S(2)}) %collective-permute-start.4) | collective-permute-done | bytes 786464 | tf_op jit(solution)/shard_map/ppermute | solution.py:213
  74.5 0.7 collective-permute-done.5.refs_3_
  75.2 4.0 %shard_map.32.p_ref = bf16[3,672,768]{2,1,0:T(8,128)(2,1)S(1)} custom-call(bf16[4,16,48,128]{3,2,1,0:T(8,128)(2,1)} %pad_maximum_fusion.refs_0_, bf16[4,16,48,128]{3,2,1,0:T(8,128)(2,1)} %collective-permute-done.3.refs_1_, bf16[4,16,48,128]{3,2,1,0:T(8,128)(2,1)} %collective-permute-done.4.refs_2_, bf16[4,16,48,128]{3,2,1,0:T(8,128)(2,1)} %collective-permute-done.5.refs_3_), custom_call_target="tpu_custom_call" | custom-call | flops 99999997952 | bytes 1000000000 | tf_op jit(solution)/shard_map/pallas_call | solution.py:249
  79.3 0.0 copy-start
  79.3 1.6 %copy-done = bf16[3,672,768]{2,1,0:T(8,128)(2,1)} copy-done((bf16[3,672,768]{2,1,0:T(8,128)(2,1)}, bf16[3,672,768]{2,1,0:T(8,128)(2,1)S(1)}, u32[]{:S(2)}) %copy-start) | copy-done | bytes 3096600
  80.9 4.1 %all-to-all-done.1 = bf16[32,18,2,128]{3,2,1,0:T(2,128)(2,1)S(1)} async-done(((bf16[32,18,2,128]{3,2,1,0:T(2,128)(2,1)}), bf16[32,18,2,128]{3,2,1,0:T(2,128)(2,1)S(1)}, u32[]{:S(2)}, u32[]{:S(2)}) %all-to-all-start.1) | async-done | bytes 294944 | tf_op jit(solution)/shard_map/all_to_all | solution.py:275
  85.0 0.3 shard_map.33
  85.2 23.4 %all_to_all.15.s_ref = bf16[16,3,48,256]{3,2,1,0:T(8,128)(2,1)S(1)} all-to-all(bf16[16,3,48,256]{3,2,1,0:T(8,128)(2,1)S(1)} %shard_map.33), channel_id=1, replica_groups=mesh['y'=4,'x'=4,'lon'=32] {'y','x'}, dimensions={0} | all-to-all | bytes 2359296 | tf_op jit(solution)/shard_map/all_to_all | solution.py:282
  108.6 1.1 shard_map.34
  109.7 3.2 %collective-permute-start.8 = (bf16[4032,128]{1,0:T(8,128)(2,1)S(1)}, bf16[4032,128]{1,0:T(8,128)(2,1)S(1)}, u32[]{:S(2)}, u32[]{:S(2)}) collective-permute-start(bf16[4032,128]{1,0:T(8,128)(2,1)S(1)} %shard_map.34), channel_id=1, source_target_pairs={{0,96},{32,0},{64,32},{96,64},{1,97},{33,1},{65,33},{97,65},{2,98}... | collective-permute-start | bytes 3096584 | tf_op jit(solution)/shard_map/ppermute | solution.py:204
  112.9 2.7 %collective-permute-start.9 = (bf16[4032,128]{1,0:T(8,128)(2,1)S(1)}, bf16[4032,128]{1,0:T(8,128)(2,1)S(1)}, u32[]{:S(2)}, u32[]{:S(2)}) collective-permute-start(bf16[4032,128]{1,0:T(8,128)(2,1)S(1)} %shard_map.34), channel_id=1, source_target_pairs={{0,32},{32,64},{64,96},{96,0},{1,33},{33,65},{65,97},{97,1},{2,34}... | collective-permute-start | bytes 3096584 | tf_op jit(solution)/shard_map/ppermute | solution.py:204
  115.6 1.0 fusion.33
  116.6 4.3 %collective-permute-start.6 = (bf16[2016,128]{1,0:T(8,128)(2,1)}, bf16[2016,128]{1,0:T(8,128)(2,1)}, u32[]{:S(2)}, u32[]{:S(2)}) collective-permute-start(bf16[2016,128]{1,0:T(8,128)(2,1)} %get-tuple-element.14), channel_id=1, source_target_pairs={{0,128},{128,256},{256,384},{384,0},{1,129},{129,257},{257,385},{3... | collective-permute-start | bytes 1548296 | tf_op jit(solution)/shard_map/ppermute | solution.py:204
  120.9 2.1 %collective-permute-start.7 = (bf16[2016,128]{1,0:T(8,128)(2,1)}, bf16[2016,128]{1,0:T(8,128)(2,1)}, u32[]{:S(2)}, u32[]{:S(2)}) collective-permute-start(bf16[2016,128]{1,0:T(8,128)(2,1)} %get-tuple-element.13), channel_id=1, source_target_pairs={{0,384},{128,0},{256,128},{384,256},{1,385},{129,1},{257,129},{385... | collective-permute-start | bytes 1548296 | tf_op jit(solution)/shard_map/ppermute | solution.py:204
  123.1 2.1 %broadcast_in_dim.38 = bf16[672,12,2,128]{3,2,1,0:T(2,128)(2,1)S(1)} broadcast(bf16[]{:T(256)} %constant.119.clone.1), dimensions={} | broadcast | bytes 4128770 | tf_op jit(solution)/shard_map/broadcast_in_dim | solution.py:300
  125.2 0.9 constant_dynamic-update-slice_fusion.4
  126.1 1.7 %collective-permute-done.6 = bf16[2016,128]{1,0:T(8,128)(2,1)} collective-permute-done((bf16[2016,128]{1,0:T(8,128)(2,1)}, bf16[2016,128]{1,0:T(8,128)(2,1)}, u32[]{:S(2)}, u32[]{:S(2)}) %collective-permute-start.6) | collective-permute-done | bytes 516128 | tf_op jit(solution)/shard_map/ppermute | solution.py:204
  127.9 1.5 %constant_dynamic-update-slice_fusion.3 = bf16[672,12,2,128]{3,2,1,0:T(2,128)(2,1)S(1)} fusion(bf16[672,12,2,128]{3,2,1,0:T(2,128)(2,1)S(1)} %constant_dynamic-update-slice_fusion.4, bf16[336,3,2,128]{3,2,1,0:T(2,128)(2,1)} %bitcast.11, s32[]{:T(128)S(6)} %select_n.170), kind=kLoop, calls=%fused_computation.53 | loop fusion | bytes 1032196 | tf_op jit(solution)/shard_map/dynamic_update_slice | solution.py:304
  129.4 4.0 %collective-permute-done.7 = bf16[2016,128]{1,0:T(8,128)(2,1)} collective-permute-done((bf16[2016,128]{1,0:T(8,128)(2,1)}, bf16[2016,128]{1,0:T(8,128)(2,1)}, u32[]{:S(2)}, u32[]{:S(2)}) %collective-permute-start.7) | collective-permute-done | bytes 516128 | tf_op jit(solution)/shard_map/ppermute | solution.py:204
  133.4 1.5 %constant_dynamic-update-slice_fusion.2 = bf16[672,12,2,128]{3,2,1,0:T(2,128)(2,1)S(1)} fusion(bf16[672,12,2,128]{3,2,1,0:T(2,128)(2,1)S(1)} %constant_dynamic-update-slice_fusion.3, bf16[336,3,2,128]{3,2,1,0:T(2,128)(2,1)} %bitcast.12, s32[]{:T(128)S(6)} %select_n.170), kind=kLoop, calls=%fused_computation.52 | loop fusion | bytes 1032196 | tf_op jit(solution)/shard_map/dynamic_update_slice | solution.py:304
  134.9 0.9 constant_dynamic-update-slice_fusion.1
  135.9 0.0 copy-start.4
  135.9 0.4 collective-permute-done.9
  136.3 1.6 %copy-done.4 = bf16[672,12,2,128]{3,2,1,0:T(2,128)(2,1)} copy-done((bf16[672,12,2,128]{3,2,1,0:T(2,128)(2,1)}, bf16[672,12,2,128]{3,2,1,0:T(2,128)(2,1)S(1)}, u32[]{:S(2)}) %copy-start.4) | copy-done | bytes 4128792
  137.9 1.7 %constant_dynamic-update-slice_fusion = bf16[672,12,2,128]{3,2,1,0:T(2,128)(2,1)} fusion(bf16[672,12,2,128]{3,2,1,0:T(2,128)(2,1)} %copy-done.4, bf16[672,3,2,128]{3,2,1,0:T(2,128)(2,1)S(1)} %bitcast.21, s32[]{:T(128)S(6)} %select_n.173), kind=kLoop, calls=%fused_computation.50 | loop fusion | bytes 2064388 | tf_op jit(solution)/shard_map/dynamic_update_slice | solution.py:304
  (9 shorter events, 0.1 us)
Async XLA Ops:
  0.0 1.1 copy-start.3
  2.1 50.6 %all-to-all-start = ((bf16[32,34,2,128]{3,2,1,0:T(2,128)(2,1)}), bf16[32,34,2,128]{3,2,1,0:T(2,128)(2,1)S(1)}, u32[]{:S(2)}, u32[]{:S(2)}) async-start(bf16[32,34,2,128]{3,2,1,0:T(2,128)(2,1)} %bitcast), calls=%async_computation | async-start | bytes 1114112 | tf_op jit(solution)/shard_map/all_to_all | solution.py:226
  17.6 1.2 copy-start.2
  19.2 11.3 %collective-permute-start = (bf16[16,48,128]{2,1,0:T(8,128)(2,1)S(1)}, bf16[16,48,128]{2,1,0:T(8,128)(2,1)S(1)}, u32[]{:S(2)}, u32[]{:S(2)}) collective-permute-start(bf16[16,48,128]{2,1,0:T(8,128)(2,1)S(1)} %get-tuple-element.18), channel_id=1, source_target_pairs={{0,128},{128,256},{256,384},{384,0},{1,129},{129,257},{257,385},{3... | collective-permute-start | bytes 589832 | tf_op jit(solution)/shard_map/ppermute | solution.py:204
  21.3 10.0 %collective-permute-start.1 = (bf16[16,48,128]{2,1,0:T(8,128)(2,1)S(1)}, bf16[16,48,128]{2,1,0:T(8,128)(2,1)S(1)}, u32[]{:S(2)}, u32[]{:S(2)}) collective-permute-start(bf16[16,48,128]{2,1,0:T(8,128)(2,1)S(1)} %get-tuple-element.17), channel_id=1, source_target_pairs={{0,32},{32,64},{64,96},{96,0},{1,33},{33,65},{65,97},{97,1},{2,34}... | collective-permute-start | bytes 589832 | tf_op jit(solution)/shard_map/ppermute | solution.py:204
  24.7 8.5 %collective-permute-start.2 = (bf16[16,48,128]{2,1,0:T(8,128)(2,1)S(1)}, bf16[16,48,128]{2,1,0:T(8,128)(2,1)S(1)}, u32[]{:S(2)}, u32[]{:S(2)}) collective-permute-start(bf16[16,48,128]{2,1,0:T(8,128)(2,1)S(1)} %get-tuple-element.16), channel_id=1, source_target_pairs={{0,96},{32,0},{64,32},{96,64},{1,97},{33,1},{65,33},{97,65},{2,98}... | collective-permute-start | bytes 589832 | tf_op jit(solution)/shard_map/ppermute | solution.py:204
  34.2 26.7 %collective-permute-start.3 = (bf16[4,16,48,128]{3,2,1,0:T(8,128)(2,1)}, bf16[4,16,48,128]{3,2,1,0:T(8,128)(2,1)}, u32[]{:S(2)}, u32[]{:S(2)}) collective-permute-start(bf16[4,16,48,128]{3,2,1,0:T(8,128)(2,1)} %pad_maximum_fusion.refs_0_), channel_id=1, source_target_pairs={{0,448},{32,480},{64,384},{96,416},{128,64},{160,96},{192,0},{224,... | collective-permute-start | bytes 2359304 | tf_op jit(solution)/shard_map/ppermute | solution.py:213
  40.0 34.5 %collective-permute-start.4 = (bf16[4,16,48,128]{3,2,1,0:T(8,128)(2,1)}, bf16[4,16,48,128]{3,2,1,0:T(8,128)(2,1)}, u32[]{:S(2)}, u32[]{:S(2)}) collective-permute-start(bf16[4,16,48,128]{3,2,1,0:T(8,128)(2,1)} %pad_maximum_fusion.refs_0_), channel_id=1, source_target_pairs={{0,192},{32,224},{64,128},{96,160},{128,320},{160,352},{192,256},{... | collective-permute-start | bytes 2359304 | tf_op jit(solution)/shard_map/ppermute | solution.py:213
  43.7 31.6 %collective-permute-start.5 = (bf16[4,16,48,128]{3,2,1,0:T(8,128)(2,1)}, bf16[4,16,48,128]{3,2,1,0:T(8,128)(2,1)}, u32[]{:S(2)}, u32[]{:S(2)}) collective-permute-start(bf16[4,16,48,128]{3,2,1,0:T(8,128)(2,1)} %pad_maximum_fusion.refs_0_), channel_id=1, source_target_pairs={{0,256},{32,288},{64,320},{96,352},{128,384},{160,416},{192,448},{... | collective-permute-start | bytes 2359304 | tf_op jit(solution)/shard_map/ppermute | solution.py:213
  54.6 30.4 %all-to-all-start.1 = ((bf16[32,18,2,128]{3,2,1,0:T(2,128)(2,1)}), bf16[32,18,2,128]{3,2,1,0:T(2,128)(2,1)S(1)}, u32[]{:S(2)}, u32[]{:S(2)}) async-start(bf16[32,18,2,128]{3,2,1,0:T(2,128)(2,1)} %bitcast.8), calls=%async_computation.1 | async-start | bytes 589824 | tf_op jit(solution)/shard_map/all_to_all | solution.py:275
  79.3 1.7 %copy-start = (bf16[3,672,768]{2,1,0:T(8,128)(2,1)}, bf16[3,672,768]{2,1,0:T(8,128)(2,1)S(1)}, u32[]{:S(2)}) copy-start(bf16[3,672,768]{2,1,0:T(8,128)(2,1)S(1)} %shard_map.32.p_ref) | copy-start | bytes 9289732
  85.0 23.6 %copy-start.1 = (bf16[3,672,768]{2,1,0:T(8,128)(2,1)S(1)}, bf16[3,672,768]{2,1,0:T(8,128)(2,1)}, u32[]{:S(2)}) copy-start(bf16[3,672,768]{2,1,0:T(8,128)(2,1)} %copy-done) | copy-start | bytes 9289732
  109.7 25.2 %collective-permute-start.8 = (bf16[4032,128]{1,0:T(8,128)(2,1)S(1)}, bf16[4032,128]{1,0:T(8,128)(2,1)S(1)}, u32[]{:S(2)}, u32[]{:S(2)}) collective-permute-start(bf16[4032,128]{1,0:T(8,128)(2,1)S(1)} %shard_map.34), channel_id=1, source_target_pairs={{0,96},{32,0},{64,32},{96,64},{1,97},{33,1},{65,33},{97,65},{2,98}... | collective-permute-start | bytes 3096584 | tf_op jit(solution)/shard_map/ppermute | solution.py:204
  112.9 23.4 %collective-permute-start.9 = (bf16[4032,128]{1,0:T(8,128)(2,1)S(1)}, bf16[4032,128]{1,0:T(8,128)(2,1)S(1)}, u32[]{:S(2)}, u32[]{:S(2)}) collective-permute-start(bf16[4032,128]{1,0:T(8,128)(2,1)S(1)} %shard_map.34), channel_id=1, source_target_pairs={{0,32},{32,64},{64,96},{96,0},{1,33},{33,65},{65,97},{97,1},{2,34}... | collective-permute-start | bytes 3096584 | tf_op jit(solution)/shard_map/ppermute | solution.py:204
  116.6 11.3 %collective-permute-start.6 = (bf16[2016,128]{1,0:T(8,128)(2,1)}, bf16[2016,128]{1,0:T(8,128)(2,1)}, u32[]{:S(2)}, u32[]{:S(2)}) collective-permute-start(bf16[2016,128]{1,0:T(8,128)(2,1)} %get-tuple-element.14), channel_id=1, source_target_pairs={{0,128},{128,256},{256,384},{384,0},{1,129},{129,257},{257,385},{3... | collective-permute-start | bytes 1548296 | tf_op jit(solution)/shard_map/ppermute | solution.py:204
  120.9 12.5 %collective-permute-start.7 = (bf16[2016,128]{1,0:T(8,128)(2,1)}, bf16[2016,128]{1,0:T(8,128)(2,1)}, u32[]{:S(2)}, u32[]{:S(2)}) collective-permute-start(bf16[2016,128]{1,0:T(8,128)(2,1)} %get-tuple-element.13), channel_id=1, source_target_pairs={{0,384},{128,0},{256,128},{384,256},{1,385},{129,1},{257,129},{385... | collective-permute-start | bytes 1548296 | tf_op jit(solution)/shard_map/ppermute | solution.py:204
  135.9 2.0 %copy-start.4 = (bf16[672,12,2,128]{3,2,1,0:T(2,128)(2,1)}, bf16[672,12,2,128]{3,2,1,0:T(2,128)(2,1)S(1)}, u32[]{:S(2)}) copy-start(bf16[672,12,2,128]{3,2,1,0:T(2,128)(2,1)S(1)} %constant_dynamic-update-slice_fusion.1) | copy-start | bytes 12386308
